TPU v7x, 32 devices: a whole 2x2x4 slice. The times are simulated.
32 devices in a mesh: ctx: 16 (over z, y, core), tp: 2 (over x).
Axes of the slice: x: 2, y: 2, z: 4, core: 2. Of those that a mesh axis runs over, the one named last changes fastest.
Arguments:
- cache_k: bfloat16 [4096, 1024], P('ctx', 'tp'), may hold values from -8 to 8
- cache_v: bfloat16 [4096, 1024], P('ctx', 'tp'), may hold values from -6 to 6
- span_q: bfloat16 [64, 4096], P('ctx', 'tp'), may hold values from -8 to 8
- span_k: bfloat16 [64, 1024], P('ctx', 'tp'), may hold values from -6 to 6
- span_v: bfloat16 [64, 1024], P('ctx', 'tp'), may hold values from -6 to 6
- span_frames: int32 [64], replicated, may hold values from 0 to 7, never falling along the last dimension, each value on 1 to 16 neighbouring positions
- action_ids: int32 [64], P('ctx'), may hold values from 0 to 17
- action_table: bfloat16 [18, 1024], P(None, 'tp'), may hold values from -6 to 6
- frame_q: bfloat16 [64, 4096], P('ctx', 'tp'), may hold values from -8 to 8
- frame_k: bfloat16 [64, 1024], P('ctx', 'tp'), may hold values from -6 to 6
- frame_v: bfloat16 [64, 1024], P('ctx', 'tp'), may hold values from -6 to 6
- revealed_k: bfloat16 [64, 1024], P('ctx', 'tp'), may hold values from -6 to 6
- revealed_v: bfloat16 [64, 1024], P('ctx', 'tp'), may hold values from -6 to 6
- mask_k: bfloat16 [1024], P('tp'), may hold values from -6 to 6
- mask_v: bfloat16 [1024], P('tp'), may hold values from -6 to 6
- pass1_idx: int32 [32], replicated, may hold values from 0 to 63, as said below
- pass2_idx: int32 [16], replicated, may hold values from 0 to 63, as said below
- out_gain: float32 [4096], P('tp'), may hold values from 0.5 to 1.5
Outputs:
- span_out: bfloat16 [64, 4096], P('ctx', 'tp')
- first_out: bfloat16 [32, 4096], P('ctx', 'tp')
- second_out: bfloat16 [16, 4096], P('ctx', 'tp')
Inputs may be any that keep to these rules, and one draw needn't show every extreme that they name: `pass1_idx`: 32 distinct frame positions, 0 and 63 among them. `pass2_idx`: 16 distinct entries of pass1_idx, 0 and 63 among them.
All inputs are finite; a program needn't handle non-finite values.
Results may differ from a plain program's by a relative error of at most 0.0095.
Values may be sent and summed in bfloat16 or wider, within the bound.
No kernel may reach another device: no remote copies, remote signals or barrier semaphores. Data moves between devices by JAX's collectives and lax.ppermute only.
A program may use at most 64 MiB of HBM per device.

v0:
```python
from functools import reduce

import jax
import jax.numpy as jnp
from jax import lax
from jax.sharding import PartitionSpec as P

H = 32
HD = 128


def shortened(array):

    def short(part):
        return part.astype(jnp.bfloat16) if part.dtype == jnp.float32 else part

    return jax.tree.map(short, array)


def from_partner(value, axis, bit):
    mask = 2**bit
    pairs = [(source, source ^ mask) for source in range(lax.axis_size(axis))]
    return lax.ppermute(value, axis, pairs)


def block_partial(query_block, frame_block, groups):
    row_count = query_block.shape[0]
    local_heads = groups[0][0].shape[1] // HD
    group_size = query_block.shape[1] // HD // local_heads
    query_heads = query_block.reshape(row_count, local_heads, group_size, HD)
    scaling = HD ** (-0.5)
    logits_all = []
    for key_rows, value_rows, key_frames in groups:
        key_heads = key_rows.reshape(key_rows.shape[0], local_heads, HD)
        logits = (
            jnp.einsum("bkgd,nkd->kgbn", query_heads, key_heads, preferred_element_type=jnp.float32)
            * scaling
        )
        if key_frames is not None:
            logits = jnp.where(
                key_frames[None, None, None, :] <= frame_block[None, None, :, None], logits, -1e30
            )
        logits_all.append(logits)
    maxima = reduce(jnp.maximum, [logits.max(axis=3) for logits in logits_all])
    numerator = jnp.zeros((local_heads, group_size, row_count, HD), jnp.float32)
    denominator = jnp.zeros((local_heads, group_size, row_count), jnp.float32)
    for (key_rows, value_rows, key_frames), logits in zip(groups, logits_all):
        weights = jnp.exp(logits - maxima[..., None])
        denominator = denominator + weights.sum(axis=3)
        value_heads = value_rows.reshape(value_rows.shape[0], local_heads, HD)
        numerator = numerator + jnp.einsum(
            "kgbn,nkd->kgbd",
            weights.astype(jnp.bfloat16),
            value_heads,
            preferred_element_type=jnp.float32,
        )
    numerator = numerator.transpose(2, 0, 1, 3).reshape(row_count, -1)
    maxima = maxima.transpose(2, 0, 1).reshape(row_count, -1)
    denominator = denominator.transpose(2, 0, 1).reshape(row_count, -1)
    return (numerator, maxima, denominator)


def attend(queries, query_frames, groups):
    row_total = queries.shape[0]
    block_rows = 64 if row_total % 64 == 0 else row_total
    query_blocks = queries.reshape(row_total // block_rows, block_rows, queries.shape[1])
    frame_blocks = query_frames.reshape(row_total // block_rows, block_rows)

    def one_block(paired):
        return block_partial(paired[0], paired[1], groups)

    numerator, maxima, denominator = lax.map(one_block, (query_blocks, frame_blocks))
    return (
        numerator.reshape(row_total, -1),
        maxima.reshape(row_total, -1),
        denominator.reshape(row_total, -1),
    )


def by_owner(arrays, owners):
    pieces = [array.reshape(owners, array.shape[0] // owners, array.shape[1]) for array in arrays]
    joined = jnp.concatenate(pieces, axis=1)
    return joined.reshape(-1, arrays[0].shape[1])


def widen(array, half_bit, width, filler):
    rows = array.shape[0]
    shaped = array.reshape(rows, 1, -1, width)
    blank = jnp.full(shaped.shape, filler, array.dtype)
    low_first = jnp.concatenate([shaped, blank], axis=1)
    high_first = jnp.concatenate([blank, shaped], axis=1)
    return jnp.where(half_bit == 0, low_first, high_first).reshape(rows, -1)


def merge_rows(numerator, maxima, denominator, half_bit):
    numerator = widen(numerator, half_bit, HD, 0.0)
    maxima = widen(maxima, half_bit, 1, -1e30)
    denominator = widen(denominator, half_bit, 1, 0.0)
    head_count = maxima.shape[1]
    highest = lax.pmax(shortened(maxima), "ctx").astype(maxima.dtype)
    factor = jnp.exp(maxima - highest)
    scaled = (numerator.reshape(-1, head_count, HD) * factor[..., None]).reshape(numerator.shape)
    summed, totals = (
        lax.psum_scatter(scaled, "ctx", scatter_dimension=0, tiled=True),
        lax.psum_scatter(denominator * factor, "ctx", scatter_dimension=0, tiled=True),
    )
    return (summed.reshape(-1, head_count, HD) / totals[..., None]).reshape(summed.shape)


def per_device(
    cache_k,
    cache_v,
    span_q,
    span_k,
    span_v,
    span_frames,
    action_ids,
    action_table,
    frame_q,
    frame_k,
    frame_v,
    revealed_k,
    revealed_v,
    mask_k,
    mask_v,
    pass1_idx,
    pass2_idx,
    out_gain,
):
    owners = lax.axis_size("ctx")
    position = lax.axis_index("ctx")
    span_rows = span_k.shape[0]
    frame_rows = frame_k.shape[0]
    action_hits = action_ids[:, None] == jnp.arange(action_table.shape[0], dtype=jnp.int32)[None, :]
    action_terms = jnp.dot(
        action_hits.astype(jnp.bfloat16), action_table, preferred_element_type=jnp.float32
    )
    span_keys = (span_k.astype(jnp.float32) + action_terms).astype(jnp.bfloat16)
    local_frames = lax.dynamic_slice_in_dim(span_frames, position * span_rows, span_rows)
    frame_pos = position * frame_rows + jnp.arange(frame_rows, dtype=jnp.int32)
    in_first = jnp.any(frame_pos[:, None] == pass1_idx[None, :], axis=1)[:, None]
    in_second = jnp.any(frame_pos[:, None] == pass2_idx[None, :], axis=1)[:, None]
    first_keys = jnp.where(in_first, mask_k[None, :], frame_k)
    first_values = jnp.where(in_first, mask_v[None, :], frame_v)
    second_keys = jnp.where(in_second, mask_k[None, :], jnp.where(in_first, revealed_k, frame_k))
    second_values = jnp.where(in_second, mask_v[None, :], jnp.where(in_first, revealed_v, frame_v))
    all_span_q, all_frame_q = (
        lax.all_gather(span_q, "ctx", axis=0, tiled=True),
        lax.all_gather(frame_q, "ctx", axis=0, tiled=True),
    )
    first_q = jnp.take(all_frame_q, pass1_idx, axis=0)
    second_q = jnp.take(all_frame_q, pass2_idx, axis=0)
    first_zero = jnp.zeros(first_q.shape[0], jnp.int32)
    second_zero = jnp.zeros(second_q.shape[0], jnp.int32)
    half_bit = position % 2
    other_bit = 1 - half_bit
    kv_half = cache_k.shape[1] // 2
    q_half = span_q.shape[1] // 2

    def columns(array, which):
        return lax.dynamic_slice_in_dim(array, which * kv_half, kv_half, 1)

    def query_columns(array):
        return lax.dynamic_slice_in_dim(array, half_bit * q_half, q_half, 1)

    own_sets = [
        columns(array, half_bit)
        for array in (
            cache_k,
            cache_v,
            span_keys,
            span_v,
            first_keys,
            first_values,
            second_keys,
            second_values,
        )
    ]
    got = from_partner(
        (
            columns(cache_k, other_bit),
            columns(cache_v, other_bit),
            columns(span_keys, other_bit),
            columns(span_v, other_bit),
            columns(first_keys, other_bit),
            columns(first_values, other_bit),
            columns(second_keys, other_bit),
            columns(second_values, other_bit),
        ),
        "ctx",
        0,
    )
    partner_frames = lax.dynamic_slice_in_dim(
        span_frames, (position + 1 - 2 * half_bit) * span_rows, span_rows
    )
    caches = [(own_sets[0], own_sets[1], None), (got[0], got[1], None)]
    span_sets = [(own_sets[2], own_sets[3], local_frames), (got[2], got[3], partner_frames)]
    span_open = [(own_sets[2], own_sets[3], None), (got[2], got[3], None)]
    firsts = [(own_sets[4], own_sets[5], None), (got[4], got[5], None)]
    seconds = [(own_sets[6], own_sets[7], None), (got[6], got[7], None)]
    prefill_part = attend(query_columns(all_span_q), span_frames, caches + span_sets)
    first_part = attend(query_columns(first_q), first_zero, caches + span_open + firsts)
    second_part = attend(query_columns(second_q), second_zero, caches + span_open + seconds)
    parts = [prefill_part, first_part, second_part]
    numerator = by_owner([member[0] for member in parts], owners)
    maxima = by_owner([member[1] for member in parts], owners)
    denominator = by_owner([member[2] for member in parts], owners)
    merged = merge_rows(numerator, maxima, denominator, half_bit)
    square_sum = jnp.sum(merged * merged, axis=1)
    total_sq = lax.psum(square_sum, "tp")
    normed = merged * lax.rsqrt(total_sq / (H * HD) + 1e-06)[:, None] * out_gain[None, :]
    result = normed.astype(jnp.bfloat16)
    prefill_own = all_span_q.shape[0] // owners
    first_own = first_q.shape[0] // owners
    span_out = result[:prefill_own]
    first_out = result[prefill_own : prefill_own + first_own]
    second_out = result[prefill_own + first_own :]
    return (span_out, first_out, second_out)


def solution(mesh):
    in_specs = (
        P("ctx", "tp"),
        P("ctx", "tp"),
        P("ctx", "tp"),
        P("ctx", "tp"),
        P("ctx", "tp"),
        P(),
        P("ctx"),
        P(None, "tp"),
        P("ctx", "tp"),
        P("ctx", "tp"),
        P("ctx", "tp"),
        P("ctx", "tp"),
        P("ctx", "tp"),
        P("tp"),
        P("tp"),
        P(),
        P(),
        P("tp"),
    )
    out_specs = (P("ctx", "tp"), P("ctx", "tp"), P("ctx", "tp"))
    return jax.shard_map(
        per_device, mesh=mesh, in_specs=in_specs, out_specs=out_specs, check_vma=False
    )
```

profile of v0, /device:TPU:0, one launch (start us, length us, event | category | flops | bytes accessed | tf_op | source)
XLA Modules:
  0.0 175.0 jit_solution(12818496911952914079)
XLA Ops:
  0.7 0.7 copy-done
  1.6 0.5 collective-permute-start.1
  2.3 0.5 collective-permute-start.3
  4.2 0.6 copy-done.4
  4.9 23.6 %all-gather.1 = bf16[16,4,2048]{2,1,0:T(4,128)(2,1)S(1)} all-gather(bf16[1,4,2048]{2,1,0:T(4,128)(2,1)S(1)} %bitcast.335), channel_id=1, replica_groups=mesh['ctx'=16,'tp'=2] {'ctx'}, dimensions={0}, use_global_device_ids=true | all-gather | bytes 278528 | tf_op jit(solution)/shard_map/all_gather | solution.py:149
  28.6 0.6 gather_fusion.1
  29.7 0.7 gather_fusion
  30.8 0.6 copy-done.1
  32.0 0.5 copy-done.5
  32.5 18.1 %all-gather = bf16[16,4,2048]{2,1,0:T(4,128)(2,1)S(1)} all-gather(bf16[1,4,2048]{2,1,0:T(4,128)(2,1)S(1)} %bitcast.336), channel_id=1, replica_groups=mesh['ctx'=16,'tp'=2] {'ctx'}, dimensions={0}, use_global_device_ids=true | all-gather | bytes 278528 | tf_op jit(solution)/shard_map/all_gather | solution.py:148
  52.4 0.5 copy-done.12
  52.9 0.6 fusion.142
  62.9 0.4 fusion.29
  64.0 31.1 %pmax.7 = bf16[112,16]{0,1:T(8,128)(2,1)S(1)} all-reduce(bf16[112,16]{0,1:T(8,128)(2,1)S(1)} %bitcast_convert_fusion), channel_id=1, replica_groups=mesh['ctx'=16,'tp'=2] {'ctx'}, use_global_device_ids=true, to_apply=%region_18.19 | all-reduce | flops 1792 | bytes 7168 | tf_op jit(solution)/shard_map/pmax | solution.py:100
  96.8 0.7 bitcast_multiply_fusion
  97.5 35.4 %fusion = f32[8,2048]{1,0:T(8,128)S(1)} fusion(f32[112,2048]{1,0:T(8,128)S(1)} %bitcast_multiply_fusion), kind=kCustom, calls=%all-reduce-scatter | all-reduce-scatter fusion | flops 262145 | bytes 983552
  133.0 1.4 collective-permute-start.8
  134.4 30.0 %all-reduce.7 = f32[112,16]{0,1:T(8,128)S(1)} all-reduce(f32[112,16]{0,1:T(8,128)S(1)} %get-tuple-element.140), channel_id=3, replica_groups=mesh['ctx'=16,'tp'=2] {'ctx'}, use_global_device_ids=true, to_apply=%region_36.37.clone | all-reduce | flops 1792 | bytes 14336
  164.5 1.3 collective-permute-start.9
  165.9 1.8 %collective-permute-done.9 = f32[7,2048]{1,0:T(8,128)S(1)} collective-permute-done((f32[7,2048]{1,0:T(8,128)S(1)}, f32[7,2048]{1,0:T(8,128)S(1)}, u32[]{:S(2)}, u32[]{:S(2)}) %collective-permute-start.9) | collective-permute-done | bytes 57376
  168.1 4.9 %psum.7 = f32[7]{0:T(128)S(1)} all-reduce(f32[7]{0:T(128)S(1)} %multiply_reduce_fusion), channel_id=1, replica_groups=mesh['ctx'=16,'tp'=2] {'tp'}, use_global_device_ids=true, to_apply=%region_38.39 | all-reduce | flops 7 | bytes 56 | tf_op jit(solution)/shard_map/psum | solution.py:210
  173.2 0.6 slice.18
  173.8 0.6 slice.17
  174.4 0.6 slice.16
  (154 shorter events, 15.8 us)
Async XLA Ops:
  0.6 0.7 copy-start
  0.7 0.7 copy-start.15
  1.4 1.4 copy-start.18
  1.4 1.8 %copy-start.11 = (bf16[4,512]{1,0:T(4,128)(2,1)S(1)}, bf16[4,512]{1,0:T(4,128)(2,1)}, u32[]{:S(2)}) copy-start(bf16[4,512]{1,0:T(4,128)(2,1)} %param.28) | copy-start | bytes 12292
  1.4 1.8 %copy-start.13 = (bf16[512]{0:T(512)(128)(2,1)S(1)}, bf16[512]{0:T(512)(128)(2,1)}, u32[]{:S(2)}) copy-start(bf16[512]{0:T(512)(128)(2,1)} %param.31) | copy-start | bytes 3076
  1.4 1.8 %copy-start.14 = (bf16[512]{0:T(512)(128)(2,1)S(1)}, bf16[512]{0:T(512)(128)(2,1)}, u32[]{:S(2)}) copy-start(bf16[512]{0:T(512)(128)(2,1)} %param.32) | copy-start | bytes 3076
  1.6 1.4 copy-start.17
  1.6 53.2 %collective-permute-start.1 = (bf16[4,256]{1,0:T(4,128)(2,1)S(1)}, bf16[4,256]{1,0:T(4,128)(2,1)S(1)}, u32[]{:S(2)}, u32[]{:S(2)}) collective-permute-start(bf16[4,256]{1,0:T(4,128)(2,1)S(1)} %constant_dynamic-slice_fusion.12), channel_id=1, source_target_pairs={{0,2},{2,0},{4,6},{6,4},{8,10},{10,8},{12,14},{14,12},{16,18},{18,... | collective-permute-start | bytes 6152 | tf_op jit(solution)/shard_map/ppermute | solution.py:23
  2.3 0.9 copy-start.9
  2.3 0.9 copy-start.10
  2.3 0.9 copy-start.8
  2.3 58.4 %collective-permute-start.3 = (bf16[4,256]{1,0:T(4,128)(2,1)S(1)}, bf16[4,256]{1,0:T(4,128)(2,1)S(1)}, u32[]{:S(2)}, u32[]{:S(2)}) collective-permute-start(bf16[4,256]{1,0:T(4,128)(2,1)S(1)} %constant_dynamic-slice_fusion.8), channel_id=1, source_target_pairs={{0,2},{2,0},{4,6},{6,4},{8,10},{10,8},{12,14},{14,12},{16,18},{18,... | collective-permute-start | bytes 6152 | tf_op jit(solution)/shard_map/ppermute | solution.py:23
  3.4 58.5 %collective-permute-start.5 = (bf16[4,256]{1,0:T(4,128)(2,1)S(1)}, bf16[4,256]{1,0:T(4,128)(2,1)S(1)}, u32[]{:S(2)}, u32[]{:S(2)}) collective-permute-start(bf16[4,256]{1,0:T(4,128)(2,1)S(1)} %constant_dynamic-slice_fusion.4), channel_id=1, source_target_pairs={{0,2},{2,0},{4,6},{6,4},{8,10},{10,8},{12,14},{14,12},{16,18},{18,... | collective-permute-start | bytes 6152 | tf_op jit(solution)/shard_map/ppermute | solution.py:23
  3.6 57.3 %collective-permute-start.7 = (bf16[4,256]{1,0:T(4,128)(2,1)S(1)}, bf16[4,256]{1,0:T(4,128)(2,1)S(1)}, u32[]{:S(2)}, u32[]{:S(2)}) collective-permute-start(bf16[4,256]{1,0:T(4,128)(2,1)S(1)} %constant_dynamic-slice_fusion), channel_id=1, source_target_pairs={{0,2},{2,0},{4,6},{6,4},{8,10},{10,8},{12,14},{14,12},{16,18},{18,... | collective-permute-start | bytes 6152 | tf_op jit(solution)/shard_map/ppermute | solution.py:23
  3.9 52.9 %collective-permute-start.6 = (bf16[4,256]{1,0:T(4,128)(2,1)S(1)}, bf16[4,256]{1,0:T(4,128)(2,1)S(1)}, u32[]{:S(2)}, u32[]{:S(2)}) collective-permute-start(bf16[4,256]{1,0:T(4,128)(2,1)S(1)} %constant_dynamic-slice_fusion.2), channel_id=1, source_target_pairs={{0,2},{2,0},{4,6},{6,4},{8,10},{10,8},{12,14},{14,12},{16,18},{18,... | collective-permute-start | bytes 6152 | tf_op jit(solution)/shard_map/ppermute | solution.py:23
  29.7 1.0 copy-start.2
  30.4 1.0 copy-start.1
  31.7 0.7 copy-start.5
  54.8 1.2 collective-permute-start.4
  56.1 1.3 collective-permute-start
  56.8 2.5 %collective-permute-start.2 = (bf16[256,256]{0,1:T(8,128)(2,1)S(1)}, bf16[256,256]{0,1:T(8,128)(2,1)S(1)}, u32[]{:S(2)}, u32[]{:S(2)}) collective-permute-start(bf16[256,256]{0,1:T(8,128)(2,1)S(1)} %copy.276), channel_id=1, source_target_pairs={{0,2},{2,0},{4,6},{6,4},{8,10},{10,8},{12,14},{14,12},{16,18},{18,... | collective-permute-start | bytes 393224 | tf_op jit(solution)/shard_map/ppermute | solution.py:23
  133.0 34.7 %collective-permute-start.8 = (f32[8,2048]{1,0:T(8,128)S(1)}, f32[8,2048]{1,0:T(8,128)S(1)}, u32[]{:S(2)}, u32[]{:S(2)}) collective-permute-start(f32[8,2048]{1,0:T(8,128)S(1)} %fusion), channel_id=1, source_target_pairs={{0,2},{2,4},{4,6},{6,8},{8,10},{10,12},{12,14},{14,16},{16,18},{18... | collective-permute-start | bytes 196616
  164.5 3.2 %collective-permute-start.9 = (f32[7,2048]{1,0:T(8,128)S(1)}, f32[7,2048]{1,0:T(8,128)S(1)}, u32[]{:S(2)}, u32[]{:S(2)}) collective-permute-start(f32[7,2048]{1,0:T(8,128)S(1)} %slice.19), channel_id=1, source_target_pairs={{0,4},{2,6},{4,8},{6,10},{8,12},{10,14},{12,16},{14,18},{16,20},{1... | collective-permute-start | bytes 172040
  167.7 5.4 %copy-start.6 = (f32[2048]{0:T(1024)S(1)}, f32[2048]{0:T(1024)}, u32[]{:S(2)}) copy-start(f32[2048]{0:T(1024)} %param.35) | copy-start | bytes 24580
  (5 other events, 3.4 us)
where the time goes:
time: 176 us; the launch traced here: 175 us
  blocking collectives  143 us (81%)
  local copies, waits for them, and re-layouts  10.4 us (6%)
  matrix products  7.6 us (4%)
  starting transfers between devices  5.44 us (3%)
  other arithmetic  3.34 us (2%)
  between operations  2.64 us (2%)
  waiting for transfers between devices  2.33 us (1%)
    unnamed x2, blocking collectives  65.4 us
    pmax x1, blocking collectives, merge_rows(): highest = lax.pmax(shortened(maxima), 'ctx').astype(maxima.dtype)  31.1 us
    all_gather x1, blocking collectives, per_device(): lax.all_gather(frame_q, 'ctx', axis=0, tiled=True)  23.6 us
    all_gather x1, blocking collectives, per_device(): lax.all_gather(span_q, 'ctx', axis=0, tiled=True)  18.1 us
    unnamed x49, local copies, waits for them, and re-layouts  5.03 us
    psum x1, blocking collectives, per_device(): total_sq = lax.psum(square_sum, 'tp')  4.93 us
    dot_general x16, matrix products, block_partial(): jnp.einsum('bkgd,nkd->kgbn', query_heads, key_heads, preferred_element_ty...  3.77 us
    dot_general x16, matrix products, block_partial(): jnp.einsum('kgbn,nkd->kgbd', weights.astype(jnp.bfloat16), value_heads, p...  3.65 us
  transfers between devices with their start and end apart: 10, of which 3 were waited for; matrix products, arithmetic and copies ran while one was open for 6% of the time, Pallas kernels for 0%

commit v1 on v0

v1 whole, which is shorter than its diff:
```python
import functools

import jax
import jax.numpy as jnp
from jax import lax
from jax.experimental import pallas as pl
from jax.experimental.pallas import tpu as pltpu
from jax.sharding import PartitionSpec as P

HD = 128
GROUP = 4
NEG = -1e30
EPS = 1e-6
F32 = jnp.float32
BF16 = jnp.bfloat16
VMEM = pltpu.VMEM


def exchange(value, axis, mask):
    pairs = [(source, source ^ mask) for source in range(lax.axis_size(axis))]
    return lax.ppermute(value, axis, pairs)


def call(kernel, name, out_shape, *operands, scratch=(), smem=(), limit=16 * 2**20):
    in_specs = [
        pl.BlockSpec(memory_space=pltpu.SMEM if i in smem else VMEM) for i in range(len(operands))
    ]
    single = not isinstance(out_shape, (list, tuple))
    out_specs = pl.BlockSpec(memory_space=VMEM)
    if not single:
        out_specs = [out_specs] * len(out_shape)
    return pl.pallas_call(
        kernel,
        out_shape=out_shape,
        in_specs=in_specs,
        out_specs=out_specs,
        scratch_shapes=list(scratch),
        compiler_params=pltpu.CompilerParams(vmem_limit_bytes=limit),
        name=name,
    )(*operands)


def prep_kernel(
    hits, table, span_k, span_v, in1, in2, fq, fk, fv, rk, rv, mk, mv, out
):
    rows = fk.shape[0]
    width = fk.shape[1]
    terms = jnp.dot(hits[...], table[...], preferred_element_type=F32)
    span_keys = span_k[...].astype(F32) + terms
    first = in1[...] > 0.0
    second = in2[...] > 0.0
    out[0:rows, :] = fq[...]

    def put(row, column, value):
        out[row : row + rows, column * width : (column + 1) * width] = value.astype(BF16)

    put(rows, 0, span_keys)
    put(rows, 1, span_v[...])
    for given, shown, token, column in ((fk, rk, mk, 0), (fv, rv, mv, 1)):
        frame = given[...].astype(F32)
        mask = token[...].astype(F32)
        put(rows, 2 + column, jnp.where(first, mask, frame))
        put(
            2 * rows,
            column,
            jnp.where(second, mask, jnp.where(first, shown[...].astype(F32), frame)),
        )
    out[2 * rows :, 2 * width :] = jnp.zeros((rows, out.shape[1] - 2 * width), BF16)


def stacked(parts):
    return jnp.concatenate([part.astype(F32) for part in parts], axis=0).astype(BF16)


def select_kernel(rows, pick, span_q, own, m1, m2, m3, out):
    given = stacked([span_q[...]] + [m[0:rows, :] for m in (own, m1, m2, m3)])
    out[...] = jnp.dot(pick[...], given, preferred_element_type=F32).astype(BF16)


def grow_kernel(spans, mine, other, out):
    a = mine[...].astype(F32)
    b = other[...].astype(F32)
    out[...] = jnp.concatenate(
        [a[:spans], b[:spans], a[spans:] + b[spans:]], axis=0
    ).astype(BF16)


def split_stats(stats):
    lane = lax.broadcasted_iota(jnp.int32, stats.shape, 1)
    stats = jnp.where(lane < 16, stats, 0.0)
    high = stats.astype(BF16).astype(F32)
    rest = stats - high
    middle = rest.astype(BF16).astype(F32)
    low = (rest - middle).astype(BF16).astype(F32)
    packed = high + pltpu.roll(middle, 16, 1) + pltpu.roll(low, 32, 1)
    return packed.astype(BF16)


def joined_stats(packed):
    packed = packed.astype(F32)
    return packed + pltpu.roll(packed, 112, 1) + pltpu.roll(packed, 96, 1)


def attention_kernel(
    heads, rows, span_rows, keep,
    perm, allowed, mine, other, k0, k1, k2, k3, v0, v1, v2, v3, m0, m1, m2, m3,
    send, kept, kept_stats, extra_k, extra_v, att,
):
    width = heads * HD
    scaling = HD ** (-0.5)
    queries = jnp.dot(
        perm[...], stacked([mine[...], other[...]]), preferred_element_type=F32
    ).astype(BF16)
    for kind, (row, column) in enumerate(
        ((span_rows, 0), (span_rows, 2), (2 * span_rows, 0))
    ):
        for place, message in enumerate((m0, m1, m2, m3)):
            at = (kind * 4 + place) * span_rows
            for target, shift in ((extra_k, 0), (extra_v, 1)):
                left = (column + shift) * width
                target[at : at + span_rows, :] = message[
                    row : row + span_rows, left : left + width
                ].astype(F32)
    extras = 12 * span_rows
    lane = lax.broadcasted_iota(jnp.int32, (rows, HD), 1)
    stats = jnp.zeros((rows, HD), F32)
    stack = GROUP if rows * GROUP <= 128 else 1
    permit = jnp.concatenate([allowed[...]] * stack, axis=0) > 0.0
    nt = (((1,), (1,)), ((), ()))
    for g in range(heads):
        columns = slice(g * HD, (g + 1) * HD)
        values = [v[:, columns] for v in (v0, v1, v2, v3)]
        values.append(extra_v[:, columns].astype(BF16))
        keys = [k[:, columns] for k in (k0, k1, k2, k3)]
        keys.append(extra_k[:, columns].astype(BF16))
        for start in range(0, GROUP, stack):
            head = g * GROUP + start
            q = jnp.concatenate(
                [queries[:, (head + i) * HD : (head + i + 1) * HD] for i in range(stack)], axis=0
            )
            scores = [
                lax.dot_general(q, key, nt, preferred_element_type=F32) * scaling for key in keys
            ]
            scores[-1] = jnp.where(permit, scores[-1], NEG)
            top = functools.reduce(
                jnp.maximum, [s.max(axis=1, keepdims=True) for s in scores]
            )
            total = jnp.zeros_like(top)
            out = jnp.zeros((rows * stack, HD), F32)
            for s, value in zip(scores, values):
                weights = jnp.exp(s - top)
                total = total + weights.sum(axis=1, keepdims=True)
                out = out + jnp.dot(
                    weights.astype(BF16), value, preferred_element_type=F32
                )
            out = out / total
            level = top + jnp.log(total)
            for i in range(stack):
                piece = slice(i * rows, (i + 1) * rows)
                att[:, (head + i) * HD : (head + i + 1) * HD] = out[piece]
                stats = jnp.where(lane == head + i, level[piece], stats)
    kept[...] = att[:keep, :]
    kept_stats[...] = stats[:keep]
    wide = heads * GROUP * HD
    send[:, :wide] = att[keep:, :].astype(BF16)
    send[:, wide:] = split_stats(stats[keep:])


def merge(heads, kept, kept_stats, got):
    wide = heads * GROUP * HD
    mine = kept_stats[...]
    theirs = joined_stats(got[:, wide:])
    top = jnp.maximum(mine, theirs)
    a = jnp.exp(mine - top)
    b = jnp.exp(theirs - top)
    total = a + b
    a = a / total
    b = b / total
    merged = []
    for h in range(heads * GROUP):
        columns = slice(h * HD, (h + 1) * HD)
        merged.append(
            kept[:, columns] * a[:, h : h + 1] + got[:, columns].astype(F32) * b[:, h : h + 1]
        )
    return merged, top + jnp.log(total)


def merge_kernel(heads, keep, kept, kept_stats, got, send, out, out_stats):
    wide = heads * GROUP * HD
    merged, stats = merge(heads, kept, kept_stats, got)
    for h, value in enumerate(merged):
        columns = slice(h * HD, (h + 1) * HD)
        out[:, columns] = value[:keep]
        send[:, columns] = value[keep:].astype(BF16)
    out_stats[...] = stats[:keep]
    send[:, wide:] = split_stats(stats[keep:])


def last_kernel(heads, kept, kept_stats, got, out, squares):
    merged, _ = merge(heads, kept, kept_stats, got)
    total = jnp.zeros_like(merged[0])
    for h, value in enumerate(merged):
        out[:, h * HD : (h + 1) * HD] = value
        total = total + value * value
    squares[...] = jnp.broadcast_to(total.sum(axis=1, keepdims=True), squares.shape)


def out_kernel(counts, columns_all, att, squares, other, gain, *outs):
    mean_sq = (squares[...] + other[...])[:, 0:1] / columns_all
    normed = att[...] * lax.rsqrt(mean_sq + EPS) * gain[...]
    at = 0
    for count, out in zip(counts, outs):
        out[...] = normed[at : at + count].astype(BF16)
        at += count


def per_device(
    cache_k,
    cache_v,
    span_q,
    span_k,
    span_v,
    span_frames,
    action_ids,
    action_table,
    frame_q,
    frame_k,
    frame_v,
    revealed_k,
    revealed_v,
    mask_k,
    mask_v,
    pass1_idx,
    pass2_idx,
    out_gain,
):
    owners = lax.axis_size("ctx")
    tp = lax.axis_size("tp")
    me = lax.axis_index("ctx")
    blocks = owners // 4
    column = me % 4
    spans = span_k.shape[0]
    frames = frame_k.shape[0]
    width = span_k.shape[1]
    q_width = span_q.shape[1]
    heads = width // HD
    n1 = pass1_idx.shape[0] // owners
    n2 = pass2_idx.shape[0] // owners
    picked = n1 + n2
    block_rows = -(-(spans + picked) // 8) * 8
    rows = blocks * block_rows

    bits = [1 << b for b in range(2, owners.bit_length() - 1)][::-1]
    masks = [0]
    for bit in bits:
        masks = masks + [m ^ bit for m in masks]

    own_pos = me * frames + jnp.arange(frames, dtype=jnp.int32)
    in_first = jnp.any(own_pos[:, None] == pass1_idx[None, :], axis=1)[:, None].astype(F32)
    in_second = jnp.any(own_pos[:, None] == pass2_idx[None, :], axis=1)[:, None].astype(F32)
    actions = jnp.arange(action_table.shape[0], dtype=jnp.int32)
    hits = (action_ids[:, None] == actions[None, :]).astype(BF16)
    message = call(
        prep_kernel,
        "plane_message",
        jax.ShapeDtypeStruct((3 * frames, q_width), BF16),
        hits, action_table, span_k, span_v, in_first, in_second, frame_q,
        frame_k, frame_v, revealed_k, revealed_v, mask_k[None, :], mask_v[None, :],
    )

    m2 = exchange(message, "ctx", 2)
    m3 = exchange(message, "ctx", 3)
    m1 = exchange(message, "ctx", 1)
    k2 = exchange(cache_k, "ctx", 2)
    v2 = exchange(cache_v, "ctx", 2)
    k1 = exchange(cache_k, "ctx", 1)
    v1 = exchange(cache_v, "ctx", 1)
    k3 = exchange(k2, "ctx", 1)
    v3 = exchange(v2, "ctx", 1)

    want1 = lax.dynamic_index_in_dim(pass1_idx.reshape(blocks, 4, n1), column, 1, False)
    want2 = lax.dynamic_index_in_dim(pass2_idx.reshape(blocks, 4, n2), column, 1, False)
    wanted = jnp.concatenate([want1, want2], axis=1).reshape(-1)
    plane = jnp.arange(4, dtype=jnp.int32) ^ me
    plane_frames = (plane[:, None] * frames + jnp.arange(frames, dtype=jnp.int32)).reshape(-1)
    pick = jnp.concatenate(
        [
            jnp.eye(spans, spans + 4 * frames, dtype=BF16),
            jnp.concatenate(
                [
                    jnp.zeros((blocks * picked, spans), BF16),
                    (wanted[:, None] == plane_frames[None, :]).astype(BF16),
                ],
                axis=1,
            ),
        ],
        axis=0,
    )
    state = call(
        functools.partial(select_kernel, frames),
        "column_queries",
        jax.ShapeDtypeStruct((spans + blocks * picked, q_width), BF16),
        pick, span_q, message, m1, m2, m3,
    )
    held = spans
    for bit in bits[:-1]:
        other = exchange(state, "ctx", bit)
        state = call(
            functools.partial(grow_kernel, held),
            "more_queries",
            jax.ShapeDtypeStruct((state.shape[0] + held, q_width), BF16),
            state, other,
        )
        held = 2 * held
    other = exchange(state, "ctx", bits[-1])

    depth = state.shape[0]
    own_block = me // 4
    at_block = jnp.arange(rows, dtype=jnp.int32) // block_rows
    at_row = jnp.arange(rows, dtype=jnp.int32) % block_rows
    mask_of = jnp.repeat(jnp.array(masks, jnp.int32), block_rows)
    half = blocks // 2
    span_at = jnp.where(
        at_block < half, at_block * spans, depth + (at_block - half) * spans
    ) + at_row
    pick_at = held + (own_block ^ (mask_of // 4)) * picked + at_row - spans
    is_span = at_row < spans
    is_pick = (at_row >= spans) & (at_row < spans + picked)
    source = jnp.arange(2 * depth, dtype=jnp.int32)[None, :]
    perm = (
        (is_span[:, None] & (source == span_at[:, None]))
        | (is_pick[:, None] & (source % depth == pick_at[:, None]))
    ).astype(BF16)

    key_frames = span_frames[
        (plane[:, None] * spans + jnp.arange(spans, dtype=jnp.int32)).reshape(-1)
    ]
    row_frames = span_frames[jnp.where(is_span, (me ^ mask_of) * spans + at_row, 0)]
    sees_span = ~is_span[:, None] | (key_frames[None, :] <= row_frames[:, None])
    sees_first = jnp.broadcast_to(
        (is_pick & (at_row < spans + n1))[:, None], (rows, 4 * frames)
    )
    sees_second = jnp.broadcast_to(
        (is_pick & (at_row >= spans + n1))[:, None], (rows, 4 * frames)
    )
    allowed = jnp.concatenate([sees_span, sees_first, sees_second], axis=1).astype(F32)

    keep = rows // 2
    packed = q_width + HD
    send, kept, stats = call(
        functools.partial(attention_kernel, heads, rows, spans, keep),
        "plane_attention",
        [
            jax.ShapeDtypeStruct((keep, packed), BF16),
            jax.ShapeDtypeStruct((keep, q_width), F32),
            jax.ShapeDtypeStruct((keep, HD), F32),
        ],
        perm, allowed, state, other,
        cache_k, k1, k2, k3, cache_v, v1, v2, v3, message, m1, m2, m3,
        scratch=[
            pltpu.VMEM((12 * spans, width), F32),
            pltpu.VMEM((12 * spans, width), F32),
            pltpu.VMEM((rows, q_width), F32),
        ],
        limit=(16 if blocks <= 4 else 40) * 2**20,
    )
    for bit in bits[:0:-1]:
        got = exchange(send, "ctx", bit)
        keep = keep // 2
        send, kept, stats = call(
            functools.partial(merge_kernel, heads, keep),
            "merge_partials",
            [
                jax.ShapeDtypeStruct((keep, packed), BF16),
                jax.ShapeDtypeStruct((keep, q_width), F32),
                jax.ShapeDtypeStruct((keep, HD), F32),
            ],
            kept, stats, got,
        )
    got = exchange(send, "ctx", bits[0])
    att, squares = call(
        functools.partial(last_kernel, heads),
        "merge_last",
        [
            jax.ShapeDtypeStruct((block_rows, q_width), F32),
            jax.ShapeDtypeStruct((block_rows, HD), F32),
        ],
        kept, stats, got,
    )
    other_squares = exchange(squares, "tp", 1)
    counts = (spans, n1, n2)
    return tuple(
        call(
            functools.partial(out_kernel, counts, float(tp * q_width)),
            "normalize",
            [jax.ShapeDtypeStruct((count, q_width), BF16) for count in counts],
            att, squares, other_squares, out_gain[None, :],
        )
    )


def solution(mesh):
    in_specs = (
        P("ctx", "tp"),
        P("ctx", "tp"),
        P("ctx", "tp"),
        P("ctx", "tp"),
        P("ctx", "tp"),
        P(),
        P("ctx"),
        P(None, "tp"),
        P("ctx", "tp"),
        P("ctx", "tp"),
        P("ctx", "tp"),
        P("ctx", "tp"),
        P("ctx", "tp"),
        P("tp"),
        P("tp"),
        P(),
        P(),
        P("tp"),
    )
    out_specs = (P("ctx", "tp"), P("ctx", "tp"), P("ctx", "tp"))
    return jax.shard_map(
        per_device, mesh=mesh, in_specs=in_specs, out_specs=out_specs, check_vma=False
    )
```

time: 176 us -> 55 us (0.31)
  blocking collectives: 143 us -> 0 us
  waiting for transfers between devices: 2.33 us -> 23.5 us
  starting transfers between devices: 5.44 us -> 14.4 us
  matrix products: 7.6 us -> 0 us
  Pallas kernels: 0 us -> 3.45 us
  between operations: 2.64 us -> 0.84 us
    unnamed x2 -> x0, blocking collectives: 65.4 us -> none
    all_gather x2 -> x0, blocking collectives: 41.8 us -> none  [the longest x1 23.6 us: per_device(): lax.all_gather(frame_q, 'ctx', axis=0, tiled=True)]
    pmax x1 -> x0, blocking collectives: 31.1 us -> none  [merge_rows(): highest = lax.pmax(shortened(maxima), 'ctx').astype(maxima.dtype)]
    ppermute x8 -> x14, waiting for transfers between devices: 0.52 us -> 23.5 us  [exchange(): return lax.ppermute(value, axis, pairs)]
    ppermute x8 -> x14, starting transfers between devices: 2.8 us -> 14.4 us  [exchange(): return lax.ppermute(value, axis, pairs)]
    dot_general x33 -> x0, matrix products: 7.6 us -> none  [the longest x16 3.77 us: block_partial(): jnp.einsum('bkgd,nkd->kgbn', query_heads, key_heads, preferred_element_ty...]
    psum x1 -> x0, blocking collectives: 4.93 us -> none  [per_device(): total_sq = lax.psum(square_sum, 'tp')]
    pallas_call x0 -> x7, Pallas kernels: none -> 3.45 us  [call(): pl.pallas_call(kernel, out_shape=out_shape, in_specs=in_specs, out_specs=...]
  transfers between devices with their start and end apart: 10 -> 14, of which waited for: 3 -> 7; matrix products, arithmetic and copies ran while one was open for 6% -> 6% of each run, Pallas kernels for 0% -> 0%
where the time goes in v1:
time: 55 us; the launch traced here: 54.5 us
  waiting for transfers between devices  23.5 us (43%)
  starting transfers between devices  14.4 us (26%)
  local copies, waits for them, and re-layouts  9.36 us (17%)
  Pallas kernels  3.45 us (6%)
  other arithmetic  2.98 us (5%)
  between operations  0.84 us (2%)
    ppermute x14, waiting for transfers between devices, exchange(): return lax.ppermute(value, axis, pairs)  23.5 us
    ppermute x14, starting transfers between devices, exchange(): return lax.ppermute(value, axis, pairs)  14.4 us
    unnamed x36, local copies, waits for them, and re-layouts  6.54 us
    pallas_call x7, Pallas kernels, call(): pl.pallas_call(kernel, out_shape=out_shape, in_specs=in_specs, out_specs=...  3.45 us
  transfers between devices with their start and end apart: 14, of which 7 were waited for; matrix products, arithmetic and copies ran while one was open for 6% of the time, Pallas kernels for 0%

profile of v1, /device:TPU:0, one launch (start us, length us, event | category | flops | bytes accessed | tf_op | source)
XLA Modules:
  0.0 54.5 jit_solution(12111975522204237660)
XLA Ops:
  0.7 0.8 %compare_reduce_fusion.1 = pred[4]{0:T(512)(128)(4,1)S(1)} fusion(s32[32]{0:T(128)} %param.34, s32[4]{0:T(128)S(1)} %iota_add_fusion.1), kind=kLoop, calls=%fused_computation.22 | loop fusion | flops 252 | bytes 148 | tf_op jit(solution)/shard_map/reduce_or | solution.py:259
  1.5 0.8 %compare_reduce_fusion = pred[4]{0:T(512)(128)(4,1)S(1)} fusion(s32[16]{0:T(128)} %param.35, s32[4]{0:T(128)S(1)} %iota_add_fusion.1), kind=kLoop, calls=%fused_computation.21 | loop fusion | flops 124 | bytes 84 | tf_op jit(solution)/shard_map/reduce_or | solution.py:260
  2.4 0.7 %fusion.4.hits = bf16[4,18]{1,0:T(4,128)(2,1)S(1)} fusion(s32[4]{0:T(128)} %param.25), kind=kLoop, calls=%fused_computation.20 | loop fusion | flops 144 | bytes 160 | tf_op jit(solution)/shard_map/convert_element_type | solution.py:262
  3.9 0.7 %copy-done.4 = bf16[4,2048]{1,0:T(4,128)(2,1)S(1)} copy-done((bf16[4,2048]{1,0:T(4,128)(2,1)S(1)}, bf16[4,2048]{1,0:T(4,128)(2,1)}, u32[]{:S(2)}) %copy-start.4) | copy-done | bytes 16408
  4.6 0.7 %copy-done.8 = bf16[4,512]{1,0:T(4,128)(2,1)S(1)} copy-done((bf16[4,512]{1,0:T(4,128)(2,1)S(1)}, bf16[4,512]{1,0:T(4,128)(2,1)}, u32[]{:S(2)}) %copy-start.8) | copy-done | bytes 4120
  5.3 0.7 %copy-done.9 = bf16[4,512]{1,0:T(4,128)(2,1)S(1)} copy-done((bf16[4,512]{1,0:T(4,128)(2,1)S(1)}, bf16[4,512]{1,0:T(4,128)(2,1)}, u32[]{:S(2)}) %copy-start.9) | copy-done | bytes 4120
  6.0 0.7 %copy-done.10 = bf16[4,512]{1,0:T(4,128)(2,1)S(1)} copy-done((bf16[4,512]{1,0:T(4,128)(2,1)S(1)}, bf16[4,512]{1,0:T(4,128)(2,1)}, u32[]{:S(2)}) %copy-start.10) | copy-done | bytes 4120
  8.2 2.4 %collective-permute-start.2 = (bf16[12,2048]{1,0:T(8,128)(2,1)S(1)}, bf16[12,2048]{1,0:T(8,128)(2,1)S(1)}, u32[]{:S(2)}, u32[]{:S(2)}) collective-permute-start(bf16[12,2048]{1,0:T(8,128)(2,1)S(1)} %plane_message.1.own.m0), channel_id=1, source_target_pairs={{0,6},{2,4},{4,2},{6,0},{8,14},{10,12},{12,10},{14,8},{16,22},{18,... | collective-permute-start | bytes 147464 | tf_op jit(solution)/shard_map/ppermute | solution.py:21
  11.3 1.7 %collective-permute-start.6 = (bf16[256,512]{1,0:T(8,128)(2,1)}, bf16[256,512]{1,0:T(8,128)(2,1)S(1)}, u32[]{:S(2)}, u32[]{:S(2)}) collective-permute-start(bf16[256,512]{1,0:T(8,128)(2,1)} %k0.1), channel_id=1, source_target_pairs={{0,4},{2,6},{4,0},{6,2},{8,12},{10,14},{12,8},{14,10},{16,20},{18,... | collective-permute-start | bytes 786440 | tf_op jit(solution)/shard_map/ppermute | solution.py:21
  16.6 0.7 %gather_fusion.1 = s32[32]{0:T(128)S(1)} fusion(s32[64]{0:T(128)S(1)} %copy-done, s32[1024]{0:T(1024)S(1)} %pad_clamp_fusion), kind=kCustom, calls=%fused_computation.1 | custom fusion | bytes 384 | tf_op jit(solution)/shard_map/gather | solution.py:338
  18.7 2.5 %collective-permute-done.6.k2 = bf16[256,512]{1,0:T(8,128)(2,1)S(1)} collective-permute-done((bf16[256,512]{1,0:T(8,128)(2,1)}, bf16[256,512]{1,0:T(8,128)(2,1)S(1)}, u32[]{:S(2)}, u32[]{:S(2)}) %collective-permute-start.6) | collective-permute-done | bytes 262176 | tf_op jit(solution)/shard_map/ppermute | solution.py:21
  21.2 5.3 %collective-permute-done.9.v2 = bf16[256,512]{1,0:T(8,128)(2,1)S(1)} collective-permute-done((bf16[256,512]{1,0:T(8,128)(2,1)}, bf16[256,512]{1,0:T(8,128)(2,1)S(1)}, u32[]{:S(2)}, u32[]{:S(2)}) %collective-permute-start.9) | collective-permute-done | bytes 262176 | tf_op jit(solution)/shard_map/ppermute | solution.py:21
  26.8 2.8 %collective-permute-start.3 = (bf16[16,2048]{1,0:T(8,128)(2,1)S(1)}, bf16[16,2048]{1,0:T(8,128)(2,1)S(1)}, u32[]{:S(2)}, u32[]{:S(2)}) collective-permute-start(bf16[16,2048]{1,0:T(8,128)(2,1)S(1)} %column_queries.1.mine), channel_id=1, source_target_pairs={{0,16},{2,18},{4,20},{6,22},{8,24},{10,26},{12,28},{14,30},{16,0},... | collective-permute-start | bytes 196616 | tf_op jit(solution)/shard_map/ppermute | solution.py:21
  29.6 4.2 %collective-permute-done.3.other = bf16[16,2048]{1,0:T(8,128)(2,1)S(1)} collective-permute-done((bf16[16,2048]{1,0:T(8,128)(2,1)S(1)}, bf16[16,2048]{1,0:T(8,128)(2,1)S(1)}, u32[]{:S(2)}, u32[]{:S(2)}) %collective-permute-start.3) | collective-permute-done | bytes 65568 | tf_op jit(solution)/shard_map/ppermute | solution.py:21
  33.8 0.8 %collective-permute-start.4 = (bf16[20,2048]{1,0:T(8,128)(2,1)S(1)}, bf16[20,2048]{1,0:T(8,128)(2,1)S(1)}, u32[]{:S(2)}, u32[]{:S(2)}) collective-permute-start(bf16[20,2048]{1,0:T(8,128)(2,1)S(1)} %more_queries.1.mine), channel_id=1, source_target_pairs={{0,8},{2,10},{4,12},{6,14},{8,0},{10,2},{12,4},{14,6},{16,24},{18,... | collective-permute-start | bytes 245768 | tf_op jit(solution)/shard_map/ppermute | solution.py:21
  34.8 3.6 %collective-permute-done.4.other = bf16[20,2048]{1,0:T(8,128)(2,1)S(1)} collective-permute-done((bf16[20,2048]{1,0:T(8,128)(2,1)S(1)}, bf16[20,2048]{1,0:T(8,128)(2,1)S(1)}, u32[]{:S(2)}, u32[]{:S(2)}) %collective-permute-start.4) | collective-permute-done | bytes 81952 | tf_op jit(solution)/shard_map/ppermute | solution.py:21
  38.5 1.9 %plane_attention.1 = (bf16[16,2176]{1,0:T(8,128)(2,1)S(1)}, f32[16,2048]{1,0:T(8,128)S(1)}, f32[16,128]{1,0:T(8,128)S(1)}) custom-call(bf16[32,40]{1,0:T(8,128)(2,1)S(1)} %fusion.2.perm, f32[32,48]{1,0:T(8,128)S(1)} %add_convert_fusion.allowed, bf16[20,2048]{1,0:T(8,128)(2,1)S(1)} %more_queries.1.mine, bf16[20,2048]{1,0:T(8,128)(2,1)S(1)} %collective-permute-done.4.other, ...), custom_call_target="tpu_custom_call" | custom-call | tf_op jit(solution)/shard_map/plane_attention/pallas_call | solution.py:32
  40.4 0.9 %collective-permute-start.11 = (bf16[16,2176]{1,0:T(8,128)(2,1)S(1)}, bf16[16,2176]{1,0:T(8,128)(2,1)S(1)}, u32[]{:S(2)}, u32[]{:S(2)}) collective-permute-start(bf16[16,2176]{1,0:T(8,128)(2,1)S(1)} %get-tuple-element.13), channel_id=1, source_target_pairs={{0,8},{2,10},{4,12},{6,14},{8,0},{10,2},{12,4},{14,6},{16,24},{18,... | collective-permute-start | bytes 208904 | tf_op jit(solution)/shard_map/ppermute | solution.py:21
  41.3 3.4 %collective-permute-done.11.got = bf16[16,2176]{1,0:T(8,128)(2,1)S(1)} collective-permute-done((bf16[16,2176]{1,0:T(8,128)(2,1)S(1)}, bf16[16,2176]{1,0:T(8,128)(2,1)S(1)}, u32[]{:S(2)}, u32[]{:S(2)}) %collective-permute-start.11) | collective-permute-done | bytes 69664 | tf_op jit(solution)/shard_map/ppermute | solution.py:21
  45.0 2.6 %collective-permute-start.12 = (bf16[8,2176]{1,0:T(8,128)(2,1)S(1)}, bf16[8,2176]{1,0:T(8,128)(2,1)S(1)}, u32[]{:S(2)}, u32[]{:S(2)}) collective-permute-start(bf16[8,2176]{1,0:T(8,128)(2,1)S(1)} %get-tuple-element.16), channel_id=1, source_target_pairs={{0,16},{2,18},{4,20},{6,22},{8,24},{10,26},{12,28},{14,30},{16,0},... | collective-permute-start | bytes 104456 | tf_op jit(solution)/shard_map/ppermute | solution.py:21
  47.6 2.3 %collective-permute-done.12.got = bf16[8,2176]{1,0:T(8,128)(2,1)S(1)} collective-permute-done((bf16[8,2176]{1,0:T(8,128)(2,1)S(1)}, bf16[8,2176]{1,0:T(8,128)(2,1)S(1)}, u32[]{:S(2)}, u32[]{:S(2)}) %collective-permute-start.12) | collective-permute-done | bytes 34848 | tf_op jit(solution)/shard_map/ppermute | solution.py:21
  50.2 1.5 %collective-permute-start.13 = (f32[8,128]{1,0:T(8,128)S(1)}, f32[8,128]{1,0:T(8,128)S(1)}, u32[]{:S(2)}, u32[]{:S(2)}) collective-permute-start(f32[8,128]{1,0:T(8,128)S(1)} %get-tuple-element.18.squares), channel_id=1, source_target_pairs={{0,1},{1,0},{2,3},{3,2},{4,5},{5,4},{6,7},{7,6},{8,9},{9,8},{10,11... | collective-permute-start | bytes 12296 | tf_op jit(solution)/shard_map/ppermute | solution.py:21
  51.7 2.1 %collective-permute-done.13.other = f32[8,128]{1,0:T(8,128)S(1)} collective-permute-done((f32[8,128]{1,0:T(8,128)S(1)}, f32[8,128]{1,0:T(8,128)S(1)}, u32[]{:S(2)}, u32[]{:S(2)}) %collective-permute-start.13) | collective-permute-done | bytes 4128 | tf_op jit(solution)/shard_map/ppermute | solution.py:21
  53.8 0.7 %normalize.1 = (bf16[4,2048]{1,0:T(4,128)(2,1)}, bf16[2,2048]{1,0:T(2,128)(2,1)}, bf16[1,2048]{1,0:T(2,128)(2,1)}) custom-call(f32[8,2048]{1,0:T(8,128)S(1)} %get-tuple-element.17.att, f32[8,128]{1,0:T(8,128)S(1)} %get-tuple-element.18.squares, f32[8,128]{1,0:T(8,128)S(1)} %collective-permute-done.13.other, f32[1,2048]{1,0:T(1,128)S(1)} %bitcast.11), custom_call_target="tpu_custom_call" | custom-call | tf_op jit(solution)/shard_map/normalize/pallas_call | solution.py:32
  (92 shorter events, 8.8 us)
Async XLA Ops:
  0.6 15.3 %copy-start = (s32[64]{0:T(128)S(1)}, s32[64]{0:T(128)}, u32[]{:S(2)}) copy-start(s32[64]{0:T(128)} %param.24) | copy-start | bytes 772
  0.6 3.2 %copy-start.3 = (bf16[18,512]{1,0:T(8,128)(2,1)S(1)}, bf16[18,512]{1,0:T(8,128)(2,1)}, u32[]{:S(2)}) copy-start(bf16[18,512]{1,0:T(8,128)(2,1)} %table.1) | copy-start | bytes 55300
  3.1 0.7 %copy-start.15 = (bf16[512]{0:T(512)(128)(2,1)S(1)}, bf16[512]{0:T(512)(128)(2,1)}, u32[]{:S(2)}) copy-start(bf16[512]{0:T(512)(128)(2,1)} %param.33) | copy-start | bytes 3076
  3.2 0.7 %copy-start.7 = (bf16[4,512]{1,0:T(4,128)(2,1)S(1)}, bf16[4,512]{1,0:T(4,128)(2,1)}, u32[]{:S(2)}) copy-start(bf16[4,512]{1,0:T(4,128)(2,1)} %span_k.1) | copy-start | bytes 12292
  3.9 0.7 %copy-start.4 = (bf16[4,2048]{1,0:T(4,128)(2,1)S(1)}, bf16[4,2048]{1,0:T(4,128)(2,1)}, u32[]{:S(2)}) copy-start(bf16[4,2048]{1,0:T(4,128)(2,1)} %fq.1) | copy-start | bytes 49156
  7.3 0.7 %copy-start.12 = (bf16[4,512]{1,0:T(4,128)(2,1)S(1)}, bf16[4,512]{1,0:T(4,128)(2,1)}, u32[]{:S(2)}) copy-start(bf16[4,512]{1,0:T(4,128)(2,1)} %rv.1) | copy-start | bytes 12292
  8.2 9.9 %collective-permute-start.2 = (bf16[12,2048]{1,0:T(8,128)(2,1)S(1)}, bf16[12,2048]{1,0:T(8,128)(2,1)S(1)}, u32[]{:S(2)}, u32[]{:S(2)}) collective-permute-start(bf16[12,2048]{1,0:T(8,128)(2,1)S(1)} %plane_message.1.own.m0), channel_id=1, source_target_pairs={{0,6},{2,4},{4,2},{6,0},{8,14},{10,12},{12,10},{14,8},{16,22},{18,... | collective-permute-start | bytes 147464 | tf_op jit(solution)/shard_map/ppermute | solution.py:21
  10.6 7.5 %collective-permute-start.1 = (bf16[12,2048]{1,0:T(8,128)(2,1)S(1)}, bf16[12,2048]{1,0:T(8,128)(2,1)S(1)}, u32[]{:S(2)}, u32[]{:S(2)}) collective-permute-start(bf16[12,2048]{1,0:T(8,128)(2,1)S(1)} %plane_message.1.own.m0), channel_id=1, source_target_pairs={{0,4},{2,6},{4,0},{6,2},{8,12},{10,14},{12,8},{14,10},{16,20},{18,... | collective-permute-start | bytes 147464 | tf_op jit(solution)/shard_map/ppermute | solution.py:21
  11.2 15.4 %collective-permute-start = (bf16[12,2048]{1,0:T(8,128)(2,1)S(1)}, bf16[12,2048]{1,0:T(8,128)(2,1)S(1)}, u32[]{:S(2)}, u32[]{:S(2)}) collective-permute-start(bf16[12,2048]{1,0:T(8,128)(2,1)S(1)} %plane_message.1.own.m0), channel_id=1, source_target_pairs={{0,2},{2,0},{4,6},{6,4},{8,10},{10,8},{12,14},{14,12},{16,18},{18,... | collective-permute-start | bytes 147464 | tf_op jit(solution)/shard_map/ppermute | solution.py:21
  11.3 9.9 %collective-permute-start.6 = (bf16[256,512]{1,0:T(8,128)(2,1)}, bf16[256,512]{1,0:T(8,128)(2,1)S(1)}, u32[]{:S(2)}, u32[]{:S(2)}) collective-permute-start(bf16[256,512]{1,0:T(8,128)(2,1)} %k0.1), channel_id=1, source_target_pairs={{0,4},{2,6},{4,0},{6,2},{8,12},{10,14},{12,8},{14,10},{16,20},{18,... | collective-permute-start | bytes 786440 | tf_op jit(solution)/shard_map/ppermute | solution.py:21
  13.0 13.5 %collective-permute-start.9 = (bf16[256,512]{1,0:T(8,128)(2,1)}, bf16[256,512]{1,0:T(8,128)(2,1)S(1)}, u32[]{:S(2)}, u32[]{:S(2)}) collective-permute-start(bf16[256,512]{1,0:T(8,128)(2,1)} %v0.1), channel_id=1, source_target_pairs={{0,4},{2,6},{4,0},{6,2},{8,12},{10,14},{12,8},{14,10},{16,20},{18,... | collective-permute-start | bytes 786440 | tf_op jit(solution)/shard_map/ppermute | solution.py:21
  16.6 1.5 %copy-start.1 = (bf16[256,512]{1,0:T(8,128)(2,1)S(1)}, bf16[256,512]{1,0:T(8,128)(2,1)}, u32[]{:S(2)}) copy-start(bf16[256,512]{1,0:T(8,128)(2,1)} %k0.1) | copy-start | bytes 786436
  16.6 1.6 %copy-start.2 = (bf16[256,512]{1,0:T(8,128)(2,1)S(1)}, bf16[256,512]{1,0:T(8,128)(2,1)}, u32[]{:S(2)}) copy-start(bf16[256,512]{1,0:T(8,128)(2,1)} %v0.1) | copy-start | bytes 786436
  17.9 8.7 %copy-start.5 = (bf16[4,2048]{1,0:T(4,128)(2,1)S(1)}, bf16[4,2048]{1,0:T(4,128)(2,1)}, u32[]{:S(2)}) copy-start(bf16[4,2048]{1,0:T(4,128)(2,1)} %span_q.1) | copy-start | bytes 49156
  18.1 20.4 %collective-permute-start.5 = (bf16[256,512]{1,0:T(8,128)(2,1)S(1)}, bf16[256,512]{1,0:T(8,128)(2,1)S(1)}, u32[]{:S(2)}, u32[]{:S(2)}) collective-permute-start(bf16[256,512]{1,0:T(8,128)(2,1)S(1)} %copy-done.1), channel_id=1, source_target_pairs={{0,2},{2,0},{4,6},{6,4},{8,10},{10,8},{12,14},{14,12},{16,18},{18,... | collective-permute-start | bytes 786440 | tf_op jit(solution)/shard_map/ppermute | solution.py:21
  18.2 20.3 %collective-permute-start.8 = (bf16[256,512]{1,0:T(8,128)(2,1)S(1)}, bf16[256,512]{1,0:T(8,128)(2,1)S(1)}, u32[]{:S(2)}, u32[]{:S(2)}) collective-permute-start(bf16[256,512]{1,0:T(8,128)(2,1)S(1)} %copy-done.2), channel_id=1, source_target_pairs={{0,2},{2,0},{4,6},{6,4},{8,10},{10,8},{12,14},{14,12},{16,18},{18,... | collective-permute-start | bytes 786440 | tf_op jit(solution)/shard_map/ppermute | solution.py:21
  21.2 17.3 %collective-permute-start.7 = (bf16[256,512]{1,0:T(8,128)(2,1)S(1)}, bf16[256,512]{1,0:T(8,128)(2,1)S(1)}, u32[]{:S(2)}, u32[]{:S(2)}) collective-permute-start(bf16[256,512]{1,0:T(8,128)(2,1)S(1)} %collective-permute-done.6.k2), channel_id=1, source_target_pairs={{0,2},{2,0},{4,6},{6,4},{8,10},{10,8},{12,14},{14,12},{16,18},{18,... | collective-permute-start | bytes 786440 | tf_op jit(solution)/shard_map/ppermute | solution.py:21
  26.5 12.0 %collective-permute-start.10 = (bf16[256,512]{1,0:T(8,128)(2,1)S(1)}, bf16[256,512]{1,0:T(8,128)(2,1)S(1)}, u32[]{:S(2)}, u32[]{:S(2)}) collective-permute-start(bf16[256,512]{1,0:T(8,128)(2,1)S(1)} %collective-permute-done.9.v2), channel_id=1, source_target_pairs={{0,2},{2,0},{4,6},{6,4},{8,10},{10,8},{12,14},{14,12},{16,18},{18,... | collective-permute-start | bytes 786440 | tf_op jit(solution)/shard_map/ppermute | solution.py:21
  26.8 7.0 %collective-permute-start.3 = (bf16[16,2048]{1,0:T(8,128)(2,1)S(1)}, bf16[16,2048]{1,0:T(8,128)(2,1)S(1)}, u32[]{:S(2)}, u32[]{:S(2)}) collective-permute-start(bf16[16,2048]{1,0:T(8,128)(2,1)S(1)} %column_queries.1.mine), channel_id=1, source_target_pairs={{0,16},{2,18},{4,20},{6,22},{8,24},{10,26},{12,28},{14,30},{16,0},... | collective-permute-start | bytes 196616 | tf_op jit(solution)/shard_map/ppermute | solution.py:21
  33.8 4.7 %collective-permute-start.4 = (bf16[20,2048]{1,0:T(8,128)(2,1)S(1)}, bf16[20,2048]{1,0:T(8,128)(2,1)S(1)}, u32[]{:S(2)}, u32[]{:S(2)}) collective-permute-start(bf16[20,2048]{1,0:T(8,128)(2,1)S(1)} %more_queries.1.mine), channel_id=1, source_target_pairs={{0,8},{2,10},{4,12},{6,14},{8,0},{10,2},{12,4},{14,6},{16,24},{18,... | collective-permute-start | bytes 245768 | tf_op jit(solution)/shard_map/ppermute | solution.py:21
  40.4 4.4 %collective-permute-start.11 = (bf16[16,2176]{1,0:T(8,128)(2,1)S(1)}, bf16[16,2176]{1,0:T(8,128)(2,1)S(1)}, u32[]{:S(2)}, u32[]{:S(2)}) collective-permute-start(bf16[16,2176]{1,0:T(8,128)(2,1)S(1)} %get-tuple-element.13), channel_id=1, source_target_pairs={{0,8},{2,10},{4,12},{6,14},{8,0},{10,2},{12,4},{14,6},{16,24},{18,... | collective-permute-start | bytes 208904 | tf_op jit(solution)/shard_map/ppermute | solution.py:21
  45.0 4.9 %collective-permute-start.12 = (bf16[8,2176]{1,0:T(8,128)(2,1)S(1)}, bf16[8,2176]{1,0:T(8,128)(2,1)S(1)}, u32[]{:S(2)}, u32[]{:S(2)}) collective-permute-start(bf16[8,2176]{1,0:T(8,128)(2,1)S(1)} %get-tuple-element.16), channel_id=1, source_target_pairs={{0,16},{2,18},{4,20},{6,22},{8,24},{10,26},{12,28},{14,30},{16,0},... | collective-permute-start | bytes 104456 | tf_op jit(solution)/shard_map/ppermute | solution.py:21
  49.9 3.9 %copy-start.6 = (f32[2048]{0:T(1024)S(1)}, f32[2048]{0:T(1024)}, u32[]{:S(2)}) copy-start(f32[2048]{0:T(1024)} %param.36) | copy-start | bytes 24580
  50.2 3.6 %collective-permute-start.13 = (f32[8,128]{1,0:T(8,128)S(1)}, f32[8,128]{1,0:T(8,128)S(1)}, u32[]{:S(2)}, u32[]{:S(2)}) collective-permute-start(f32[8,128]{1,0:T(8,128)S(1)} %get-tuple-element.18.squares), channel_id=1, source_target_pairs={{0,1},{1,0},{2,3},{3,2},{4,5},{5,4},{6,7},{7,6},{8,9},{9,8},{10,11... | collective-permute-start | bytes 12296 | tf_op jit(solution)/shard_map/ppermute | solution.py:21
  (8 other events, 5.4 us)

commit v2 on v1

v2 whole, which is shorter than its diff:
```python
import functools

import jax
import jax.numpy as jnp
from jax import lax
from jax.experimental import pallas as pl
from jax.experimental.pallas import tpu as pltpu
from jax.sharding import PartitionSpec as P

HD = 128
GROUP = 4
NEG = -1e30
EPS = 1e-6
F32 = jnp.float32
BF16 = jnp.bfloat16
VMEM = pltpu.VMEM
PLAN_LIMIT = 60 * 2**20


def exchange(value, axis, mask):
    pairs = [(source, source ^ mask) for source in range(lax.axis_size(axis))]
    return lax.ppermute(value, axis, pairs)


def call(
    kernel, name, out_shape, *operands, scratch=(), places=None, aliases=None, out_any=(), limit=16 * 2**20
):
    places = places or {}
    in_specs = [
        pl.BlockSpec(memory_space=places.get(i, VMEM)) for i in range(len(operands))
    ]
    single = not isinstance(out_shape, (list, tuple))
    out_specs = pl.BlockSpec(memory_space=VMEM)
    aliases = aliases or {}
    if not single:
        moved = {*aliases.values(), *out_any}
        out_specs = [
            pl.BlockSpec(memory_space=pl.ANY if i in moved else VMEM)
            for i in range(len(out_shape))
        ]
    return pl.pallas_call(
        kernel,
        out_shape=out_shape,
        in_specs=in_specs,
        out_specs=out_specs,
        scratch_shapes=list(scratch),
        input_output_aliases=aliases,
        compiler_params=pltpu.CompilerParams(vmem_limit_bytes=limit),
        name=name,
    )(*operands)


def iota(shape, dim):
    return lax.broadcasted_iota(jnp.int32, shape, dim)


def split_index(index, size):
    whole = ((index.astype(F32) + 0.5) * (1.0 / size)).astype(jnp.int32)
    return whole, index - whole * size


def at_lane(row, index):
    lanes = iota((index.shape[0], row.shape[1]), 1)
    return jnp.where(lanes == index, row.astype(F32), 0.0).sum(axis=1, keepdims=True)


def plan_kernel(
    sizes, place,
    ids_h, idx1_h, idx2_h, span_frames_h, table_h, span_k_h, span_v_h,
    fk_h, fv_h, rk_h, rv_h, mk_h, mv_h, cache_k_h, cache_v_h,
    k0, v0, perm, allowed, *scratch,
):
    spans, frames, n1, n2, blocks, block_rows, mask_bits = sizes
    given = (ids_h, idx1_h, idx2_h, span_frames_h, table_h, span_k_h, span_v_h,
             fk_h, fv_h, rk_h, rv_h, mk_h, mv_h, cache_k_h, cache_v_h)
    held, (whole_k, whole_v, sems) = scratch[:-3], scratch[-3:]
    cached = cache_k_h.shape[0]
    extras = whole_k.shape[0] - cached
    staged = (whole_k.at[0:cached], whole_v.at[0:cached])
    copies = [
        pltpu.make_async_copy(source, target, sems.at[i])
        for i, (source, target) in enumerate(zip(given, (*held, *staged)))
    ]
    for copy in copies:
        copy.start()
    for copy in copies[:-2]:
        copy.wait()
    ids, idx1, idx2, span_frames, table, span_k, span_v, fk, fv, rk, rv, mk, mv = held
    me = place[0]
    own_block = me >> 2
    picked = n1 + n2

    hits = at_lane(ids[...], iota((spans, 1), 0))
    hits = (iota((spans, table.shape[0]), 1).astype(F32) == hits).astype(BF16)
    terms = jnp.dot(hits, table[...], preferred_element_type=F32)
    position = me * frames + iota((frames, 1), 0)

    def listed(idx):
        same = jnp.where(idx[...] == position, 1.0, 0.0)
        return same.sum(axis=1, keepdims=True) > 0.0

    first = listed(idx1)
    second = listed(idx2)
    sets = [span_k[...].astype(F32) + terms, span_v[...].astype(F32)]
    shown = []
    for frame, revealed, token in ((fk, rk, mk), (fv, rv, mv)):
        frame = frame[...].astype(F32)
        token = token[...].astype(F32).reshape(1, -1)
        sets.append(jnp.where(first, token, frame))
        shown.append(
            jnp.where(second, token, jnp.where(first, revealed[...].astype(F32), frame))
        )
    sets += shown
    for i, (whole, target) in enumerate(((whole_k, k0), (whole_v, v0))):
        rest = jnp.zeros((extras - 3 * spans, whole.shape[1]), F32)
        whole[cached:, :] = jnp.concatenate(sets[i::2] + [rest], axis=0).astype(BF16)
        copies[i - 2].wait()
    out_copies = [
        pltpu.make_async_copy(whole, target, sems.at[len(given) + i])
        for i, (whole, target) in enumerate(((whole_k, k0), (whole_v, v0)))
    ]
    for copy in out_copies:
        copy.start()

    rows, both = perm.shape
    depth = both // 2
    row = iota((rows, 1), 0)
    block, at = split_index(row, block_rows)
    mask = jnp.zeros_like(block)
    for i in range(mask_bits):
        mask = mask + (((block >> i) & 1) << (mask_bits + 1 - i))
    half = blocks // 2
    span_at = block * spans + at + jnp.where(block < half, 0, depth - half * spans)
    pick_at = depth - blocks * picked + (own_block ^ (mask >> 2)) * picked + at - spans
    is_span = at < spans
    is_pick = (at >= spans) & (at < spans + picked)
    lane = iota((1, both), 1)
    same = (is_span & (lane == span_at)) | (
        is_pick & ((lane == pick_at) | (lane == pick_at + depth))
    )
    perm[...] = jnp.where(same, 1.0, 0.0).astype(BF16)

    count = allowed.shape[1]
    lane = iota((1, count), 1)
    member, key_at = split_index(lane, extras)
    key = jnp.where(key_at < spans, (member ^ me) * spans + key_at, -1)
    total = span_frames.shape[1]
    numbers = jnp.broadcast_to(span_frames[...].astype(F32), (8, total)).astype(BF16)
    key_hits = jnp.where(iota((total, 1), 0) == key, 1.0, 0.0).astype(BF16)
    key_frames = jnp.dot(numbers, key_hits, preferred_element_type=F32)[0:1]
    row_frames = at_lane(span_frames[...], jnp.where(is_span, (me ^ mask) * spans + at, -1))
    sees = (key_at < spans) & ((at >= spans) | (key_frames <= row_frames))
    in_first = (key_at >= spans) & (key_at < 2 * spans)
    in_second = (key_at >= 2 * spans) & (key_at < 3 * spans)
    sees = sees | (in_first & is_pick & (at < spans + n1))
    sees = sees | (in_second & is_pick & (at >= spans + n1))
    allowed[...] = jnp.where(sees, 1.0, 0.0)
    for copy in out_copies:
        copy.wait()


def stacked(parts):
    return jnp.concatenate([part.astype(F32) for part in parts], axis=0).astype(BF16)


def select_kernel(sizes, place, idx1, idx2, span_q, own, q1, q2, q3, out):
    spans, frames, n1, n2 = sizes
    me = place[0]
    column = me & 3
    picked = n1 + n2
    shape = (out.shape[0], spans + 4 * frames)
    row = iota((shape[0], 1), 0)
    block, at = split_index(jnp.maximum(row - spans, 0), picked)
    owner = block * 4 + column
    wanted = jnp.where(
        at < n1,
        at_lane(idx1[...], owner * n1 + at),
        at_lane(idx2[...], owner * n2 + at - n1),
    )
    lane = iota((1, shape[1]), 1)
    member, at = split_index(jnp.maximum(lane - spans, 0), frames)
    position = ((member ^ me) * frames + at).astype(F32)
    chosen = jnp.where((lane >= spans) & (row >= spans) & (wanted == position), 1.0, 0.0)
    copied = jnp.where((row < spans) & (lane == row), 1.0, 0.0)
    pick = (chosen + copied).astype(BF16)
    given = stacked([q[...] for q in (span_q, own, q1, q2, q3)])
    out[...] = jnp.dot(pick, given, preferred_element_type=F32).astype(BF16)


def tie_kernel(*_):
    pass


def tie(*arrays):
    count = len(arrays)
    return call(
        tie_kernel,
        "arrived",
        [jax.ShapeDtypeStruct(array.shape, array.dtype) for array in arrays],
        *arrays,
        places={i: pl.ANY for i in range(count)},
        aliases={i: i for i in range(count)},
    )


def grow_kernel(spans, mine, other, out):
    a = mine[...].astype(F32)
    b = other[...].astype(F32)
    out[...] = jnp.concatenate(
        [a[:spans], b[:spans], a[spans:] + b[spans:]], axis=0
    ).astype(BF16)


def split_stats(stats):
    lane = lax.broadcasted_iota(jnp.int32, stats.shape, 1)
    stats = jnp.where(lane < 16, stats, 0.0)
    high = stats.astype(BF16).astype(F32)
    rest = stats - high
    middle = rest.astype(BF16).astype(F32)
    low = (rest - middle).astype(BF16).astype(F32)
    packed = high + pltpu.roll(middle, 16, 1) + pltpu.roll(low, 32, 1)
    return packed.astype(BF16)


def joined_stats(packed):
    packed = packed.astype(F32)
    return packed + pltpu.roll(packed, 112, 1) + pltpu.roll(packed, 96, 1)


def softmax_parts(heads, rows, queries, permit, key_refs, value_refs, extras, visit, before=None):
    scaling = HD ** (-0.5)
    cached = key_refs[0].shape[0] - extras
    stack = GROUP if rows * GROUP <= 128 else 1
    permit = jnp.concatenate([permit] * stack, axis=0) > 0.0
    nt = (((1,), (1,)), ((), ()))
    for g in range(heads):
        columns = slice(g * HD, (g + 1) * HD)
        keys = [ref[0:cached, columns] for ref in key_refs]
        keys.append(jnp.concatenate([ref[cached:, columns] for ref in key_refs], axis=0))
        values = [ref[0:cached, columns] for ref in value_refs]
        values.append(jnp.concatenate([ref[cached:, columns] for ref in value_refs], axis=0))
        for head in range(g * GROUP, (g + 1) * GROUP, stack):
            q = jnp.concatenate(
                [queries[:, (head + i) * HD : (head + i + 1) * HD] for i in range(stack)], axis=0
            )
            scores = [
                lax.dot_general(q, key, nt, preferred_element_type=F32) * scaling for key in keys
            ]
            scores[-1] = jnp.where(permit, scores[-1], NEG)
            top = functools.reduce(jnp.maximum, scores[:-1]).max(axis=1, keepdims=True)
            top = jnp.maximum(top, scores[-1].max(axis=1, keepdims=True))
            if before is not None:
                earlier = [ref[head * rows : (head + stack) * rows, :] for ref in before]
                top = jnp.maximum(top, earlier[0][:, 0:1])
            weights = [jnp.exp(s - top) for s in scores]
            total = functools.reduce(jnp.add, weights[:-1]).sum(axis=1, keepdims=True)
            total = total + weights[-1].sum(axis=1, keepdims=True)
            out = functools.reduce(
                jnp.add,
                [
                    jnp.dot(w.astype(BF16), value, preferred_element_type=F32)
                    for w, value in zip(weights, values)
                ],
            )
            top = jnp.broadcast_to(top, out.shape)
            if before is not None:
                scale = jnp.exp(earlier[0] - top)
                total = earlier[1] * scale + total
                out = earlier[2] * scale + out
            visit(head, stack, top, jnp.broadcast_to(total, out.shape), out)


def first_attention_kernel(
    heads, rows, extras, perm, allowed, mine, other, k0, k1, k2, v0, v1, v2,
    queries, tops, totals, sums,
):
    queries[...] = jnp.dot(
        perm[...], stacked([mine[...], other[...]]), preferred_element_type=F32
    ).astype(BF16)

    def visit(head, stack, top, total, out):
        place = slice(head * rows, (head + stack) * rows)
        tops[place, :] = top
        totals[place, :] = total
        sums[place, :] = out

    softmax_parts(
        heads, rows, queries, allowed[:, 0 : 3 * extras], (k0, k1, k2), (v0, v1, v2), extras, visit
    )


def second_attention_kernel(
    heads, rows, extras, keep, queries, allowed, tops, totals, sums, k3, v3,
    send, kept, kept_stats,
):
    wide = heads * GROUP * HD
    lane = iota((rows, HD), 1)
    held = [jnp.zeros((rows, HD), F32)]

    def visit(head, stack, top, total, out):
        out = out / total
        level = top + jnp.log(total)
        for i in range(stack):
            first = i * rows
            columns = slice((head + i) * HD, (head + i + 1) * HD)
            kept[:, columns] = out[first : first + keep]
            send[:, columns] = out[first + keep : first + rows].astype(BF16)
            held[0] = jnp.where(lane == head + i, level[first : first + rows], held[0])

    softmax_parts(
        heads, rows, queries, allowed[:, 3 * extras : 4 * extras], (k3,), (v3,), extras, visit,
        (tops, totals, sums),
    )
    kept_stats[...] = held[0][:keep]
    send[:, wide:] = split_stats(held[0][keep:])


def merge(heads, kept, kept_stats, got):
    wide = heads * GROUP * HD
    mine = kept_stats[...]
    theirs = joined_stats(got[:, wide:])
    top = jnp.maximum(mine, theirs)
    a = jnp.exp(mine - top)
    b = jnp.exp(theirs - top)
    total = a + b
    a = a / total
    b = b / total
    merged = []
    for h in range(heads * GROUP):
        columns = slice(h * HD, (h + 1) * HD)
        merged.append(
            kept[:, columns] * a[:, h : h + 1] + got[:, columns].astype(F32) * b[:, h : h + 1]
        )
    return merged, top + jnp.log(total)


def merge_kernel(heads, keep, kept, kept_stats, got, send, out, out_stats):
    wide = heads * GROUP * HD
    merged, stats = merge(heads, kept, kept_stats, got)
    for h, value in enumerate(merged):
        columns = slice(h * HD, (h + 1) * HD)
        out[:, columns] = value[:keep]
        send[:, columns] = value[keep:].astype(BF16)
    out_stats[...] = stats[:keep]
    send[:, wide:] = split_stats(stats[keep:])


def last_kernel(heads, kept, kept_stats, got, out, squares):
    merged, _ = merge(heads, kept, kept_stats, got)
    total = jnp.zeros_like(merged[0])
    for h, value in enumerate(merged):
        out[:, h * HD : (h + 1) * HD] = value
        total = total + value * value
    squares[...] = jnp.broadcast_to(total.sum(axis=1, keepdims=True), squares.shape)


def out_kernel(counts, columns_all, att, squares, other, gain, *outs):
    mean_sq = (squares[...] + other[...])[:, 0:1] / columns_all
    normed = att[...] * lax.rsqrt(mean_sq + EPS) * gain[...]
    at = 0
    for count, out in zip(counts, outs):
        out[...] = normed[at : at + count].astype(BF16)
        at += count


def per_device(
    cache_k,
    cache_v,
    span_q,
    span_k,
    span_v,
    span_frames,
    action_ids,
    action_table,
    frame_q,
    frame_k,
    frame_v,
    revealed_k,
    revealed_v,
    mask_k,
    mask_v,
    pass1_idx,
    pass2_idx,
    out_gain,
):
    owners = lax.axis_size("ctx")
    tp = lax.axis_size("tp")
    me = lax.axis_index("ctx")
    blocks = owners // 4
    spans = span_k.shape[0]
    frames = frame_k.shape[0]
    width = span_k.shape[1]
    q_width = span_q.shape[1]
    heads = width // HD
    n1 = pass1_idx.shape[0] // owners
    n2 = pass2_idx.shape[0] // owners
    picked = n1 + n2
    block_rows = -(-(spans + picked) // 8) * 8
    rows = blocks * block_rows

    bits = [1 << b for b in range(2, owners.bit_length() - 1)][::-1]

    depth = (blocks // 2) * spans + blocks * picked
    extras = -(-3 * spans // 16) * 16

    q2 = exchange(frame_q, "ctx", 2)
    q3 = exchange(frame_q, "ctx", 3)
    q1 = exchange(frame_q, "ctx", 1)
    small = (
        action_ids[None, :], pass1_idx[None, :], pass2_idx[None, :], span_frames[None, :],
        action_table, span_k, span_v, frame_k, frame_v, revealed_k, revealed_v,
        mask_k, mask_v,
    )
    sizes = (spans, frames, n1, n2, blocks, block_rows, len(bits))
    keys = cache_k.shape[0] + extras
    place = me.reshape(1)
    k0, v0, perm, allowed = call(
        functools.partial(plan_kernel, sizes),
        "plane_keys",
        [
            jax.ShapeDtypeStruct((keys, width), BF16),
            jax.ShapeDtypeStruct((keys, width), BF16),
            jax.ShapeDtypeStruct((rows, 2 * depth), BF16),
            jax.ShapeDtypeStruct((rows, 4 * extras), F32),
        ],
        place, *small, cache_k, cache_v,
        places={0: pltpu.SMEM, **{i + 1: pl.ANY for i in range(len(small) + 2)}},
        out_any=(0, 1),
        scratch=[pltpu.VMEM(array.shape, array.dtype) for array in small]
        + [pltpu.VMEM((keys, width), BF16)] * 2
        + [pltpu.SemaphoreType.DMA((len(small) + 4,))],
        limit=PLAN_LIMIT,
    )
    q1, q2, q3, k0, v0 = tie(q1, q2, q3, k0, v0)
    k2 = exchange(k0, "ctx", 2)
    v2 = exchange(v0, "ctx", 2)
    k1 = exchange(k0, "ctx", 1)
    v1 = exchange(v0, "ctx", 1)

    state = call(
        functools.partial(select_kernel, (spans, frames, n1, n2)),
        "column_queries",
        jax.ShapeDtypeStruct((spans + blocks * picked, q_width), BF16),
        place, pass1_idx[None, :], pass2_idx[None, :], span_q, frame_q, q1, q2, q3,
        places={0: pltpu.SMEM},
    )
    held = spans
    for bit in bits[:-1]:
        other = exchange(state, "ctx", bit)
        state = call(
            functools.partial(grow_kernel, held),
            "more_queries",
            jax.ShapeDtypeStruct((state.shape[0] + held, q_width), BF16),
            state, other,
        )
        held = 2 * held
    other = exchange(state, "ctx", bits[-1])
    other, k2, v2 = tie(other, k2, v2)
    k3 = exchange(k2, "ctx", 1)
    v3 = exchange(v2, "ctx", 1)

    keep = rows // 2
    packed = q_width + HD
    limit = (16 if blocks <= 4 else 40) * 2**20
    queries, *before = call(
        functools.partial(first_attention_kernel, heads, rows, extras),
        "plane_attention",
        [
            jax.ShapeDtypeStruct((rows, q_width), BF16),
            *[jax.ShapeDtypeStruct((rows * q_width // HD, HD), F32)] * 3,
        ],
        perm, allowed, state, other, k0, k1, k2, v0, v1, v2,
        limit=limit,
    )
    send, kept, stats = call(
        functools.partial(second_attention_kernel, heads, rows, extras, keep),
        "rest_attention",
        [
            jax.ShapeDtypeStruct((keep, packed), BF16),
            jax.ShapeDtypeStruct((keep, q_width), F32),
            jax.ShapeDtypeStruct((keep, HD), F32),
        ],
        queries, allowed, *before, k3, v3,
        limit=limit,
    )
    for bit in bits[:0:-1]:
        got = exchange(send, "ctx", bit)
        keep = keep // 2
        send, kept, stats = call(
            functools.partial(merge_kernel, heads, keep),
            "merge_partials",
            [
                jax.ShapeDtypeStruct((keep, packed), BF16),
                jax.ShapeDtypeStruct((keep, q_width), F32),
                jax.ShapeDtypeStruct((keep, HD), F32),
            ],
            kept, stats, got,
        )
    got = exchange(send, "ctx", bits[0])
    att, squares = call(
        functools.partial(last_kernel, heads),
        "merge_last",
        [
            jax.ShapeDtypeStruct((block_rows, q_width), F32),
            jax.ShapeDtypeStruct((block_rows, HD), F32),
        ],
        kept, stats, got,
    )
    other_squares = exchange(squares, "tp", 1)
    counts = (spans, n1, n2)
    return tuple(
        call(
            functools.partial(out_kernel, counts, float(tp * q_width)),
            "normalize",
            [jax.ShapeDtypeStruct((count, q_width), BF16) for count in counts],
            att, squares, other_squares, out_gain[None, :],
        )
    )


def solution(mesh):
    in_specs = (
        P("ctx", "tp"),
        P("ctx", "tp"),
        P("ctx", "tp"),
        P("ctx", "tp"),
        P("ctx", "tp"),
        P(),
        P("ctx"),
        P(None, "tp"),
        P("ctx", "tp"),
        P("ctx", "tp"),
        P("ctx", "tp"),
        P("ctx", "tp"),
        P("ctx", "tp"),
        P("tp"),
        P("tp"),
        P(),
        P(),
        P("tp"),
    )
    out_specs = (P("ctx", "tp"), P("ctx", "tp"), P("ctx", "tp"))
    return jax.shard_map(
        per_device, mesh=mesh, in_specs=in_specs, out_specs=out_specs, check_vma=False
    )
```

time: 55 us -> 43.4 us (0.79)
  local copies, waits for them, and re-layouts: 9.36 us -> 1.83 us
  waiting for transfers between devices: 23.5 us -> 16.1 us
  Pallas kernels: 3.45 us -> 9.15 us
  other arithmetic: 2.98 us -> 0 us
  starting transfers between devices: 14.4 us -> 15.2 us
    ppermute x14, waiting for transfers between devices: 23.5 us -> 16.1 us  [exchange(): return lax.ppermute(value, axis, pairs)]
    pallas_call x7 -> x10, Pallas kernels: 3.45 us -> 9.15 us  [call(): pl.pallas_call(kernel, out_shape=out_shape, in_specs=in_specs, out_specs=...]
    unnamed x36 -> x16, local copies, waits for them, and re-layouts: 6.54 us -> 1.83 us
    reduce_or x2 -> x0, other arithmetic: 1.68 us -> none  [the longest x1 0.84 us: per_device(): jnp.any(own_pos[:, None] == pass1_idx[None, :], axis=1)[:, None].astype(F32)]
    gather x2 -> x0, local copies, waits for them, and re-layouts: 1.36 us -> none  [the longest x1 0.7 us: per_device(): span_frames[jnp.where(is_span, (me ^ mask_of) * spans + at_row, 0)]]
    convert_element_type x5 -> x0, other arithmetic: 0.91 us -> none  [the longest x1 0.73 us: per_device(): hits = (action_ids[:, None] == actions[None, :]).astype(BF16)]
    ppermute x14, starting transfers between devices: 14.4 us -> 15.2 us  [exchange(): return lax.ppermute(value, axis, pairs)]
  transfers between devices with their start and end apart: 14 -> 14, of which waited for: 7 -> 7; matrix products, arithmetic and copies ran while one was open for 6% -> 0% of each run, Pallas kernels for 0% -> 13%
where the time goes in v2:
time: 43.4 us; the launch traced here: 43 us
  waiting for transfers between devices  16.1 us (37%)
  starting transfers between devices  15.2 us (35%)
  Pallas kernels  9.15 us (21%)
  local copies, waits for them, and re-layouts  1.83 us (4%)
  between operations  0.73 us (2%)
    ppermute x14, waiting for transfers between devices, exchange(): return lax.ppermute(value, axis, pairs)  16.1 us
    ppermute x14, starting transfers between devices, exchange(): return lax.ppermute(value, axis, pairs)  15.2 us
    pallas_call x10, Pallas kernels, call(): pl.pallas_call(kernel, out_shape=out_shape, in_specs=in_specs, out_specs=...  9.15 us
    unnamed x16, local copies, waits for them, and re-layouts  1.83 us
  transfers between devices with their start and end apart: 14, of which 7 were waited for; matrix products, arithmetic and copies ran while one was open for 0% of the time, Pallas kernels for 13%

profile of v2, /device:TPU:0, one launch (start us, length us, event | category | flops | bytes accessed | tf_op | source)
XLA Modules:
  0.0 43.0 jit_solution(15168385828949127844)
XLA Ops:
  0.6 3.0 %collective-permute-start.1 = (bf16[4,2048]{1,0:T(4,128)(2,1)}, bf16[4,2048]{1,0:T(4,128)(2,1)S(1)}, u32[]{:S(2)}, u32[]{:S(2)}) collective-permute-start(bf16[4,2048]{1,0:T(4,128)(2,1)} %own.1), channel_id=1, source_target_pairs={{0,4},{2,6},{4,0},{6,2},{8,12},{10,14},{12,8},{14,10},{16,20},{18,... | collective-permute-start | bytes 49160 | tf_op jit(solution)/shard_map/ppermute | solution.py:22
  3.9 2.8 %plane_keys.1 = (bf16[272,512]{1,0:T(8,128)(2,1)}, bf16[272,512]{1,0:T(8,128)(2,1)}, bf16[32,40]{1,0:T(8,128)(2,1)}, f32[32,64]{1,0:T(8,128)}) custom-call(s32[1]{0:T(128)} %bitcast.place, s32[1,4]{1,0:T(1,128)} %bitcast.11, s32[1,32]{1,0:T(1,128)} %bitcast.7, s32[1,16]{1,0:T(1,128)} %bitcast.9, s32[1,64]{1,0:T(1,128)} %bitcast.12, bf16[18,512]{1,0:T(8,128)(2,1)} %table_h.1, ...), custom_call_target="tpu_custom_call" | custom-call | tf_op jit(solution)/shard_map/plane_keys/pallas_call | solution.py:41
  6.7 0.4 collective-permute-done.2.__2_
  7.0 1.0 %copy-done = bf16[272,512]{1,0:T(8,128)(2,1)S(1)} copy-done((bf16[272,512]{1,0:T(8,128)(2,1)S(1)}, bf16[272,512]{1,0:T(8,128)(2,1)}, u32[]{:S(2)}) %copy-start) | copy-done | bytes 278552
  8.0 1.6 %collective-permute-start.5 = (bf16[272,512]{1,0:T(8,128)(2,1)}, bf16[272,512]{1,0:T(8,128)(2,1)S(1)}, u32[]{:S(2)}, u32[]{:S(2)}) collective-permute-start(bf16[272,512]{1,0:T(8,128)(2,1)} %get-tuple-element.34.k0), channel_id=1, source_target_pairs={{0,4},{2,6},{4,0},{6,2},{8,12},{10,14},{12,8},{14,10},{16,20},{18,... | collective-permute-start | bytes 835592 | tf_op jit(solution)/shard_map/ppermute | solution.py:22
  9.6 0.4 %collective-permute-start.6 = (bf16[272,512]{1,0:T(8,128)(2,1)S(1)}, bf16[272,512]{1,0:T(8,128)(2,1)S(1)}, u32[]{:S(2)}, u32[]{:S(2)}) collective-permute-start(bf16[272,512]{1,0:T(8,128)(2,1)S(1)} %get-tuple-element.35.v0), channel_id=1, source_target_pairs={{0,4},{2,6},{4,0},{6,2},{8,12},{10,14},{12,8},{14,10},{16,20},{18,... | collective-permute-start | bytes 835592 | tf_op jit(solution)/shard_map/ppermute | solution.py:22
  10.0 0.6 %copy-done.6 = s32[32]{0:T(128)S(1)} copy-done((s32[32]{0:T(128)S(1)}, s32[32]{0:T(128)}, u32[]{:S(2)}) %copy-start.6) | copy-done | bytes 152
  10.9 2.7 %collective-permute-start.3 = (bf16[16,2048]{1,0:T(8,128)(2,1)S(1)}, bf16[16,2048]{1,0:T(8,128)(2,1)S(1)}, u32[]{:S(2)}, u32[]{:S(2)}) collective-permute-start(bf16[16,2048]{1,0:T(8,128)(2,1)S(1)} %column_queries.1.mine), channel_id=1, source_target_pairs={{0,16},{2,18},{4,20},{6,22},{8,24},{10,26},{12,28},{14,30},{16,0},... | collective-permute-start | bytes 196616 | tf_op jit(solution)/shard_map/ppermute | solution.py:22
  13.7 3.9 %collective-permute-done.3.other = bf16[16,2048]{1,0:T(8,128)(2,1)S(1)} collective-permute-done((bf16[16,2048]{1,0:T(8,128)(2,1)S(1)}, bf16[16,2048]{1,0:T(8,128)(2,1)S(1)}, u32[]{:S(2)}, u32[]{:S(2)}) %collective-permute-start.3) | collective-permute-done | bytes 65568 | tf_op jit(solution)/shard_map/ppermute | solution.py:22
  17.6 0.4 collective-permute-start.4
  18.0 0.5 %collective-permute-start.8 = (bf16[272,512]{1,0:T(8,128)(2,1)S(1)}, bf16[272,512]{1,0:T(8,128)(2,1)S(1)}, u32[]{:S(2)}, u32[]{:S(2)}) collective-permute-start(bf16[272,512]{1,0:T(8,128)(2,1)S(1)} %get-tuple-element.35.v0), channel_id=1, source_target_pairs={{0,2},{2,0},{4,6},{6,4},{8,10},{10,8},{12,14},{14,12},{16,18},{18,... | collective-permute-start | bytes 835592 | tf_op jit(solution)/shard_map/ppermute | solution.py:22
  18.5 3.7 %collective-permute-done.4.__0_ = bf16[20,2048]{1,0:T(8,128)(2,1)S(1)} collective-permute-done((bf16[20,2048]{1,0:T(8,128)(2,1)S(1)}, bf16[20,2048]{1,0:T(8,128)(2,1)S(1)}, u32[]{:S(2)}, u32[]{:S(2)}) %collective-permute-start.4) | collective-permute-done | bytes 81952 | tf_op jit(solution)/shard_map/ppermute | solution.py:22
  22.3 1.0 %collective-permute-done.6.__2_ = bf16[272,512]{1,0:T(8,128)(2,1)S(1)} collective-permute-done((bf16[272,512]{1,0:T(8,128)(2,1)S(1)}, bf16[272,512]{1,0:T(8,128)(2,1)S(1)}, u32[]{:S(2)}, u32[]{:S(2)}) %collective-permute-start.6) | collective-permute-done | bytes 278560 | tf_op jit(solution)/shard_map/ppermute | solution.py:22
  23.3 0.5 %collective-permute-start.10 = (bf16[272,512]{1,0:T(8,128)(2,1)S(1)}, bf16[272,512]{1,0:T(8,128)(2,1)S(1)}, u32[]{:S(2)}, u32[]{:S(2)}) collective-permute-start(bf16[272,512]{1,0:T(8,128)(2,1)S(1)} %get-tuple-element.38.v2), channel_id=1, source_target_pairs={{0,2},{2,0},{4,6},{6,4},{8,10},{10,8},{12,14},{14,12},{16,18},{18,... | collective-permute-start | bytes 835592 | tf_op jit(solution)/shard_map/ppermute | solution.py:22
  24.0 2.6 %plane_attention.1 = (bf16[32,2048]{1,0:T(8,128)(2,1)S(1)}, f32[512,128]{1,0:T(8,128)S(1)}, f32[512,128]{1,0:T(8,128)S(1)}, f32[512,128]{1,0:T(8,128)S(1)}) custom-call(bf16[32,40]{1,0:T(8,128)(2,1)S(1)} %copy-done.5, f32[32,64]{1,0:T(8,128)S(1)} %copy-done.1, bf16[20,2048]{1,0:T(8,128)(2,1)S(1)} %more_queries.1.mine, ...), custom_call_target="tpu_custom_call" | custom-call | tf_op jit(solution)/shard_map/plane_attention/pallas_call | solution.py:41
  26.6 2.3 %rest_attention.1 = (bf16[16,2176]{1,0:T(8,128)(2,1)S(1)}, f32[16,2048]{1,0:T(8,128)S(1)}, f32[16,128]{1,0:T(8,128)S(1)}) custom-call(bf16[32,2048]{1,0:T(8,128)(2,1)S(1)} %get-tuple-element.39.queries, f32[32,64]{1,0:T(8,128)S(1)} %copy-done.1, f32[512,128]{1,0:T(8,128)S(1)} %get-tuple-element.40.tops, f32[512,128]{1,0:T(8,128)S(1)} %get-tuple-element.41.totals, ...), custom_call_target="tpu_custom_call" | custom-call | tf_op jit(solution)/shard_map/rest_attention/pallas_call | solution.py:41
  28.9 1.6 %collective-permute-start.11 = (bf16[16,2176]{1,0:T(8,128)(2,1)S(1)}, bf16[16,2176]{1,0:T(8,128)(2,1)S(1)}, u32[]{:S(2)}, u32[]{:S(2)}) collective-permute-start(bf16[16,2176]{1,0:T(8,128)(2,1)S(1)} %get-tuple-element.45), channel_id=1, source_target_pairs={{0,8},{2,10},{4,12},{6,14},{8,0},{10,2},{12,4},{14,6},{16,24},{18,... | collective-permute-start | bytes 208904 | tf_op jit(solution)/shard_map/ppermute | solution.py:22
  30.5 2.7 %collective-permute-done.11.got = bf16[16,2176]{1,0:T(8,128)(2,1)S(1)} collective-permute-done((bf16[16,2176]{1,0:T(8,128)(2,1)S(1)}, bf16[16,2176]{1,0:T(8,128)(2,1)S(1)}, u32[]{:S(2)}, u32[]{:S(2)}) %collective-permute-start.11) | collective-permute-done | bytes 69664 | tf_op jit(solution)/shard_map/ppermute | solution.py:22
  33.5 2.7 %collective-permute-start.12 = (bf16[8,2176]{1,0:T(8,128)(2,1)S(1)}, bf16[8,2176]{1,0:T(8,128)(2,1)S(1)}, u32[]{:S(2)}, u32[]{:S(2)}) collective-permute-start(bf16[8,2176]{1,0:T(8,128)(2,1)S(1)} %get-tuple-element.48), channel_id=1, source_target_pairs={{0,16},{2,18},{4,20},{6,22},{8,24},{10,26},{12,28},{14,30},{16,0},... | collective-permute-start | bytes 104456 | tf_op jit(solution)/shard_map/ppermute | solution.py:22
  36.2 2.2 %collective-permute-done.12.got = bf16[8,2176]{1,0:T(8,128)(2,1)S(1)} collective-permute-done((bf16[8,2176]{1,0:T(8,128)(2,1)S(1)}, bf16[8,2176]{1,0:T(8,128)(2,1)S(1)}, u32[]{:S(2)}, u32[]{:S(2)}) %collective-permute-start.12) | collective-permute-done | bytes 34848 | tf_op jit(solution)/shard_map/ppermute | solution.py:22
  38.4 0.3 merge_last.1
  38.7 1.5 %collective-permute-start.13 = (f32[8,128]{1,0:T(8,128)S(1)}, f32[8,128]{1,0:T(8,128)S(1)}, u32[]{:S(2)}, u32[]{:S(2)}) collective-permute-start(f32[8,128]{1,0:T(8,128)S(1)} %get-tuple-element.50.squares), channel_id=1, source_target_pairs={{0,1},{1,0},{2,3},{3,2},{4,5},{5,4},{6,7},{7,6},{8,9},{9,8},{10,11... | collective-permute-start | bytes 12296 | tf_op jit(solution)/shard_map/ppermute | solution.py:22
  40.2 2.1 %collective-permute-done.13.other = f32[8,128]{1,0:T(8,128)S(1)} collective-permute-done((f32[8,128]{1,0:T(8,128)S(1)}, f32[8,128]{1,0:T(8,128)S(1)}, u32[]{:S(2)}, u32[]{:S(2)}) %collective-permute-start.13) | collective-permute-done | bytes 4128 | tf_op jit(solution)/shard_map/ppermute | solution.py:22
  42.3 0.7 %normalize.1 = (bf16[4,2048]{1,0:T(4,128)(2,1)}, bf16[2,2048]{1,0:T(2,128)(2,1)}, bf16[1,2048]{1,0:T(2,128)(2,1)}) custom-call(f32[8,2048]{1,0:T(8,128)S(1)} %get-tuple-element.49.att, f32[8,128]{1,0:T(8,128)S(1)} %get-tuple-element.50.squares, f32[8,128]{1,0:T(8,128)S(1)} %collective-permute-done.13.other, f32[1,2048]{1,0:T(1,128)S(1)} %bitcast.6), custom_call_target="tpu_custom_call" | custom-call | tf_op jit(solution)/shard_map/normalize/pallas_call | solution.py:41
  (30 shorter events, 1.0 us)
Async XLA Ops:
  0.6 6.0 %collective-permute-start.1 = (bf16[4,2048]{1,0:T(4,128)(2,1)}, bf16[4,2048]{1,0:T(4,128)(2,1)S(1)}, u32[]{:S(2)}, u32[]{:S(2)}) collective-permute-start(bf16[4,2048]{1,0:T(4,128)(2,1)} %own.1), channel_id=1, source_target_pairs={{0,4},{2,6},{4,0},{6,2},{8,12},{10,14},{12,8},{14,10},{16,20},{18,... | collective-permute-start | bytes 49160 | tf_op jit(solution)/shard_map/ppermute | solution.py:22
  3.7 3.0 %collective-permute-start = (bf16[4,2048]{1,0:T(4,128)(2,1)}, bf16[4,2048]{1,0:T(4,128)(2,1)S(1)}, u32[]{:S(2)}, u32[]{:S(2)}) collective-permute-start(bf16[4,2048]{1,0:T(4,128)(2,1)} %own.1), channel_id=1, source_target_pairs={{0,2},{2,0},{4,6},{6,4},{8,10},{10,8},{12,14},{14,12},{16,18},{18,... | collective-permute-start | bytes 49160 | tf_op jit(solution)/shard_map/ppermute | solution.py:22
  3.7 3.4 %collective-permute-start.2 = (bf16[4,2048]{1,0:T(4,128)(2,1)}, bf16[4,2048]{1,0:T(4,128)(2,1)S(1)}, u32[]{:S(2)}, u32[]{:S(2)}) collective-permute-start(bf16[4,2048]{1,0:T(4,128)(2,1)} %own.1), channel_id=1, source_target_pairs={{0,6},{2,4},{4,2},{6,0},{8,14},{10,12},{12,10},{14,8},{16,22},{18,... | collective-permute-start | bytes 49160 | tf_op jit(solution)/shard_map/ppermute | solution.py:22
  7.0 1.0 %copy-start = (bf16[272,512]{1,0:T(8,128)(2,1)S(1)}, bf16[272,512]{1,0:T(8,128)(2,1)}, u32[]{:S(2)}) copy-start(bf16[272,512]{1,0:T(8,128)(2,1)} %get-tuple-element.30.__4_) | copy-start | bytes 835588
  8.0 2.0 %copy-start.2 = (bf16[4,2048]{1,0:T(4,128)(2,1)S(1)}, bf16[4,2048]{1,0:T(4,128)(2,1)}, u32[]{:S(2)}) copy-start(bf16[4,2048]{1,0:T(4,128)(2,1)} %span_q.1) | copy-start | bytes 49156
  8.0 2.0 %copy-start.3 = (bf16[4,2048]{1,0:T(4,128)(2,1)S(1)}, bf16[4,2048]{1,0:T(4,128)(2,1)}, u32[]{:S(2)}) copy-start(bf16[4,2048]{1,0:T(4,128)(2,1)} %own.1) | copy-start | bytes 49156
  8.0 14.3 %collective-permute-start.5 = (bf16[272,512]{1,0:T(8,128)(2,1)}, bf16[272,512]{1,0:T(8,128)(2,1)S(1)}, u32[]{:S(2)}, u32[]{:S(2)}) collective-permute-start(bf16[272,512]{1,0:T(8,128)(2,1)} %get-tuple-element.34.k0), channel_id=1, source_target_pairs={{0,4},{2,6},{4,0},{6,2},{8,12},{10,14},{12,8},{14,10},{16,20},{18,... | collective-permute-start | bytes 835592 | tf_op jit(solution)/shard_map/ppermute | solution.py:22
  9.6 13.7 %collective-permute-start.6 = (bf16[272,512]{1,0:T(8,128)(2,1)S(1)}, bf16[272,512]{1,0:T(8,128)(2,1)S(1)}, u32[]{:S(2)}, u32[]{:S(2)}) collective-permute-start(bf16[272,512]{1,0:T(8,128)(2,1)S(1)} %get-tuple-element.35.v0), channel_id=1, source_target_pairs={{0,4},{2,6},{4,0},{6,2},{8,12},{10,14},{12,8},{14,10},{16,20},{18,... | collective-permute-start | bytes 835592 | tf_op jit(solution)/shard_map/ppermute | solution.py:22
  10.0 0.7 %copy-start.6 = (s32[32]{0:T(128)S(1)}, s32[32]{0:T(128)}, u32[]{:S(2)}) copy-start(s32[32]{0:T(128)} %param.33) | copy-start | bytes 388
  10.0 0.7 %copy-start.7 = (s32[16]{0:T(128)S(1)}, s32[16]{0:T(128)}, u32[]{:S(2)}) copy-start(s32[16]{0:T(128)} %param.34) | copy-start | bytes 196
  10.9 6.6 %collective-permute-start.3 = (bf16[16,2048]{1,0:T(8,128)(2,1)S(1)}, bf16[16,2048]{1,0:T(8,128)(2,1)S(1)}, u32[]{:S(2)}, u32[]{:S(2)}) collective-permute-start(bf16[16,2048]{1,0:T(8,128)(2,1)S(1)} %column_queries.1.mine), channel_id=1, source_target_pairs={{0,16},{2,18},{4,20},{6,22},{8,24},{10,26},{12,28},{14,30},{16,0},... | collective-permute-start | bytes 196616 | tf_op jit(solution)/shard_map/ppermute | solution.py:22
  17.6 4.7 %collective-permute-start.4 = (bf16[20,2048]{1,0:T(8,128)(2,1)S(1)}, bf16[20,2048]{1,0:T(8,128)(2,1)S(1)}, u32[]{:S(2)}, u32[]{:S(2)}) collective-permute-start(bf16[20,2048]{1,0:T(8,128)(2,1)S(1)} %more_queries.1.mine), channel_id=1, source_target_pairs={{0,8},{2,10},{4,12},{6,14},{8,0},{10,2},{12,4},{14,6},{16,24},{18,... | collective-permute-start | bytes 245768 | tf_op jit(solution)/shard_map/ppermute | solution.py:22
  18.0 5.8 %collective-permute-start.7 = (bf16[272,512]{1,0:T(8,128)(2,1)}, bf16[272,512]{1,0:T(8,128)(2,1)S(1)}, u32[]{:S(2)}, u32[]{:S(2)}) collective-permute-start(bf16[272,512]{1,0:T(8,128)(2,1)} %get-tuple-element.34.k0), channel_id=1, source_target_pairs={{0,2},{2,0},{4,6},{6,4},{8,10},{10,8},{12,14},{14,12},{16,18},{18,... | collective-permute-start | bytes 835592 | tf_op jit(solution)/shard_map/ppermute | solution.py:22
  18.0 5.8 %collective-permute-start.8 = (bf16[272,512]{1,0:T(8,128)(2,1)S(1)}, bf16[272,512]{1,0:T(8,128)(2,1)S(1)}, u32[]{:S(2)}, u32[]{:S(2)}) collective-permute-start(bf16[272,512]{1,0:T(8,128)(2,1)S(1)} %get-tuple-element.35.v0), channel_id=1, source_target_pairs={{0,2},{2,0},{4,6},{6,4},{8,10},{10,8},{12,14},{14,12},{16,18},{18,... | collective-permute-start | bytes 835592 | tf_op jit(solution)/shard_map/ppermute | solution.py:22
  23.3 0.7 %copy-start.1 = (f32[32,64]{1,0:T(8,128)S(1)}, f32[32,64]{1,0:T(8,128)}, u32[]{:S(2)}) copy-start(f32[32,64]{1,0:T(8,128)} %get-tuple-element.28.allowed) | copy-start | bytes 24580
  23.3 0.7 %copy-start.5 = (bf16[32,40]{1,0:T(8,128)(2,1)S(1)}, bf16[32,40]{1,0:T(8,128)(2,1)}, u32[]{:S(2)}) copy-start(bf16[32,40]{1,0:T(8,128)(2,1)} %get-tuple-element.27.perm) | copy-start | bytes 7684
  23.3 3.4 %collective-permute-start.9 = (bf16[272,512]{1,0:T(8,128)(2,1)S(1)}, bf16[272,512]{1,0:T(8,128)(2,1)S(1)}, u32[]{:S(2)}, u32[]{:S(2)}) collective-permute-start(bf16[272,512]{1,0:T(8,128)(2,1)S(1)} %get-tuple-element.37.k2), channel_id=1, source_target_pairs={{0,2},{2,0},{4,6},{6,4},{8,10},{10,8},{12,14},{14,12},{16,18},{18,... | collective-permute-start | bytes 835592 | tf_op jit(solution)/shard_map/ppermute | solution.py:22
  23.3 3.4 %collective-permute-start.10 = (bf16[272,512]{1,0:T(8,128)(2,1)S(1)}, bf16[272,512]{1,0:T(8,128)(2,1)S(1)}, u32[]{:S(2)}, u32[]{:S(2)}) collective-permute-start(bf16[272,512]{1,0:T(8,128)(2,1)S(1)} %get-tuple-element.38.v2), channel_id=1, source_target_pairs={{0,2},{2,0},{4,6},{6,4},{8,10},{10,8},{12,14},{14,12},{16,18},{18,... | collective-permute-start | bytes 835592 | tf_op jit(solution)/shard_map/ppermute | solution.py:22
  28.9 4.4 %collective-permute-start.11 = (bf16[16,2176]{1,0:T(8,128)(2,1)S(1)}, bf16[16,2176]{1,0:T(8,128)(2,1)S(1)}, u32[]{:S(2)}, u32[]{:S(2)}) collective-permute-start(bf16[16,2176]{1,0:T(8,128)(2,1)S(1)} %get-tuple-element.45), channel_id=1, source_target_pairs={{0,8},{2,10},{4,12},{6,14},{8,0},{10,2},{12,4},{14,6},{16,24},{18,... | collective-permute-start | bytes 208904 | tf_op jit(solution)/shard_map/ppermute | solution.py:22
  33.5 4.9 %collective-permute-start.12 = (bf16[8,2176]{1,0:T(8,128)(2,1)S(1)}, bf16[8,2176]{1,0:T(8,128)(2,1)S(1)}, u32[]{:S(2)}, u32[]{:S(2)}) collective-permute-start(bf16[8,2176]{1,0:T(8,128)(2,1)S(1)} %get-tuple-element.48), channel_id=1, source_target_pairs={{0,16},{2,18},{4,20},{6,22},{8,24},{10,26},{12,28},{14,30},{16,0},... | collective-permute-start | bytes 104456 | tf_op jit(solution)/shard_map/ppermute | solution.py:22
  38.4 3.9 %copy-start.4 = (f32[2048]{0:T(1024)S(1)}, f32[2048]{0:T(1024)}, u32[]{:S(2)}) copy-start(f32[2048]{0:T(1024)} %param.35) | copy-start | bytes 24580
  38.7 3.6 %collective-permute-start.13 = (f32[8,128]{1,0:T(8,128)S(1)}, f32[8,128]{1,0:T(8,128)S(1)}, u32[]{:S(2)}, u32[]{:S(2)}) collective-permute-start(f32[8,128]{1,0:T(8,128)S(1)} %get-tuple-element.50.squares), channel_id=1, source_target_pairs={{0,1},{1,0},{2,3},{3,2},{4,5},{5,4},{6,7},{7,6},{8,9},{9,8},{10,11... | collective-permute-start | bytes 12296 | tf_op jit(solution)/shard_map/ppermute | solution.py:22

commit v3 on v2

--- a/solution.py
+++ b/solution.py
@@ -14,7 +14,7 @@
 F32 = jnp.float32
 BF16 = jnp.bfloat16
 VMEM = pltpu.VMEM
-PLAN_LIMIT = 60 * 2**20
+PLAN_LIMIT = 59 * 2**20
 
 
 def exchange(value, axis, mask):
@@ -64,31 +64,39 @@
     return jnp.where(lanes == index, row.astype(F32), 0.0).sum(axis=1, keepdims=True)
 
 
-def plan_kernel(
-    sizes, place,
-    ids_h, idx1_h, idx2_h, span_frames_h, table_h, span_k_h, span_v_h,
-    fk_h, fv_h, rk_h, rv_h, mk_h, mv_h, cache_k_h, cache_v_h,
-    k0, v0, perm, allowed, *scratch,
-):
-    spans, frames, n1, n2, blocks, block_rows, mask_bits = sizes
-    given = (ids_h, idx1_h, idx2_h, span_frames_h, table_h, span_k_h, span_v_h,
-             fk_h, fv_h, rk_h, rv_h, mk_h, mv_h, cache_k_h, cache_v_h)
-    held, (whole_k, whole_v, sems) = scratch[:-3], scratch[-3:]
-    cached = cache_k_h.shape[0]
-    extras = whole_k.shape[0] - cached
-    staged = (whole_k.at[0:cached], whole_v.at[0:cached])
+def parity(index, count):
+    total = jnp.zeros_like(index)
+    for i in range(count):
+        total = total ^ (index >> i)
+    return total & 1
+
+
+def fetch(given, held, sems):
     copies = [
         pltpu.make_async_copy(source, target, sems.at[i])
-        for i, (source, target) in enumerate(zip(given, (*held, *staged)))
+        for i, (source, target) in enumerate(zip(given, held))
     ]
     for copy in copies:
         copy.start()
-    for copy in copies[:-2]:
+    return copies
+
+
+def keys_kernel(
+    sizes, place,
+    ids_h, idx1_h, idx2_h, table_h, span_k_h, span_v_h,
+    fk_h, fv_h, rk_h, rv_h, mk_h, mv_h, cache_v_h,
+    values, extra, *scratch,
+):
+    spans, frames = sizes
+    given = (ids_h, idx1_h, idx2_h, table_h, span_k_h, span_v_h,
+             fk_h, fv_h, rk_h, rv_h, mk_h, mv_h, cache_v_h)
+    held, sems = scratch[:-1], scratch[-1]
+    cached = cache_v_h.shape[0]
+    copies = fetch(given, (*held, values.at[0:cached]), sems)
+    for copy in copies[:-1]:
         copy.wait()
-    ids, idx1, idx2, span_frames, table, span_k, span_v, fk, fv, rk, rv, mk, mv = held
+    ids, idx1, idx2, table, span_k, span_v, fk, fv, rk, rv, mk, mv = held
     me = place[0]
-    own_block = me >> 2
-    picked = n1 + n2
 
     hits = at_lane(ids[...], iota((spans, 1), 0))
     hits = (iota((spans, table.shape[0]), 1).astype(F32) == hits).astype(BF16)
@@ -111,22 +119,25 @@
             jnp.where(second, token, jnp.where(first, revealed[...].astype(F32), frame))
         )
     sets += shown
-    for i, (whole, target) in enumerate(((whole_k, k0), (whole_v, v0))):
-        rest = jnp.zeros((extras - 3 * spans, whole.shape[1]), F32)
-        whole[cached:, :] = jnp.concatenate(sets[i::2] + [rest], axis=0).astype(BF16)
-        copies[i - 2].wait()
-    out_copies = [
-        pltpu.make_async_copy(whole, target, sems.at[len(given) + i])
-        for i, (whole, target) in enumerate(((whole_k, k0), (whole_v, v0)))
-    ]
-    for copy in out_copies:
-        copy.start()
+    half = extra.shape[0] // 2
+    rest = jnp.zeros((half - 3 * spans, extra.shape[1]), F32)
+    parts = jnp.concatenate([*sets[0::2], rest, *sets[1::2], rest], axis=0).astype(BF16)
+    extra[...] = parts
+    values[cached:, :] = parts
+    copies[-1].wait()
+
+
+def plan_kernel(sizes, place, span_frames, perm, allowed):
+    spans, n1, n2, blocks, block_rows, mask_bits, extras = sizes
+    me = place[0]
+    own_block = me >> 2
+    picked = n1 + n2
 
     rows, both = perm.shape
     depth = both // 2
     row = iota((rows, 1), 0)
     block, at = split_index(row, block_rows)
-    mask = jnp.zeros_like(block)
+    mask = parity(block, mask_bits)
     for i in range(mask_bits):
         mask = mask + (((block >> i) & 1) << (mask_bits + 1 - i))
     half = blocks // 2
@@ -155,8 +166,6 @@
     sees = sees | (in_first & is_pick & (at < spans + n1))
     sees = sees | (in_second & is_pick & (at >= spans + n1))
     allowed[...] = jnp.where(sees, 1.0, 0.0)
-    for copy in out_copies:
-        copy.wait()
 
 
 def stacked(parts):
@@ -164,14 +173,14 @@
 
 
 def select_kernel(sizes, place, idx1, idx2, span_q, own, q1, q2, q3, out):
-    spans, frames, n1, n2 = sizes
+    spans, frames, n1, n2, mask_bits = sizes
     me = place[0]
-    column = me & 3
+    column = (me & 3) ^ parity(me >> 2, mask_bits)
     picked = n1 + n2
     shape = (out.shape[0], spans + 4 * frames)
     row = iota((shape[0], 1), 0)
     block, at = split_index(jnp.maximum(row - spans, 0), picked)
-    owner = block * 4 + column
+    owner = block * 4 + (column ^ parity(block, mask_bits))
     wanted = jnp.where(
         at < n1,
         at_lane(idx1[...], owner * n1 + at),
@@ -189,6 +198,10 @@
 
 def tie_kernel(*_):
     pass
+
+
+def stage_kernel(*refs):
+    refs[-1][...] = refs[len(refs) // 2 - 1][...]
 
 
 def tie(*arrays):
@@ -203,7 +216,7 @@
     )
 
 
-def grow_kernel(spans, mine, other, out):
+def grow_kernel(spans, mine, other, _, out, __):
     a = mine[...].astype(F32)
     b = other[...].astype(F32)
     out[...] = jnp.concatenate(
@@ -227,92 +240,75 @@
     return packed + pltpu.roll(packed, 112, 1) + pltpu.roll(packed, 96, 1)
 
 
-def softmax_parts(heads, rows, queries, permit, key_refs, value_refs, extras, visit, before=None):
+def attention_kernel(
+    heads, rows, extras, keep,
+    perm, allowed, mine, other, k0, k1, k2, k3, v0, v1, v2, v3, extra,
+    send, kept, kept_stats,
+):
+    queries = jnp.dot(
+        perm[...], stacked([mine[...], other[...]]), preferred_element_type=F32
+    ).astype(BF16)
+    wide = heads * GROUP * HD
     scaling = HD ** (-0.5)
-    cached = key_refs[0].shape[0] - extras
+    cached = k0.shape[0]
     stack = GROUP if rows * GROUP <= 128 else 1
-    permit = jnp.concatenate([permit] * stack, axis=0) > 0.0
+    permit = jnp.concatenate([allowed[...]] * stack, axis=0) > 0.0
     nt = (((1,), (1,)), ((), ()))
-    for g in range(heads):
+    lane = iota((rows, HD), 1)
+    stats = jnp.zeros((rows, HD), F32)
+
+    def blocks_of(refs, g, first):
         columns = slice(g * HD, (g + 1) * HD)
-        keys = [ref[0:cached, columns] for ref in key_refs]
-        keys.append(jnp.concatenate([ref[cached:, columns] for ref in key_refs], axis=0))
-        values = [ref[0:cached, columns] for ref in value_refs]
-        values.append(jnp.concatenate([ref[cached:, columns] for ref in value_refs], axis=0))
-        for head in range(g * GROUP, (g + 1) * GROUP, stack):
-            q = jnp.concatenate(
-                [queries[:, (head + i) * HD : (head + i + 1) * HD] for i in range(stack)], axis=0
-            )
-            scores = [
-                lax.dot_general(q, key, nt, preferred_element_type=F32) * scaling for key in keys
-            ]
-            scores[-1] = jnp.where(permit, scores[-1], NEG)
-            top = functools.reduce(jnp.maximum, scores[:-1]).max(axis=1, keepdims=True)
-            top = jnp.maximum(top, scores[-1].max(axis=1, keepdims=True))
-            if before is not None:
-                earlier = [ref[head * rows : (head + stack) * rows, :] for ref in before]
-                top = jnp.maximum(top, earlier[0][:, 0:1])
-            weights = [jnp.exp(s - top) for s in scores]
-            total = functools.reduce(jnp.add, weights[:-1]).sum(axis=1, keepdims=True)
-            total = total + weights[-1].sum(axis=1, keepdims=True)
+        parts = [ref[0:cached, columns] for ref in refs]
+        rest = [extra[first : first + extras, columns]]
+        at = cached + first
+        rest += [ref[at : at + extras, columns] for ref in (v1, v2, v3)]
+        parts.append(jnp.concatenate(rest, axis=0))
+        return parts
+
+    def scores_of(head):
+        q = jnp.concatenate(
+            [queries[:, (head + i) * HD : (head + i + 1) * HD] for i in range(stack)], axis=0
+        )
+        scores = [
+            lax.dot_general(q, key, nt, preferred_element_type=F32) * scaling
+            for key in blocks_of((k0, k1, k2, k3), head // GROUP, 0)
+        ]
+        scores[-1] = jnp.where(permit, scores[-1], NEG)
+        return scores
+
+    def weights_of(scores):
+        top = functools.reduce(jnp.maximum, scores[:-1]).max(axis=1, keepdims=True)
+        top = jnp.maximum(top, scores[-1].max(axis=1, keepdims=True))
+        weights = [jnp.exp(s - top) for s in scores]
+        total = functools.reduce(jnp.add, weights[:-1]).sum(axis=1, keepdims=True)
+        return top, total + weights[-1].sum(axis=1, keepdims=True), weights
+
+    steps = range(0, heads * GROUP, stack)
+    for first in range(0, len(steps), 2):
+        group = steps[first : first + 2]
+        scored = [scores_of(head) for head in group]
+        weighed = [weights_of(scores) for scores in scored]
+        for head, (top, total, weights) in zip(group, weighed):
             out = functools.reduce(
                 jnp.add,
                 [
                     jnp.dot(w.astype(BF16), value, preferred_element_type=F32)
-                    for w, value in zip(weights, values)
+                    for w, value in zip(
+                        weights, blocks_of((v0, v1, v2, v3), head // GROUP, extras)
+                    )
                 ],
             )
-            top = jnp.broadcast_to(top, out.shape)
-            if before is not None:
-                scale = jnp.exp(earlier[0] - top)
-                total = earlier[1] * scale + total
-                out = earlier[2] * scale + out
-            visit(head, stack, top, jnp.broadcast_to(total, out.shape), out)
-
-
-def first_attention_kernel(
-    heads, rows, extras, perm, allowed, mine, other, k0, k1, k2, v0, v1, v2,
-    queries, tops, totals, sums,
-):
-    queries[...] = jnp.dot(
-        perm[...], stacked([mine[...], other[...]]), preferred_element_type=F32
-    ).astype(BF16)
-
-    def visit(head, stack, top, total, out):
-        place = slice(head * rows, (head + stack) * rows)
-        tops[place, :] = top
-        totals[place, :] = total
-        sums[place, :] = out
-
-    softmax_parts(
-        heads, rows, queries, allowed[:, 0 : 3 * extras], (k0, k1, k2), (v0, v1, v2), extras, visit
-    )
-
-
-def second_attention_kernel(
-    heads, rows, extras, keep, queries, allowed, tops, totals, sums, k3, v3,
-    send, kept, kept_stats,
-):
-    wide = heads * GROUP * HD
-    lane = iota((rows, HD), 1)
-    held = [jnp.zeros((rows, HD), F32)]
-
-    def visit(head, stack, top, total, out):
-        out = out / total
-        level = top + jnp.log(total)
-        for i in range(stack):
-            first = i * rows
-            columns = slice((head + i) * HD, (head + i + 1) * HD)
-            kept[:, columns] = out[first : first + keep]
-            send[:, columns] = out[first + keep : first + rows].astype(BF16)
-            held[0] = jnp.where(lane == head + i, level[first : first + rows], held[0])
-
-    softmax_parts(
-        heads, rows, queries, allowed[:, 3 * extras : 4 * extras], (k3,), (v3,), extras, visit,
-        (tops, totals, sums),
-    )
-    kept_stats[...] = held[0][:keep]
-    send[:, wide:] = split_stats(held[0][keep:])
+            out = out / total
+            level = top + jnp.log(total)
+            for i in range(stack):
+                at = i * rows
+                columns = slice((head + i) * HD, (head + i + 1) * HD)
+                kept[:, columns] = out[at : at + keep]
+                send[:, columns] = out[at + keep : at + rows].astype(BF16)
+                stats = jnp.where(lane == head + i, level[at : at + rows], stats)
+    kept_stats[...] = stats[:keep]
+    send[:, wide:] = split_stats(stats[keep:])
 
 
 def merge(heads, kept, kept_stats, got):
@@ -398,90 +394,97 @@
     block_rows = -(-(spans + picked) // 8) * 8
     rows = blocks * block_rows
 
-    bits = [1 << b for b in range(2, owners.bit_length() - 1)][::-1]
+    bits = [(1 << b) + 1 for b in range(2, owners.bit_length() - 1)][::-1]
 
     depth = (blocks // 2) * spans + blocks * picked
     extras = -(-3 * spans // 16) * 16
 
-    q2 = exchange(frame_q, "ctx", 2)
     q3 = exchange(frame_q, "ctx", 3)
     q1 = exchange(frame_q, "ctx", 1)
     small = (
-        action_ids[None, :], pass1_idx[None, :], pass2_idx[None, :], span_frames[None, :],
+        action_ids[None, :], pass1_idx[None, :], pass2_idx[None, :],
         action_table, span_k, span_v, frame_k, frame_v, revealed_k, revealed_v,
         mask_k, mask_v,
     )
-    sizes = (spans, frames, n1, n2, blocks, block_rows, len(bits))
-    keys = cache_k.shape[0] + extras
     place = me.reshape(1)
-    k0, v0, perm, allowed = call(
-        functools.partial(plan_kernel, sizes),
-        "plane_keys",
+    values, extra = call(
+        functools.partial(keys_kernel, (spans, frames)),
+        "plane_values",
         [
-            jax.ShapeDtypeStruct((keys, width), BF16),
-            jax.ShapeDtypeStruct((keys, width), BF16),
-            jax.ShapeDtypeStruct((rows, 2 * depth), BF16),
-            jax.ShapeDtypeStruct((rows, 4 * extras), F32),
+            jax.ShapeDtypeStruct((cache_v.shape[0] + 2 * extras, width), BF16),
+            jax.ShapeDtypeStruct((2 * extras, width), BF16),
         ],
-        place, *small, cache_k, cache_v,
-        places={0: pltpu.SMEM, **{i + 1: pl.ANY for i in range(len(small) + 2)}},
-        out_any=(0, 1),
+        place, *small, cache_v,
+        places={0: pltpu.SMEM, **{i + 1: pl.ANY for i in range(len(small) + 1)}},
         scratch=[pltpu.VMEM(array.shape, array.dtype) for array in small]
-        + [pltpu.VMEM((keys, width), BF16)] * 2
-        + [pltpu.SemaphoreType.DMA((len(small) + 4,))],
+        + [pltpu.SemaphoreType.DMA((len(small) + 1,))],
         limit=PLAN_LIMIT,
     )
-    q1, q2, q3, k0, v0 = tie(q1, q2, q3, k0, v0)
-    k2 = exchange(k0, "ctx", 2)
-    v2 = exchange(v0, "ctx", 2)
+    moved = (q1, q3, values)
+    q1, q3, values, k0 = call(
+        stage_kernel,
+        "plane_queries_arrived",
+        [jax.ShapeDtypeStruct(array.shape, array.dtype) for array in (*moved, cache_k)],
+        *moved, cache_k,
+        places={i: pl.ANY for i in range(len(moved))},
+        aliases={i: i for i in range(len(moved))},
+    )
+    q2 = exchange(q3, "ctx", 1)
+    k3 = exchange(k0, "ctx", 3)
+    v3 = exchange(values, "ctx", 3)
     k1 = exchange(k0, "ctx", 1)
-    v1 = exchange(v0, "ctx", 1)
+    v1 = exchange(values, "ctx", 1)
 
     state = call(
-        functools.partial(select_kernel, (spans, frames, n1, n2)),
+        functools.partial(select_kernel, (spans, frames, n1, n2, len(bits))),
         "column_queries",
         jax.ShapeDtypeStruct((spans + blocks * picked, q_width), BF16),
         place, pass1_idx[None, :], pass2_idx[None, :], span_q, frame_q, q1, q2, q3,
         places={0: pltpu.SMEM},
     )
+
     held = spans
     for bit in bits[:-1]:
         other = exchange(state, "ctx", bit)
-        state = call(
+        state, k3 = call(
             functools.partial(grow_kernel, held),
             "more_queries",
-            jax.ShapeDtypeStruct((state.shape[0] + held, q_width), BF16),
-            state, other,
+            [
+                jax.ShapeDtypeStruct((state.shape[0] + held, q_width), BF16),
+                jax.ShapeDtypeStruct(k3.shape, BF16),
+            ],
+            state, other, k3,
+            places={2: pl.ANY},
+            aliases={2: 1},
         )
         held = 2 * held
     other = exchange(state, "ctx", bits[-1])
-    other, k2, v2 = tie(other, k2, v2)
-    k3 = exchange(k2, "ctx", 1)
-    v3 = exchange(v2, "ctx", 1)
-
+    k2 = exchange(k3, "ctx", 1)
+    other, v3 = tie(other, v3)
+    v2 = exchange(v3, "ctx", 1)
+
+    perm, allowed = call(
+        functools.partial(plan_kernel, (spans, n1, n2, blocks, block_rows, len(bits), extras)),
+        "row_plan",
+        [
+            jax.ShapeDtypeStruct((rows, 2 * depth), BF16),
+            jax.ShapeDtypeStruct((rows, 4 * extras), F32),
+        ],
+        place, span_frames[None, :],
+        places={0: pltpu.SMEM},
+    )
     keep = rows // 2
     packed = q_width + HD
-    limit = (16 if blocks <= 4 else 40) * 2**20
-    queries, *before = call(
-        functools.partial(first_attention_kernel, heads, rows, extras),
+    send, kept, stats = call(
+        functools.partial(attention_kernel, heads, rows, extras, keep),
         "plane_attention",
-        [
-            jax.ShapeDtypeStruct((rows, q_width), BF16),
-            *[jax.ShapeDtypeStruct((rows * q_width // HD, HD), F32)] * 3,
-        ],
-        perm, allowed, state, other, k0, k1, k2, v0, v1, v2,
-        limit=limit,
-    )
-    send, kept, stats = call(
-        functools.partial(second_attention_kernel, heads, rows, extras, keep),
-        "rest_attention",
         [
             jax.ShapeDtypeStruct((keep, packed), BF16),
             jax.ShapeDtypeStruct((keep, q_width), F32),
             jax.ShapeDtypeStruct((keep, HD), F32),
         ],
-        queries, allowed, *before, k3, v3,
-        limit=limit,
+        perm, allowed, state, other, k0, k1, k2, k3, cache_v, v1, v2, v3, extra,
+        limit=(16 if blocks <= 4 else 40) * 2**20,
     )
     for bit in bits[:0:-1]:
         got = exchange(send, "ctx", bit)

time: 43.4 us -> 38 us (0.88)
  Pallas kernels: 9.15 us -> 4.99 us
  local copies, waits for them, and re-layouts: 1.83 us -> 0.58 us
  starting transfers between devices: 15.2 us -> 15.8 us
    pallas_call x10, Pallas kernels: 9.15 us -> 4.99 us  [call(): pl.pallas_call(kernel, out_shape=out_shape, in_specs=in_specs, out_specs=...]
    unnamed x16 -> x18, local copies, waits for them, and re-layouts: 1.83 us -> 0.58 us
    ppermute x14, starting transfers between devices: 15.2 us -> 15.8 us  [exchange(): return lax.ppermute(value, axis, pairs)]
  transfers between devices with their start and end apart: 14 -> 14, of which waited for: 7 -> 9; matrix products, arithmetic and copies ran while one was open for 0% -> 0% of each run, Pallas kernels for 13% -> 6%
where the time goes in v3:
time: 38 us; the launch traced here: 37.8 us
  starting transfers between devices  15.8 us (42%)
  waiting for transfers between devices  15.7 us (41%)
  Pallas kernels  4.99 us (13%)
  between operations  0.76 us (2%)
  local copies, waits for them, and re-layouts  0.58 us (2%)
    ppermute x14, starting transfers between devices, exchange(): return lax.ppermute(value, axis, pairs)  15.8 us
    ppermute x14, waiting for transfers between devices, exchange(): return lax.ppermute(value, axis, pairs)  15.7 us
    pallas_call x10, Pallas kernels, call(): pl.pallas_call(kernel, out_shape=out_shape, in_specs=in_specs, out_specs=...  4.99 us
  transfers between devices with their start and end apart: 14, of which 9 were waited for; matrix products, arithmetic and copies ran while one was open for 0% of the time, Pallas kernels for 6%

profile of v3, /device:TPU:0, one launch (start us, length us, event | category | flops | bytes accessed | tf_op | source)
XLA Modules:
  0.0 37.8 jit_solution(17772618447209359818)
XLA Ops:
  0.6 0.5 %collective-permute-start = (bf16[4,2048]{1,0:T(4,128)(2,1)}, bf16[4,2048]{1,0:T(4,128)(2,1)S(1)}, u32[]{:S(2)}, u32[]{:S(2)}) collective-permute-start(bf16[4,2048]{1,0:T(4,128)(2,1)} %own.1), channel_id=1, source_target_pairs={{0,2},{2,0},{4,6},{6,4},{8,10},{10,8},{12,14},{14,12},{16,18},{18,... | collective-permute-start | bytes 49160 | tf_op jit(solution)/shard_map/ppermute | solution.py:22
  1.2 2.6 %collective-permute-start.1 = (bf16[4,2048]{1,0:T(4,128)(2,1)}, bf16[4,2048]{1,0:T(4,128)(2,1)S(1)}, u32[]{:S(2)}, u32[]{:S(2)}) collective-permute-start(bf16[4,2048]{1,0:T(4,128)(2,1)} %own.1), channel_id=1, source_target_pairs={{0,6},{2,4},{4,2},{6,0},{8,14},{10,12},{12,10},{14,8},{16,22},{18,... | collective-permute-start | bytes 49160 | tf_op jit(solution)/shard_map/ppermute | solution.py:22
  3.8 1.9 %plane_values.1 = (bf16[288,512]{1,0:T(8,128)(2,1)}, bf16[32,512]{1,0:T(8,128)(2,1)}) custom-call(s32[1]{0:T(128)} %bitcast.place, s32[1,4]{1,0:T(1,128)} %bitcast.12, s32[1,32]{1,0:T(1,128)} %bitcast.7, s32[1,16]{1,0:T(1,128)} %bitcast.9, bf16[18,512]{1,0:T(8,128)(2,1)} %table_h.1, bf16[4,512]{1,0:T(4,128)(2,1)} %span_k_h.1, bf16[4,512]{1,0:T(4,128)(2,1)} %span_v_h.1, ...), custom_call_target="tpu_custom_call" | custom-call | tf_op jit(solution)/shard_map/plane_values/pallas_call | solution.py:41
  5.8 1.4 %collective-permute-start.4 = (bf16[256,512]{1,0:T(8,128)(2,1)S(1)}, bf16[256,512]{1,0:T(8,128)(2,1)S(1)}, u32[]{:S(2)}, u32[]{:S(2)}) collective-permute-start(bf16[256,512]{1,0:T(8,128)(2,1)S(1)} %get-tuple-element.28.k0), channel_id=1, source_target_pairs={{0,6},{2,4},{4,2},{6,0},{8,14},{10,12},{12,10},{14,8},{16,22},{18,... | collective-permute-start | bytes 786440 | tf_op jit(solution)/shard_map/ppermute | solution.py:22
  7.3 0.4 collective-permute-start.6
  7.7 1.1 %collective-permute-done.2.q2 = bf16[4,2048]{1,0:T(4,128)(2,1)S(1)} collective-permute-done((bf16[4,2048]{1,0:T(4,128)(2,1)S(1)}, bf16[4,2048]{1,0:T(4,128)(2,1)S(1)}, u32[]{:S(2)}, u32[]{:S(2)}) %collective-permute-start.2) | collective-permute-done | bytes 16416 | tf_op jit(solution)/shard_map/ppermute | solution.py:22
  9.1 2.5 %collective-permute-start.3 = (bf16[16,2048]{1,0:T(8,128)(2,1)S(1)}, bf16[16,2048]{1,0:T(8,128)(2,1)S(1)}, u32[]{:S(2)}, u32[]{:S(2)}) collective-permute-start(bf16[16,2048]{1,0:T(8,128)(2,1)S(1)} %column_queries.1.mine), channel_id=1, source_target_pairs={{0,18},{2,16},{4,22},{6,20},{8,26},{10,24},{12,30},{14,28},{16,2},... | collective-permute-start | bytes 196616 | tf_op jit(solution)/shard_map/ppermute | solution.py:22
  11.6 2.5 %collective-permute-done.3.other = bf16[16,2048]{1,0:T(8,128)(2,1)S(1)} collective-permute-done((bf16[16,2048]{1,0:T(8,128)(2,1)S(1)}, bf16[16,2048]{1,0:T(8,128)(2,1)S(1)}, u32[]{:S(2)}, u32[]{:S(2)}) %collective-permute-start.3) | collective-permute-done | bytes 65568 | tf_op jit(solution)/shard_map/ppermute | solution.py:22
  14.3 2.0 %collective-permute-start.5 = (bf16[20,2048]{1,0:T(8,128)(2,1)S(1)}, bf16[20,2048]{1,0:T(8,128)(2,1)S(1)}, u32[]{:S(2)}, u32[]{:S(2)}) collective-permute-start(bf16[20,2048]{1,0:T(8,128)(2,1)S(1)} %get-tuple-element.29.mine), channel_id=1, source_target_pairs={{0,10},{2,8},{4,14},{6,12},{8,2},{10,0},{12,6},{14,4},{16,26},{18,... | collective-permute-start | bytes 245768 | tf_op jit(solution)/shard_map/ppermute | solution.py:22
  16.3 0.5 %collective-permute-start.9 = (bf16[288,512]{1,0:T(8,128)(2,1)}, bf16[288,512]{1,0:T(8,128)(2,1)S(1)}, u32[]{:S(2)}, u32[]{:S(2)}) collective-permute-start(bf16[288,512]{1,0:T(8,128)(2,1)} %get-tuple-element.30), channel_id=1, source_target_pairs={{0,2},{2,0},{4,6},{6,4},{8,10},{10,8},{12,14},{14,12},{16,18},{18,... | collective-permute-start | bytes 884744 | tf_op jit(solution)/shard_map/ppermute | solution.py:22
  16.8 3.8 %collective-permute-done.6.__1_ = bf16[288,512]{1,0:T(8,128)(2,1)S(1)} collective-permute-done((bf16[288,512]{1,0:T(8,128)(2,1)}, bf16[288,512]{1,0:T(8,128)(2,1)S(1)}, u32[]{:S(2)}, u32[]{:S(2)}) %collective-permute-start.6) | collective-permute-done | bytes 294944 | tf_op jit(solution)/shard_map/ppermute | solution.py:22
  20.7 0.4 %collective-permute-start.7 = (bf16[256,512]{1,0:T(8,128)(2,1)S(1)}, bf16[256,512]{1,0:T(8,128)(2,1)S(1)}, u32[]{:S(2)}, u32[]{:S(2)}) collective-permute-start(bf16[256,512]{1,0:T(8,128)(2,1)S(1)} %get-tuple-element.28.k0), channel_id=1, source_target_pairs={{0,2},{2,0},{4,6},{6,4},{8,10},{10,8},{12,14},{14,12},{16,18},{18,... | collective-permute-start | bytes 786440 | tf_op jit(solution)/shard_map/ppermute | solution.py:22
  21.2 0.5 %copy-done.8 = s32[64]{0:T(128)S(1)} copy-done((s32[64]{0:T(128)S(1)}, s32[64]{0:T(128)}, u32[]{:S(2)}) %copy-start.8) | copy-done | bytes 280
  21.9 0.6 %collective-permute-done.7.k1 = bf16[256,512]{1,0:T(8,128)(2,1)S(1)} collective-permute-done((bf16[256,512]{1,0:T(8,128)(2,1)S(1)}, bf16[256,512]{1,0:T(8,128)(2,1)S(1)}, u32[]{:S(2)}, u32[]{:S(2)}) %collective-permute-start.7) | collective-permute-done | bytes 262176 | tf_op jit(solution)/shard_map/ppermute | solution.py:22
  22.5 0.4 collective-permute-done.8.k2
  22.9 1.4 %plane_attention.1 = (bf16[16,2176]{1,0:T(8,128)(2,1)S(1)}, f32[16,2048]{1,0:T(8,128)S(1)}, f32[16,128]{1,0:T(8,128)S(1)}) custom-call(bf16[32,40]{1,0:T(8,128)(2,1)S(1)} %get-tuple-element.23.perm, f32[32,64]{1,0:T(8,128)S(1)} %get-tuple-element.24.allowed, bf16[20,2048]{1,0:T(8,128)(2,1)S(1)} %get-tuple-element.29.mine, ...), custom_call_target="tpu_custom_call" | custom-call | tf_op jit(solution)/shard_map/plane_attention/pallas_call | solution.py:41
  24.3 1.3 %collective-permute-start.11 = (bf16[16,2176]{1,0:T(8,128)(2,1)S(1)}, bf16[16,2176]{1,0:T(8,128)(2,1)S(1)}, u32[]{:S(2)}, u32[]{:S(2)}) collective-permute-start(bf16[16,2176]{1,0:T(8,128)(2,1)S(1)} %get-tuple-element.37), channel_id=1, source_target_pairs={{0,10},{2,8},{4,14},{6,12},{8,2},{10,0},{12,6},{14,4},{16,26},{18,... | collective-permute-start | bytes 208904 | tf_op jit(solution)/shard_map/ppermute | solution.py:22
  25.6 2.9 %collective-permute-done.11.got = bf16[16,2176]{1,0:T(8,128)(2,1)S(1)} collective-permute-done((bf16[16,2176]{1,0:T(8,128)(2,1)S(1)}, bf16[16,2176]{1,0:T(8,128)(2,1)S(1)}, u32[]{:S(2)}, u32[]{:S(2)}) %collective-permute-start.11) | collective-permute-done | bytes 69664 | tf_op jit(solution)/shard_map/ppermute | solution.py:22
  28.8 2.3 %collective-permute-start.12 = (bf16[8,2176]{1,0:T(8,128)(2,1)S(1)}, bf16[8,2176]{1,0:T(8,128)(2,1)S(1)}, u32[]{:S(2)}, u32[]{:S(2)}) collective-permute-start(bf16[8,2176]{1,0:T(8,128)(2,1)S(1)} %get-tuple-element.40), channel_id=1, source_target_pairs={{0,18},{2,16},{4,22},{6,20},{8,26},{10,24},{12,30},{14,28},{16,2},... | collective-permute-start | bytes 104456 | tf_op jit(solution)/shard_map/ppermute | solution.py:22
  31.1 2.1 %collective-permute-done.12.got = bf16[8,2176]{1,0:T(8,128)(2,1)S(1)} collective-permute-done((bf16[8,2176]{1,0:T(8,128)(2,1)S(1)}, bf16[8,2176]{1,0:T(8,128)(2,1)S(1)}, u32[]{:S(2)}, u32[]{:S(2)}) %collective-permute-start.12) | collective-permute-done | bytes 34848 | tf_op jit(solution)/shard_map/ppermute | solution.py:22
  33.2 0.3 merge_last.1
  33.5 1.5 %collective-permute-start.13 = (f32[8,128]{1,0:T(8,128)S(1)}, f32[8,128]{1,0:T(8,128)S(1)}, u32[]{:S(2)}, u32[]{:S(2)}) collective-permute-start(f32[8,128]{1,0:T(8,128)S(1)} %get-tuple-element.42.squares), channel_id=1, source_target_pairs={{0,1},{1,0},{2,3},{3,2},{4,5},{5,4},{6,7},{7,6},{8,9},{9,8},{10,11... | collective-permute-start | bytes 12296 | tf_op jit(solution)/shard_map/ppermute | solution.py:22
  35.0 2.1 %collective-permute-done.13.other = f32[8,128]{1,0:T(8,128)S(1)} collective-permute-done((f32[8,128]{1,0:T(8,128)S(1)}, f32[8,128]{1,0:T(8,128)S(1)}, u32[]{:S(2)}, u32[]{:S(2)}) %collective-permute-start.13) | collective-permute-done | bytes 4128 | tf_op jit(solution)/shard_map/ppermute | solution.py:22
  37.1 0.7 %normalize.1 = (bf16[4,2048]{1,0:T(4,128)(2,1)}, bf16[2,2048]{1,0:T(2,128)(2,1)}, bf16[1,2048]{1,0:T(2,128)(2,1)}) custom-call(f32[8,2048]{1,0:T(8,128)S(1)} %get-tuple-element.41.att, f32[8,128]{1,0:T(8,128)S(1)} %get-tuple-element.42.squares, f32[8,128]{1,0:T(8,128)S(1)} %collective-permute-done.13.other, f32[1,2048]{1,0:T(1,128)S(1)} %bitcast.6), custom_call_target="tpu_custom_call" | custom-call | tf_op jit(solution)/shard_map/normalize/pallas_call | solution.py:41
  (32 shorter events, 1.2 us)
Async XLA Ops:
  0.6 5.1 %copy-start.1 = (bf16[256,512]{1,0:T(8,128)(2,1)S(1)}, bf16[256,512]{1,0:T(8,128)(2,1)}, u32[]{:S(2)}) copy-start(bf16[256,512]{1,0:T(8,128)(2,1)} %refs_3_.1) | copy-start | bytes 786436
  0.6 5.1 %collective-permute-start = (bf16[4,2048]{1,0:T(4,128)(2,1)}, bf16[4,2048]{1,0:T(4,128)(2,1)S(1)}, u32[]{:S(2)}, u32[]{:S(2)}) collective-permute-start(bf16[4,2048]{1,0:T(4,128)(2,1)} %own.1), channel_id=1, source_target_pairs={{0,2},{2,0},{4,6},{6,4},{8,10},{10,8},{12,14},{14,12},{16,18},{18,... | collective-permute-start | bytes 49160 | tf_op jit(solution)/shard_map/ppermute | solution.py:22
  1.2 4.6 %collective-permute-start.1 = (bf16[4,2048]{1,0:T(4,128)(2,1)}, bf16[4,2048]{1,0:T(4,128)(2,1)S(1)}, u32[]{:S(2)}, u32[]{:S(2)}) collective-permute-start(bf16[4,2048]{1,0:T(4,128)(2,1)} %own.1), channel_id=1, source_target_pairs={{0,6},{2,4},{4,2},{6,0},{8,14},{10,12},{12,10},{14,8},{16,22},{18,... | collective-permute-start | bytes 49160 | tf_op jit(solution)/shard_map/ppermute | solution.py:22
  5.8 3.1 %copy-start.3 = (bf16[4,2048]{1,0:T(4,128)(2,1)S(1)}, bf16[4,2048]{1,0:T(4,128)(2,1)}, u32[]{:S(2)}) copy-start(bf16[4,2048]{1,0:T(4,128)(2,1)} %span_q.1) | copy-start | bytes 49156
  5.8 3.0 %copy-start.4 = (bf16[4,2048]{1,0:T(4,128)(2,1)S(1)}, bf16[4,2048]{1,0:T(4,128)(2,1)}, u32[]{:S(2)}) copy-start(bf16[4,2048]{1,0:T(4,128)(2,1)} %own.1) | copy-start | bytes 49156
  5.8 8.4 %collective-permute-start.4 = (bf16[256,512]{1,0:T(8,128)(2,1)S(1)}, bf16[256,512]{1,0:T(8,128)(2,1)S(1)}, u32[]{:S(2)}, u32[]{:S(2)}) collective-permute-start(bf16[256,512]{1,0:T(8,128)(2,1)S(1)} %get-tuple-element.28.k0), channel_id=1, source_target_pairs={{0,6},{2,4},{4,2},{6,0},{8,14},{10,12},{12,10},{14,8},{16,22},{18,... | collective-permute-start | bytes 786440 | tf_op jit(solution)/shard_map/ppermute | solution.py:22
  7.3 13.3 %collective-permute-start.6 = (bf16[288,512]{1,0:T(8,128)(2,1)}, bf16[288,512]{1,0:T(8,128)(2,1)S(1)}, u32[]{:S(2)}, u32[]{:S(2)}) collective-permute-start(bf16[288,512]{1,0:T(8,128)(2,1)} %get-tuple-element.30), channel_id=1, source_target_pairs={{0,6},{2,4},{4,2},{6,0},{8,14},{10,12},{12,10},{14,8},{16,22},{18,... | collective-permute-start | bytes 884744 | tf_op jit(solution)/shard_map/ppermute | solution.py:22
  7.6 1.2 %copy-start.6 = (s32[32]{0:T(128)S(1)}, s32[32]{0:T(128)}, u32[]{:S(2)}) copy-start(s32[32]{0:T(128)} %param.33) | copy-start | bytes 388
  7.6 1.2 %copy-start.7 = (s32[16]{0:T(128)S(1)}, s32[16]{0:T(128)}, u32[]{:S(2)}) copy-start(s32[16]{0:T(128)} %param.34) | copy-start | bytes 196
  7.7 1.2 %collective-permute-start.2 = (bf16[4,2048]{1,0:T(4,128)(2,1)S(1)}, bf16[4,2048]{1,0:T(4,128)(2,1)S(1)}, u32[]{:S(2)}, u32[]{:S(2)}) collective-permute-start(bf16[4,2048]{1,0:T(4,128)(2,1)S(1)} %get-tuple-element.27.q3), channel_id=1, source_target_pairs={{0,2},{2,0},{4,6},{6,4},{8,10},{10,8},{12,14},{14,12},{16,18},{18,... | collective-permute-start | bytes 49160 | tf_op jit(solution)/shard_map/ppermute | solution.py:22
  9.1 5.0 %collective-permute-start.3 = (bf16[16,2048]{1,0:T(8,128)(2,1)S(1)}, bf16[16,2048]{1,0:T(8,128)(2,1)S(1)}, u32[]{:S(2)}, u32[]{:S(2)}) collective-permute-start(bf16[16,2048]{1,0:T(8,128)(2,1)S(1)} %column_queries.1.mine), channel_id=1, source_target_pairs={{0,18},{2,16},{4,22},{6,20},{8,26},{10,24},{12,30},{14,28},{16,2},... | collective-permute-start | bytes 196616 | tf_op jit(solution)/shard_map/ppermute | solution.py:22
  14.3 8.6 %copy-start = (bf16[256,512]{1,0:T(8,128)(2,1)S(1)}, bf16[256,512]{1,0:T(8,128)(2,1)}, u32[]{:S(2)}) copy-start(bf16[256,512]{1,0:T(8,128)(2,1)} %v0.1) | copy-start | bytes 786436
  14.3 6.3 %collective-permute-start.5 = (bf16[20,2048]{1,0:T(8,128)(2,1)S(1)}, bf16[20,2048]{1,0:T(8,128)(2,1)S(1)}, u32[]{:S(2)}, u32[]{:S(2)}) collective-permute-start(bf16[20,2048]{1,0:T(8,128)(2,1)S(1)} %get-tuple-element.29.mine), channel_id=1, source_target_pairs={{0,10},{2,8},{4,14},{6,12},{8,2},{10,0},{12,6},{14,4},{16,26},{18,... | collective-permute-start | bytes 245768 | tf_op jit(solution)/shard_map/ppermute | solution.py:22
  16.3 6.2 %collective-permute-start.9 = (bf16[288,512]{1,0:T(8,128)(2,1)}, bf16[288,512]{1,0:T(8,128)(2,1)S(1)}, u32[]{:S(2)}, u32[]{:S(2)}) collective-permute-start(bf16[288,512]{1,0:T(8,128)(2,1)} %get-tuple-element.30), channel_id=1, source_target_pairs={{0,2},{2,0},{4,6},{6,4},{8,10},{10,8},{12,14},{14,12},{16,18},{18,... | collective-permute-start | bytes 884744 | tf_op jit(solution)/shard_map/ppermute | solution.py:22
  20.6 2.3 %copy-start.2 = (bf16[32,512]{1,0:T(8,128)(2,1)S(1)}, bf16[32,512]{1,0:T(8,128)(2,1)}, u32[]{:S(2)}) copy-start(bf16[32,512]{1,0:T(8,128)(2,1)} %get-tuple-element.34.extra) | copy-start | bytes 98308
  20.6 2.3 %collective-permute-start.10 = (bf16[288,512]{1,0:T(8,128)(2,1)S(1)}, bf16[288,512]{1,0:T(8,128)(2,1)S(1)}, u32[]{:S(2)}, u32[]{:S(2)}) collective-permute-start(bf16[288,512]{1,0:T(8,128)(2,1)S(1)} %get-tuple-element.33.v3), channel_id=1, source_target_pairs={{0,2},{2,0},{4,6},{6,4},{8,10},{10,8},{12,14},{14,12},{16,18},{18,... | collective-permute-start | bytes 884744 | tf_op jit(solution)/shard_map/ppermute | solution.py:22
  20.7 1.8 %collective-permute-start.7 = (bf16[256,512]{1,0:T(8,128)(2,1)S(1)}, bf16[256,512]{1,0:T(8,128)(2,1)S(1)}, u32[]{:S(2)}, u32[]{:S(2)}) collective-permute-start(bf16[256,512]{1,0:T(8,128)(2,1)S(1)} %get-tuple-element.28.k0), channel_id=1, source_target_pairs={{0,2},{2,0},{4,6},{6,4},{8,10},{10,8},{12,14},{14,12},{16,18},{18,... | collective-permute-start | bytes 786440 | tf_op jit(solution)/shard_map/ppermute | solution.py:22
  21.1 0.7 %copy-start.8 = (s32[64]{0:T(128)S(1)}, s32[64]{0:T(128)}, u32[]{:S(2)}) copy-start(s32[64]{0:T(128)} %param.23) | copy-start | bytes 772
  21.1 1.8 %collective-permute-start.8 = (bf16[256,512]{1,0:T(8,128)(2,1)S(1)}, bf16[256,512]{1,0:T(8,128)(2,1)S(1)}, u32[]{:S(2)}, u32[]{:S(2)}) collective-permute-start(bf16[256,512]{1,0:T(8,128)(2,1)S(1)} %get-tuple-element.32.k3), channel_id=1, source_target_pairs={{0,2},{2,0},{4,6},{6,4},{8,10},{10,8},{12,14},{14,12},{16,18},{18,... | collective-permute-start | bytes 786440 | tf_op jit(solution)/shard_map/ppermute | solution.py:22
  24.3 4.2 %collective-permute-start.11 = (bf16[16,2176]{1,0:T(8,128)(2,1)S(1)}, bf16[16,2176]{1,0:T(8,128)(2,1)S(1)}, u32[]{:S(2)}, u32[]{:S(2)}) collective-permute-start(bf16[16,2176]{1,0:T(8,128)(2,1)S(1)} %get-tuple-element.37), channel_id=1, source_target_pairs={{0,10},{2,8},{4,14},{6,12},{8,2},{10,0},{12,6},{14,4},{16,26},{18,... | collective-permute-start | bytes 208904 | tf_op jit(solution)/shard_map/ppermute | solution.py:22
  28.8 4.4 %collective-permute-start.12 = (bf16[8,2176]{1,0:T(8,128)(2,1)S(1)}, bf16[8,2176]{1,0:T(8,128)(2,1)S(1)}, u32[]{:S(2)}, u32[]{:S(2)}) collective-permute-start(bf16[8,2176]{1,0:T(8,128)(2,1)S(1)} %get-tuple-element.40), channel_id=1, source_target_pairs={{0,18},{2,16},{4,22},{6,20},{8,26},{10,24},{12,30},{14,28},{16,2},... | collective-permute-start | bytes 104456 | tf_op jit(solution)/shard_map/ppermute | solution.py:22
  33.2 3.9 %copy-start.5 = (f32[2048]{0:T(1024)S(1)}, f32[2048]{0:T(1024)}, u32[]{:S(2)}) copy-start(f32[2048]{0:T(1024)} %param.35) | copy-start | bytes 24580
  33.5 3.6 %collective-permute-start.13 = (f32[8,128]{1,0:T(8,128)S(1)}, f32[8,128]{1,0:T(8,128)S(1)}, u32[]{:S(2)}, u32[]{:S(2)}) collective-permute-start(f32[8,128]{1,0:T(8,128)S(1)} %get-tuple-element.42.squares), channel_id=1, source_target_pairs={{0,1},{1,0},{2,3},{3,2},{4,5},{5,4},{6,7},{7,6},{8,9},{9,8},{10,11... | collective-permute-start | bytes 12296 | tf_op jit(solution)/shard_map/ppermute | solution.py:22

commit v4 on v3

--- a/solution.py
+++ b/solution.py
@@ -15,6 +15,8 @@
 BF16 = jnp.bfloat16
 VMEM = pltpu.VMEM
 PLAN_LIMIT = 59 * 2**20
+PLAN_BYTES = 108000000
+PLAN_FLOPS = 34500000000
 
 
 def exchange(value, axis, mask):
@@ -23,7 +25,7 @@
 
 
 def call(
-    kernel, name, out_shape, *operands, scratch=(), places=None, aliases=None, out_any=(), limit=16 * 2**20
+    kernel, name, out_shape, *operands, scratch=(), places=None, cost=None, aliases=None, out_any=(), limit=16 * 2**20
 ):
     places = places or {}
     in_specs = [
@@ -46,6 +48,7 @@
         scratch_shapes=list(scratch),
         input_output_aliases=aliases,
         compiler_params=pltpu.CompilerParams(vmem_limit_bytes=limit),
+        cost_estimate=cost,
         name=name,
     )(*operands)
 
@@ -85,7 +88,7 @@
     sizes, place,
     ids_h, idx1_h, idx2_h, table_h, span_k_h, span_v_h,
     fk_h, fv_h, rk_h, rv_h, mk_h, mv_h, cache_v_h,
-    values, extra, *scratch,
+    values, extra, done, *scratch,
 ):
     spans, frames = sizes
     given = (ids_h, idx1_h, idx2_h, table_h, span_k_h, span_v_h,
@@ -124,6 +127,7 @@
     parts = jnp.concatenate([*sets[0::2], rest, *sets[1::2], rest], axis=0).astype(BF16)
     extra[...] = parts
     values[cached:, :] = parts
+    done[...] = jnp.zeros(done.shape, F32)
     copies[-1].wait()
 
 
@@ -172,7 +176,7 @@
     return jnp.concatenate([part.astype(F32) for part in parts], axis=0).astype(BF16)
 
 
-def select_kernel(sizes, place, idx1, idx2, span_q, own, q1, q2, q3, out):
+def select_kernel(sizes, place, idx1, idx2, span_q, pair, other, out):
     spans, frames, n1, n2, mask_bits = sizes
     me = place[0]
     column = (me & 3) ^ parity(me >> 2, mask_bits)
@@ -192,7 +196,7 @@
     chosen = jnp.where((lane >= spans) & (row >= spans) & (wanted == position), 1.0, 0.0)
     copied = jnp.where((row < spans) & (lane == row), 1.0, 0.0)
     pick = (chosen + copied).astype(BF16)
-    given = stacked([q[...] for q in (span_q, own, q1, q2, q3)])
+    given = stacked([span_q[...], pair[0:frames], other[...], pair[frames:]])
     out[...] = jnp.dot(pick, given, preferred_element_type=F32).astype(BF16)
 
 
@@ -200,8 +204,15 @@
     pass
 
 
-def stage_kernel(*refs):
-    refs[-1][...] = refs[len(refs) // 2 - 1][...]
+def listed_kernel(_, idx1, idx2, out1, out2):
+    out1[...] = idx1[...]
+    out2[...] = idx2[...]
+
+
+def stage_kernel(cached, spans, mine, other, copied, pair, copied_spans):
+    copied[...] = cached[...]
+    copied_spans[...] = spans[...]
+    pair[...] = stacked([mine[...], other[...]])
 
 
 def tie(*arrays):
@@ -216,7 +227,7 @@
     )
 
 
-def grow_kernel(spans, mine, other, _, out, __):
+def grow_kernel(spans, mine, other, _, __, out, *___):
     a = mine[...].astype(F32)
     b = other[...].astype(F32)
     out[...] = jnp.concatenate(
@@ -400,37 +411,47 @@
     extras = -(-3 * spans // 16) * 16
 
     q3 = exchange(frame_q, "ctx", 3)
-    q1 = exchange(frame_q, "ctx", 1)
     small = (
         action_ids[None, :], pass1_idx[None, :], pass2_idx[None, :],
         action_table, span_k, span_v, frame_k, frame_v, revealed_k, revealed_v,
         mask_k, mask_v,
     )
     place = me.reshape(1)
-    values, extra = call(
+    values, extra, token = call(
         functools.partial(keys_kernel, (spans, frames)),
         "plane_values",
         [
             jax.ShapeDtypeStruct((cache_v.shape[0] + 2 * extras, width), BF16),
             jax.ShapeDtypeStruct((2 * extras, width), BF16),
+            jax.ShapeDtypeStruct((8, HD), F32),
         ],
         place, *small, cache_v,
         places={0: pltpu.SMEM, **{i + 1: pl.ANY for i in range(len(small) + 1)}},
         scratch=[pltpu.VMEM(array.shape, array.dtype) for array in small]
         + [pltpu.SemaphoreType.DMA((len(small) + 1,))],
         limit=PLAN_LIMIT,
-    )
-    moved = (q1, q3, values)
-    q1, q3, values, k0 = call(
+        cost=pl.CostEstimate(flops=PLAN_FLOPS, bytes_accessed=PLAN_BYTES, transcendentals=0),
+    )
+    k0, chip, own_spans = call(
         stage_kernel,
-        "plane_queries_arrived",
-        [jax.ShapeDtypeStruct(array.shape, array.dtype) for array in (*moved, cache_k)],
-        *moved, cache_k,
-        places={i: pl.ANY for i in range(len(moved))},
-        aliases={i: i for i in range(len(moved))},
-    )
-    q2 = exchange(q3, "ctx", 1)
-    k3 = exchange(k0, "ctx", 3)
+        "queries_arrived",
+        [
+            jax.ShapeDtypeStruct(cache_k.shape, BF16),
+            jax.ShapeDtypeStruct((2 * frames, q_width), BF16),
+            jax.ShapeDtypeStruct(span_q.shape, BF16),
+        ],
+        cache_k, span_q, frame_q, q3,
+    )
+    other_chip = exchange(chip, "ctx", 1)
+    idx1, idx2 = call(
+        listed_kernel,
+        "listed",
+        [jax.ShapeDtypeStruct((1, idx.shape[0]), idx.dtype) for idx in (pass1_idx, pass2_idx)],
+        token, pass1_idx[None, :], pass2_idx[None, :],
+        places={0: pl.ANY},
+        cost=pl.CostEstimate(flops=PLAN_FLOPS, bytes_accessed=PLAN_BYTES, transcendentals=0),
+    )
+    k3 = exchange(cache_k, "ctx", 3)
     v3 = exchange(values, "ctx", 3)
     k1 = exchange(k0, "ctx", 1)
     v1 = exchange(values, "ctx", 1)
@@ -439,28 +460,29 @@
         functools.partial(select_kernel, (spans, frames, n1, n2, len(bits))),
         "column_queries",
         jax.ShapeDtypeStruct((spans + blocks * picked, q_width), BF16),
-        place, pass1_idx[None, :], pass2_idx[None, :], span_q, frame_q, q1, q2, q3,
+        place, idx1, idx2, own_spans, chip, other_chip,
         places={0: pltpu.SMEM},
     )
 
     held = spans
     for bit in bits[:-1]:
         other = exchange(state, "ctx", bit)
-        state, k3 = call(
+        state, k3, k1 = call(
             functools.partial(grow_kernel, held),
             "more_queries",
             [
                 jax.ShapeDtypeStruct((state.shape[0] + held, q_width), BF16),
                 jax.ShapeDtypeStruct(k3.shape, BF16),
+                jax.ShapeDtypeStruct(k1.shape, BF16),
             ],
-            state, other, k3,
-            places={2: pl.ANY},
-            aliases={2: 1},
+            state, other, k3, k1,
+            places={2: pl.ANY, 3: pl.ANY},
+            aliases={2: 1, 3: 2},
         )
         held = 2 * held
     other = exchange(state, "ctx", bits[-1])
     k2 = exchange(k3, "ctx", 1)
-    other, v3 = tie(other, v3)
+    other, v3, k2 = tie(other, v3, k2)
     v2 = exchange(v3, "ctx", 1)
 
     perm, allowed = call(

time: 38 us -> 35.3 us (0.929)
  waiting for transfers between devices: 15.7 us -> 11.3 us
  starting transfers between devices: 15.8 us -> 17.2 us
    ppermute x14 -> x13, waiting for transfers between devices: 15.7 us -> 11.3 us  [exchange(): return lax.ppermute(value, axis, pairs)]
    ppermute x14 -> x13, starting transfers between devices: 15.8 us -> 17.2 us  [exchange(): return lax.ppermute(value, axis, pairs)]
    unnamed x18 -> x22, local copies, waits for them, and re-layouts: 0.58 us -> 0.9 us
    pallas_call x10 -> x11, Pallas kernels: 4.99 us -> 4.96 us  [call(): pl.pallas_call(kernel, out_shape=out_shape, in_specs=in_specs, out_specs=...]
  transfers between devices with their start and end apart: 14 -> 13, of which waited for: 9 -> 7; matrix products, arithmetic and copies ran while one was open for 0% -> 0% of each run, Pallas kernels for 6% -> 7%
where the time goes in v4:
time: 35.3 us; the launch traced here: 35.1 us
  starting transfers between devices  17.2 us (49%)
  waiting for transfers between devices  11.3 us (32%)
  Pallas kernels  4.96 us (14%)
  local copies, waits for them, and re-layouts  0.9 us (3%)
  between operations  0.76 us (2%)
    ppermute x13, starting transfers between devices, exchange(): return lax.ppermute(value, axis, pairs)  17.2 us
    ppermute x13, waiting for transfers between devices, exchange(): return lax.ppermute(value, axis, pairs)  11.3 us
    pallas_call x11, Pallas kernels, call(): pl.pallas_call(kernel, out_shape=out_shape, in_specs=in_specs, out_specs=...  4.96 us
    unnamed x22, local copies, waits for them, and re-layouts  0.9 us
  transfers between devices with their start and end apart: 13, of which 7 were waited for; matrix products, arithmetic and copies ran while one was open for 0% of the time, Pallas kernels for 7%

profile of v4, /device:TPU:0, one launch (start us, length us, event | category | flops | bytes accessed | tf_op | source)
XLA Modules:
  0.0 35.1 jit_solution(378461064119013356)
XLA Ops:
  0.6 2.5 %collective-permute-start = (bf16[4,2048]{1,0:T(4,128)(2,1)}, bf16[4,2048]{1,0:T(4,128)(2,1)S(1)}, u32[]{:S(2)}, u32[]{:S(2)}) collective-permute-start(bf16[4,2048]{1,0:T(4,128)(2,1)} %mine.1), channel_id=1, source_target_pairs={{0,6},{2,4},{4,2},{6,0},{8,14},{10,12},{12,10},{14,8},{16,22},{18,... | collective-permute-start | bytes 49160 | tf_op jit(solution)/shard_map/ppermute | solution.py:24
  3.2 1.9 %plane_values.1 = (bf16[288,512]{1,0:T(8,128)(2,1)}, bf16[32,512]{1,0:T(8,128)(2,1)}, f32[8,128]{1,0:T(8,128)}) custom-call(s32[1]{0:T(128)} %bitcast.place, s32[1,4]{1,0:T(1,128)} %bitcast.12, s32[1,32]{1,0:T(1,128)} %bitcast.7, s32[1,16]{1,0:T(1,128)} %bitcast.9, bf16[18,512]{1,0:T(8,128)(2,1)} %table_h.1, bf16[4,512]{1,0:T(4,128)(2,1)} %span_k_h.1, ...), custom_call_target="tpu_custom_call" | custom-call | flops 34500001792 | bytes 108000000 | tf_op jit(solution)/shard_map/plane_values/pallas_call | solution.py:43
  5.2 0.7 %collective-permute-start.1 = (bf16[8,2048]{1,0:T(8,128)(2,1)S(1)}, bf16[8,2048]{1,0:T(8,128)(2,1)S(1)}, u32[]{:S(2)}, u32[]{:S(2)}) collective-permute-start(bf16[8,2048]{1,0:T(8,128)(2,1)S(1)} %get-tuple-element.33.pair), channel_id=1, source_target_pairs={{0,2},{2,0},{4,6},{6,4},{8,10},{10,8},{12,14},{14,12},{16,18},{18,... | collective-permute-start | bytes 98312 | tf_op jit(solution)/shard_map/ppermute | solution.py:24
  6.1 0.5 %copy-done.6 = s32[32]{0:T(128)S(1)} copy-done((s32[32]{0:T(128)S(1)}, s32[32]{0:T(128)}, u32[]{:S(2)}) %copy-start.6) | copy-done | bytes 152
  6.8 0.2 column_queries.1.mine
  7.0 2.8 %collective-permute-start.2 = (bf16[16,2048]{1,0:T(8,128)(2,1)S(1)}, bf16[16,2048]{1,0:T(8,128)(2,1)S(1)}, u32[]{:S(2)}, u32[]{:S(2)}) collective-permute-start(bf16[16,2048]{1,0:T(8,128)(2,1)S(1)} %column_queries.1.mine), channel_id=1, source_target_pairs={{0,18},{2,16},{4,22},{6,20},{8,26},{10,24},{12,30},{14,28},{16,2},... | collective-permute-start | bytes 196616 | tf_op jit(solution)/shard_map/ppermute | solution.py:24
  9.8 1.5 %collective-permute-start.6 = (bf16[288,512]{1,0:T(8,128)(2,1)S(1)}, bf16[288,512]{1,0:T(8,128)(2,1)S(1)}, u32[]{:S(2)}, u32[]{:S(2)}) collective-permute-start(bf16[288,512]{1,0:T(8,128)(2,1)S(1)} %copy-done.10), channel_id=1, source_target_pairs={{0,6},{2,4},{4,2},{6,0},{8,14},{10,12},{12,10},{14,8},{16,22},{18,... | collective-permute-start | bytes 884744 | tf_op jit(solution)/shard_map/ppermute | solution.py:24
  11.3 0.7 %collective-permute-done.2.other = bf16[16,2048]{1,0:T(8,128)(2,1)S(1)} collective-permute-done((bf16[16,2048]{1,0:T(8,128)(2,1)S(1)}, bf16[16,2048]{1,0:T(8,128)(2,1)S(1)}, u32[]{:S(2)}, u32[]{:S(2)}) %collective-permute-start.2) | collective-permute-done | bytes 65568 | tf_op jit(solution)/shard_map/ppermute | solution.py:24
  12.1 1.8 %collective-permute-start.7 = (bf16[256,512]{1,0:T(8,128)(2,1)S(1)}, bf16[256,512]{1,0:T(8,128)(2,1)S(1)}, u32[]{:S(2)}, u32[]{:S(2)}) collective-permute-start(bf16[256,512]{1,0:T(8,128)(2,1)S(1)} %get-tuple-element.37.k3), channel_id=1, source_target_pairs={{0,2},{2,0},{4,6},{6,4},{8,10},{10,8},{12,14},{14,12},{16,18},{18,... | collective-permute-start | bytes 786440 | tf_op jit(solution)/shard_map/ppermute | solution.py:24
  13.8 1.3 %collective-permute-start.5 = (bf16[20,2048]{1,0:T(8,128)(2,1)S(1)}, bf16[20,2048]{1,0:T(8,128)(2,1)S(1)}, u32[]{:S(2)}, u32[]{:S(2)}) collective-permute-start(bf16[20,2048]{1,0:T(8,128)(2,1)S(1)} %get-tuple-element.35.mine), channel_id=1, source_target_pairs={{0,10},{2,8},{4,14},{6,12},{8,2},{10,0},{12,6},{14,4},{16,26},{18,... | collective-permute-start | bytes 245768 | tf_op jit(solution)/shard_map/ppermute | solution.py:24
  15.2 3.5 %collective-permute-done.6.__1_ = bf16[288,512]{1,0:T(8,128)(2,1)S(1)} collective-permute-done((bf16[288,512]{1,0:T(8,128)(2,1)S(1)}, bf16[288,512]{1,0:T(8,128)(2,1)S(1)}, u32[]{:S(2)}, u32[]{:S(2)}) %collective-permute-start.6) | collective-permute-done | bytes 294944 | tf_op jit(solution)/shard_map/ppermute | solution.py:24
  18.7 0.4 %collective-permute-start.9 = (bf16[288,512]{1,0:T(8,128)(2,1)S(1)}, bf16[288,512]{1,0:T(8,128)(2,1)S(1)}, u32[]{:S(2)}, u32[]{:S(2)}) collective-permute-start(bf16[288,512]{1,0:T(8,128)(2,1)S(1)} %get-tuple-element.41.v3), channel_id=1, source_target_pairs={{0,2},{2,0},{4,6},{6,4},{8,10},{10,8},{12,14},{14,12},{16,18},{18,... | collective-permute-start | bytes 884744 | tf_op jit(solution)/shard_map/ppermute | solution.py:24
  19.1 0.3 copy-done.8
  19.5 0.8 %collective-permute-done.9.v2 = bf16[288,512]{1,0:T(8,128)(2,1)S(1)} collective-permute-done((bf16[288,512]{1,0:T(8,128)(2,1)S(1)}, bf16[288,512]{1,0:T(8,128)(2,1)S(1)}, u32[]{:S(2)}, u32[]{:S(2)}) %collective-permute-start.9) | collective-permute-done | bytes 294944 | tf_op jit(solution)/shard_map/ppermute | solution.py:24
  20.4 1.4 %plane_attention.1 = (bf16[16,2176]{1,0:T(8,128)(2,1)S(1)}, f32[16,2048]{1,0:T(8,128)S(1)}, f32[16,128]{1,0:T(8,128)S(1)}) custom-call(bf16[32,40]{1,0:T(8,128)(2,1)S(1)} %get-tuple-element.27.perm, f32[32,64]{1,0:T(8,128)S(1)} %get-tuple-element.28.allowed, bf16[20,2048]{1,0:T(8,128)(2,1)S(1)} %get-tuple-element.35.mine, ...), custom_call_target="tpu_custom_call" | custom-call | tf_op jit(solution)/shard_map/plane_attention/pallas_call | solution.py:43
  21.8 1.5 %collective-permute-start.10 = (bf16[16,2176]{1,0:T(8,128)(2,1)S(1)}, bf16[16,2176]{1,0:T(8,128)(2,1)S(1)}, u32[]{:S(2)}, u32[]{:S(2)}) collective-permute-start(bf16[16,2176]{1,0:T(8,128)(2,1)S(1)} %get-tuple-element.45), channel_id=1, source_target_pairs={{0,10},{2,8},{4,14},{6,12},{8,2},{10,0},{12,6},{14,4},{16,26},{18,... | collective-permute-start | bytes 208904 | tf_op jit(solution)/shard_map/ppermute | solution.py:24
  23.3 2.6 %collective-permute-done.10.got = bf16[16,2176]{1,0:T(8,128)(2,1)S(1)} collective-permute-done((bf16[16,2176]{1,0:T(8,128)(2,1)S(1)}, bf16[16,2176]{1,0:T(8,128)(2,1)S(1)}, u32[]{:S(2)}, u32[]{:S(2)}) %collective-permute-start.10) | collective-permute-done | bytes 69664 | tf_op jit(solution)/shard_map/ppermute | solution.py:24
  25.9 0.3 merge_partials.1
  26.2 2.7 %collective-permute-start.11 = (bf16[8,2176]{1,0:T(8,128)(2,1)S(1)}, bf16[8,2176]{1,0:T(8,128)(2,1)S(1)}, u32[]{:S(2)}, u32[]{:S(2)}) collective-permute-start(bf16[8,2176]{1,0:T(8,128)(2,1)S(1)} %get-tuple-element.48), channel_id=1, source_target_pairs={{0,18},{2,16},{4,22},{6,20},{8,26},{10,24},{12,30},{14,28},{16,2},... | collective-permute-start | bytes 104456 | tf_op jit(solution)/shard_map/ppermute | solution.py:24
  28.8 1.7 %collective-permute-done.11.got = bf16[8,2176]{1,0:T(8,128)(2,1)S(1)} collective-permute-done((bf16[8,2176]{1,0:T(8,128)(2,1)S(1)}, bf16[8,2176]{1,0:T(8,128)(2,1)S(1)}, u32[]{:S(2)}, u32[]{:S(2)}) %collective-permute-start.11) | collective-permute-done | bytes 34848 | tf_op jit(solution)/shard_map/ppermute | solution.py:24
  30.5 0.3 merge_last.1
  30.8 1.9 %collective-permute-start.12 = (f32[8,128]{1,0:T(8,128)S(1)}, f32[8,128]{1,0:T(8,128)S(1)}, u32[]{:S(2)}, u32[]{:S(2)}) collective-permute-start(f32[8,128]{1,0:T(8,128)S(1)} %get-tuple-element.50.squares), channel_id=1, source_target_pairs={{0,1},{1,0},{2,3},{3,2},{4,5},{5,4},{6,7},{7,6},{8,9},{9,8},{10,11... | collective-permute-start | bytes 12296 | tf_op jit(solution)/shard_map/ppermute | solution.py:24
  32.6 1.8 %collective-permute-done.12.other = f32[8,128]{1,0:T(8,128)S(1)} collective-permute-done((f32[8,128]{1,0:T(8,128)S(1)}, f32[8,128]{1,0:T(8,128)S(1)}, u32[]{:S(2)}, u32[]{:S(2)}) %collective-permute-start.12) | collective-permute-done | bytes 4128 | tf_op jit(solution)/shard_map/ppermute | solution.py:24
  34.4 0.7 %normalize.1 = (bf16[4,2048]{1,0:T(4,128)(2,1)}, bf16[2,2048]{1,0:T(2,128)(2,1)}, bf16[1,2048]{1,0:T(2,128)(2,1)}) custom-call(f32[8,2048]{1,0:T(8,128)S(1)} %get-tuple-element.49.att, f32[8,128]{1,0:T(8,128)S(1)} %get-tuple-element.50.squares, f32[8,128]{1,0:T(8,128)S(1)} %collective-permute-done.12.other, f32[1,2048]{1,0:T(1,128)S(1)} %bitcast.6), custom_call_target="tpu_custom_call" | custom-call | tf_op jit(solution)/shard_map/normalize/pallas_call | solution.py:43
  (35 shorter events, 0.7 us)
Async XLA Ops:
  0.6 4.5 %collective-permute-start = (bf16[4,2048]{1,0:T(4,128)(2,1)}, bf16[4,2048]{1,0:T(4,128)(2,1)S(1)}, u32[]{:S(2)}, u32[]{:S(2)}) collective-permute-start(bf16[4,2048]{1,0:T(4,128)(2,1)} %mine.1), channel_id=1, source_target_pairs={{0,6},{2,4},{4,2},{6,0},{8,14},{10,12},{12,10},{14,8},{16,22},{18,... | collective-permute-start | bytes 49160 | tf_op jit(solution)/shard_map/ppermute | solution.py:24
  3.1 8.9 %collective-permute-start.3 = (bf16[256,512]{1,0:T(8,128)(2,1)}, bf16[256,512]{1,0:T(8,128)(2,1)S(1)}, u32[]{:S(2)}, u32[]{:S(2)}) collective-permute-start(bf16[256,512]{1,0:T(8,128)(2,1)} %cached.1), channel_id=1, source_target_pairs={{0,6},{2,4},{4,2},{6,0},{8,14},{10,12},{12,10},{14,8},{16,22},{18,... | collective-permute-start | bytes 786440 | tf_op jit(solution)/shard_map/ppermute | solution.py:24
  3.2 2.0 %copy-start.1 = (bf16[256,512]{1,0:T(8,128)(2,1)S(1)}, bf16[256,512]{1,0:T(8,128)(2,1)}, u32[]{:S(2)}) copy-start(bf16[256,512]{1,0:T(8,128)(2,1)} %cached.1) | copy-start | bytes 786436
  3.2 2.0 %copy-start.3 = (bf16[4,2048]{1,0:T(4,128)(2,1)S(1)}, bf16[4,2048]{1,0:T(4,128)(2,1)}, u32[]{:S(2)}) copy-start(bf16[4,2048]{1,0:T(4,128)(2,1)} %spans.1) | copy-start | bytes 49156
  3.2 2.0 %copy-start.4 = (bf16[4,2048]{1,0:T(4,128)(2,1)S(1)}, bf16[4,2048]{1,0:T(4,128)(2,1)}, u32[]{:S(2)}) copy-start(bf16[4,2048]{1,0:T(4,128)(2,1)} %mine.1) | copy-start | bytes 49156
  5.2 0.9 %copy-start.9 = (f32[8,128]{1,0:T(8,128)S(1)}, f32[8,128]{1,0:T(8,128)}, u32[]{:S(2)}) copy-start(f32[8,128]{1,0:T(8,128)} %get-tuple-element.29._) | copy-start | bytes 12292
  5.2 1.6 %collective-permute-start.1 = (bf16[8,2048]{1,0:T(8,128)(2,1)S(1)}, bf16[8,2048]{1,0:T(8,128)(2,1)S(1)}, u32[]{:S(2)}, u32[]{:S(2)}) collective-permute-start(bf16[8,2048]{1,0:T(8,128)(2,1)S(1)} %get-tuple-element.33.pair), channel_id=1, source_target_pairs={{0,2},{2,0},{4,6},{6,4},{8,10},{10,8},{12,14},{14,12},{16,18},{18,... | collective-permute-start | bytes 98312 | tf_op jit(solution)/shard_map/ppermute | solution.py:24
  6.0 0.7 %copy-start.6 = (s32[32]{0:T(128)S(1)}, s32[32]{0:T(128)}, u32[]{:S(2)}) copy-start(s32[32]{0:T(128)} %param.33) | copy-start | bytes 388
  6.0 0.7 %copy-start.7 = (s32[16]{0:T(128)S(1)}, s32[16]{0:T(128)}, u32[]{:S(2)}) copy-start(s32[16]{0:T(128)} %param.34) | copy-start | bytes 196
  6.0 6.1 %collective-permute-start.4 = (bf16[256,512]{1,0:T(8,128)(2,1)S(1)}, bf16[256,512]{1,0:T(8,128)(2,1)S(1)}, u32[]{:S(2)}, u32[]{:S(2)}) collective-permute-start(bf16[256,512]{1,0:T(8,128)(2,1)S(1)} %get-tuple-element.34.k0), channel_id=1, source_target_pairs={{0,2},{2,0},{4,6},{6,4},{8,10},{10,8},{12,14},{14,12},{16,18},{18,... | collective-permute-start | bytes 786440 | tf_op jit(solution)/shard_map/ppermute | solution.py:24
  6.6 3.2 %copy-start.10 = (bf16[288,512]{1,0:T(8,128)(2,1)S(1)}, bf16[288,512]{1,0:T(8,128)(2,1)}, u32[]{:S(2)}) copy-start(bf16[288,512]{1,0:T(8,128)(2,1)} %get-tuple-element.36) | copy-start | bytes 884740
  7.0 5.0 %collective-permute-start.2 = (bf16[16,2048]{1,0:T(8,128)(2,1)S(1)}, bf16[16,2048]{1,0:T(8,128)(2,1)S(1)}, u32[]{:S(2)}, u32[]{:S(2)}) collective-permute-start(bf16[16,2048]{1,0:T(8,128)(2,1)S(1)} %column_queries.1.mine), channel_id=1, source_target_pairs={{0,18},{2,16},{4,22},{6,20},{8,26},{10,24},{12,30},{14,28},{16,2},... | collective-permute-start | bytes 196616 | tf_op jit(solution)/shard_map/ppermute | solution.py:24
  9.8 8.8 %collective-permute-start.6 = (bf16[288,512]{1,0:T(8,128)(2,1)S(1)}, bf16[288,512]{1,0:T(8,128)(2,1)S(1)}, u32[]{:S(2)}, u32[]{:S(2)}) collective-permute-start(bf16[288,512]{1,0:T(8,128)(2,1)S(1)} %copy-done.10), channel_id=1, source_target_pairs={{0,6},{2,4},{4,2},{6,0},{8,14},{10,12},{12,10},{14,8},{16,22},{18,... | collective-permute-start | bytes 884744 | tf_op jit(solution)/shard_map/ppermute | solution.py:24
  12.1 6.6 %collective-permute-start.7 = (bf16[256,512]{1,0:T(8,128)(2,1)S(1)}, bf16[256,512]{1,0:T(8,128)(2,1)S(1)}, u32[]{:S(2)}, u32[]{:S(2)}) collective-permute-start(bf16[256,512]{1,0:T(8,128)(2,1)S(1)} %get-tuple-element.37.k3), channel_id=1, source_target_pairs={{0,2},{2,0},{4,6},{6,4},{8,10},{10,8},{12,14},{14,12},{16,18},{18,... | collective-permute-start | bytes 786440 | tf_op jit(solution)/shard_map/ppermute | solution.py:24
  13.8 6.5 %copy-start = (bf16[256,512]{1,0:T(8,128)(2,1)S(1)}, bf16[256,512]{1,0:T(8,128)(2,1)}, u32[]{:S(2)}) copy-start(bf16[256,512]{1,0:T(8,128)(2,1)} %v0.1) | copy-start | bytes 786436
  13.8 4.9 %collective-permute-start.5 = (bf16[20,2048]{1,0:T(8,128)(2,1)S(1)}, bf16[20,2048]{1,0:T(8,128)(2,1)S(1)}, u32[]{:S(2)}, u32[]{:S(2)}) collective-permute-start(bf16[20,2048]{1,0:T(8,128)(2,1)S(1)} %get-tuple-element.35.mine), channel_id=1, source_target_pairs={{0,10},{2,8},{4,14},{6,12},{8,2},{10,0},{12,6},{14,4},{16,26},{18,... | collective-permute-start | bytes 245768 | tf_op jit(solution)/shard_map/ppermute | solution.py:24
  15.1 4.4 %collective-permute-start.8 = (bf16[288,512]{1,0:T(8,128)(2,1)S(1)}, bf16[288,512]{1,0:T(8,128)(2,1)S(1)}, u32[]{:S(2)}, u32[]{:S(2)}) collective-permute-start(bf16[288,512]{1,0:T(8,128)(2,1)S(1)} %copy-done.10), channel_id=1, source_target_pairs={{0,2},{2,0},{4,6},{6,4},{8,10},{10,8},{12,14},{14,12},{16,18},{18,... | collective-permute-start | bytes 884744 | tf_op jit(solution)/shard_map/ppermute | solution.py:24
  18.7 1.7 %copy-start.2 = (bf16[32,512]{1,0:T(8,128)(2,1)S(1)}, bf16[32,512]{1,0:T(8,128)(2,1)}, u32[]{:S(2)}) copy-start(bf16[32,512]{1,0:T(8,128)(2,1)} %get-tuple-element.42.extra) | copy-start | bytes 98308
  18.7 0.7 %copy-start.8 = (s32[64]{0:T(128)S(1)}, s32[64]{0:T(128)}, u32[]{:S(2)}) copy-start(s32[64]{0:T(128)} %param.23) | copy-start | bytes 772
  18.7 1.6 %collective-permute-start.9 = (bf16[288,512]{1,0:T(8,128)(2,1)S(1)}, bf16[288,512]{1,0:T(8,128)(2,1)S(1)}, u32[]{:S(2)}, u32[]{:S(2)}) collective-permute-start(bf16[288,512]{1,0:T(8,128)(2,1)S(1)} %get-tuple-element.41.v3), channel_id=1, source_target_pairs={{0,2},{2,0},{4,6},{6,4},{8,10},{10,8},{12,14},{14,12},{16,18},{18,... | collective-permute-start | bytes 884744 | tf_op jit(solution)/shard_map/ppermute | solution.py:24
  21.8 4.2 %collective-permute-start.10 = (bf16[16,2176]{1,0:T(8,128)(2,1)S(1)}, bf16[16,2176]{1,0:T(8,128)(2,1)S(1)}, u32[]{:S(2)}, u32[]{:S(2)}) collective-permute-start(bf16[16,2176]{1,0:T(8,128)(2,1)S(1)} %get-tuple-element.45), channel_id=1, source_target_pairs={{0,10},{2,8},{4,14},{6,12},{8,2},{10,0},{12,6},{14,4},{16,26},{18,... | collective-permute-start | bytes 208904 | tf_op jit(solution)/shard_map/ppermute | solution.py:24
  26.2 4.3 %collective-permute-start.11 = (bf16[8,2176]{1,0:T(8,128)(2,1)S(1)}, bf16[8,2176]{1,0:T(8,128)(2,1)S(1)}, u32[]{:S(2)}, u32[]{:S(2)}) collective-permute-start(bf16[8,2176]{1,0:T(8,128)(2,1)S(1)} %get-tuple-element.48), channel_id=1, source_target_pairs={{0,18},{2,16},{4,22},{6,20},{8,26},{10,24},{12,30},{14,28},{16,2},... | collective-permute-start | bytes 104456 | tf_op jit(solution)/shard_map/ppermute | solution.py:24
  30.5 3.9 %copy-start.5 = (f32[2048]{0:T(1024)S(1)}, f32[2048]{0:T(1024)}, u32[]{:S(2)}) copy-start(f32[2048]{0:T(1024)} %param.35) | copy-start | bytes 24580
  30.8 3.6 %collective-permute-start.12 = (f32[8,128]{1,0:T(8,128)S(1)}, f32[8,128]{1,0:T(8,128)S(1)}, u32[]{:S(2)}, u32[]{:S(2)}) collective-permute-start(f32[8,128]{1,0:T(8,128)S(1)} %get-tuple-element.50.squares), channel_id=1, source_target_pairs={{0,1},{1,0},{2,3},{3,2},{4,5},{5,4},{6,7},{7,6},{8,9},{9,8},{10,11... | collective-permute-start | bytes 12296 | tf_op jit(solution)/shard_map/ppermute | solution.py:24

commit v5 on v4

--- a/solution.py
+++ b/solution.py
@@ -252,18 +252,20 @@
 
 
 def attention_kernel(
-    heads, rows, extras, keep,
-    perm, allowed, mine, other, k0, k1, k2, k3, v0, v1, v2, v3, extra,
-    send, kept, kept_stats,
+    heads, first_row, extras,
+    perm, allowed, mine, other, k0, k1, k2, k3, v0, v1, v2, v3, extra, *outs,
 ):
+    rows = perm.shape[0] // 2
+    half = slice(first_row, first_row + rows)
+    message = len(outs) == 1
     queries = jnp.dot(
-        perm[...], stacked([mine[...], other[...]]), preferred_element_type=F32
+        perm[half, :], stacked([mine[...], other[...]]), preferred_element_type=F32
     ).astype(BF16)
     wide = heads * GROUP * HD
     scaling = HD ** (-0.5)
     cached = k0.shape[0]
     stack = GROUP if rows * GROUP <= 128 else 1
-    permit = jnp.concatenate([allowed[...]] * stack, axis=0) > 0.0
+    permit = jnp.concatenate([allowed[half, :]] * stack, axis=0) > 0.0
     nt = (((1,), (1,)), ((), ()))
     lane = iota((rows, HD), 1)
     stats = jnp.zeros((rows, HD), F32)
@@ -296,36 +298,36 @@
         return top, total + weights[-1].sum(axis=1, keepdims=True), weights
 
     steps = range(0, heads * GROUP, stack)
-    for first in range(0, len(steps), 2):
-        group = steps[first : first + 2]
+    for first in range(0, len(steps), 4):
+        group = steps[first : first + 4]
         scored = [scores_of(head) for head in group]
         weighed = [weights_of(scores) for scores in scored]
         for head, (top, total, weights) in zip(group, weighed):
-            out = functools.reduce(
-                jnp.add,
-                [
-                    jnp.dot(w.astype(BF16), value, preferred_element_type=F32)
-                    for w, value in zip(
-                        weights, blocks_of((v0, v1, v2, v3), head // GROUP, extras)
-                    )
-                ],
-            )
+            values = blocks_of((v0, v1, v2, v3), head // GROUP, extras)
+            weights = [w.astype(BF16) for w in weights]
+            out = jnp.dot(
+                jnp.concatenate(weights[:-1], axis=1),
+                jnp.concatenate(values[:-1], axis=0),
+                preferred_element_type=F32,
+            ) + jnp.dot(weights[-1], values[-1], preferred_element_type=F32)
             out = out / total
             level = top + jnp.log(total)
             for i in range(stack):
                 at = i * rows
                 columns = slice((head + i) * HD, (head + i + 1) * HD)
-                kept[:, columns] = out[at : at + keep]
-                send[:, columns] = out[at + keep : at + rows].astype(BF16)
+                outs[0][:, columns] = out[at : at + rows].astype(outs[0].dtype)
                 stats = jnp.where(lane == head + i, level[at : at + rows], stats)
-    kept_stats[...] = stats[:keep]
-    send[:, wide:] = split_stats(stats[keep:])
-
-
-def merge(heads, kept, kept_stats, got):
+    if message:
+        outs[0][:, wide:] = split_stats(stats)
+    else:
+        outs[1][...] = stats
+
+
+def merge(heads, kept, kept_stats, got, first, rows):
     wide = heads * GROUP * HD
-    mine = kept_stats[...]
-    theirs = joined_stats(got[:, wide:])
+    half = slice(first, first + rows)
+    mine = kept_stats[half, :]
+    theirs = joined_stats(got[half, wide:])
     top = jnp.maximum(mine, theirs)
     a = jnp.exp(mine - top)
     b = jnp.exp(theirs - top)
@@ -336,24 +338,25 @@
     for h in range(heads * GROUP):
         columns = slice(h * HD, (h + 1) * HD)
         merged.append(
-            kept[:, columns] * a[:, h : h + 1] + got[:, columns].astype(F32) * b[:, h : h + 1]
+            kept[half, columns] * a[:, h : h + 1]
+            + got[half, columns].astype(F32) * b[:, h : h + 1]
         )
     return merged, top + jnp.log(total)
 
 
-def merge_kernel(heads, keep, kept, kept_stats, got, send, out, out_stats):
+def merge_kernel(heads, first, kept, kept_stats, got, *outs):
     wide = heads * GROUP * HD
-    merged, stats = merge(heads, kept, kept_stats, got)
+    merged, stats = merge(heads, kept, kept_stats, got, first, kept.shape[0] // 2)
     for h, value in enumerate(merged):
-        columns = slice(h * HD, (h + 1) * HD)
-        out[:, columns] = value[:keep]
-        send[:, columns] = value[keep:].astype(BF16)
-    out_stats[...] = stats[:keep]
-    send[:, wide:] = split_stats(stats[keep:])
+        outs[0][:, h * HD : (h + 1) * HD] = value.astype(outs[0].dtype)
+    if len(outs) == 1:
+        outs[0][:, wide:] = split_stats(stats)
+    else:
+        outs[1][...] = stats
 
 
 def last_kernel(heads, kept, kept_stats, got, out, squares):
-    merged, _ = merge(heads, kept, kept_stats, got)
+    merged, _ = merge(heads, kept, kept_stats, got, 0, kept.shape[0])
     total = jnp.zeros_like(merged[0])
     for h, value in enumerate(merged):
         out[:, h * HD : (h + 1) * HD] = value
@@ -497,29 +500,43 @@
     )
     keep = rows // 2
     packed = q_width + HD
-    send, kept, stats = call(
-        functools.partial(attention_kernel, heads, rows, extras, keep),
-        "plane_attention",
+    given = (perm, allowed, state, other, k0, k1, k2, k3, cache_v, v1, v2, v3, extra)
+    limit = (16 if blocks <= 4 else 40) * 2**20
+    send = call(
+        functools.partial(attention_kernel, heads, keep, extras),
+        "sent_attention",
+        jax.ShapeDtypeStruct((keep, packed), BF16),
+        *given,
+        limit=limit,
+    )
+    kept, stats = call(
+        functools.partial(attention_kernel, heads, 0, extras),
+        "kept_attention",
         [
-            jax.ShapeDtypeStruct((keep, packed), BF16),
             jax.ShapeDtypeStruct((keep, q_width), F32),
             jax.ShapeDtypeStruct((keep, HD), F32),
         ],
-        perm, allowed, state, other, k0, k1, k2, k3, cache_v, v1, v2, v3, extra,
-        limit=(16 if blocks <= 4 else 40) * 2**20,
+        *given,
+        limit=limit,
     )
     for bit in bits[:0:-1]:
         got = exchange(send, "ctx", bit)
         keep = keep // 2
-        send, kept, stats = call(
+        given = (kept, stats, got)
+        send = call(
             functools.partial(merge_kernel, heads, keep),
-            "merge_partials",
+            "sent_partials",
+            jax.ShapeDtypeStruct((keep, packed), BF16),
+            *given,
+        )
+        kept, stats = call(
+            functools.partial(merge_kernel, heads, 0),
+            "kept_partials",
             [
-                jax.ShapeDtypeStruct((keep, packed), BF16),
                 jax.ShapeDtypeStruct((keep, q_width), F32),
                 jax.ShapeDtypeStruct((keep, HD), F32),
             ],
-            kept, stats, got,
+            *given,
         )
     got = exchange(send, "ctx", bits[0])
     att, squares = call(

time: 35.3 us -> 34.8 us (0.986)
  waiting for transfers between devices: 11.3 us -> 10.2 us
  Pallas kernels: 4.96 us -> 5.58 us
    ppermute x13, waiting for transfers between devices: 11.3 us -> 10.2 us  [exchange(): return lax.ppermute(value, axis, pairs)]
    pallas_call x11 -> x13, Pallas kernels: 4.96 us -> 5.58 us  [call(): pl.pallas_call(kernel, out_shape=out_shape, in_specs=in_specs, out_specs=...]
  transfers between devices with their start and end apart: 13 -> 13, of which waited for: 7 -> 7; matrix products, arithmetic and copies ran while one was open for 0% -> 0% of each run, Pallas kernels for 7% -> 10%
where the time goes in v5:
time: 34.8 us; the launch traced here: 34.6 us
  starting transfers between devices  17.1 us (49%)
  waiting for transfers between devices  10.2 us (29%)
  Pallas kernels  5.58 us (16%)
  local copies, waits for them, and re-layouts  0.9 us (3%)
  between operations  0.77 us (2%)
    ppermute x13, starting transfers between devices, exchange(): return lax.ppermute(value, axis, pairs)  17.1 us
    ppermute x13, waiting for transfers between devices, exchange(): return lax.ppermute(value, axis, pairs)  10.2 us
    pallas_call x13, Pallas kernels, call(): pl.pallas_call(kernel, out_shape=out_shape, in_specs=in_specs, out_specs=...  5.58 us
    unnamed x22, local copies, waits for them, and re-layouts  0.9 us
  transfers between devices with their start and end apart: 13, of which 7 were waited for; matrix products, arithmetic and copies ran while one was open for 0% of the time, Pallas kernels for 10%

profile of v5, /device:TPU:0, one launch (start us, length us, event | category | flops | bytes accessed | tf_op | source)
XLA Modules:
  0.0 34.6 jit_solution(7645765447401392789)
XLA Ops:
  0.6 2.5 %collective-permute-start = (bf16[4,2048]{1,0:T(4,128)(2,1)}, bf16[4,2048]{1,0:T(4,128)(2,1)S(1)}, u32[]{:S(2)}, u32[]{:S(2)}) collective-permute-start(bf16[4,2048]{1,0:T(4,128)(2,1)} %mine.1), channel_id=1, source_target_pairs={{0,6},{2,4},{4,2},{6,0},{8,14},{10,12},{12,10},{14,8},{16,22},{18,... | collective-permute-start | bytes 49160 | tf_op jit(solution)/shard_map/ppermute | solution.py:24
  3.2 1.9 %plane_values.1 = (bf16[288,512]{1,0:T(8,128)(2,1)}, bf16[32,512]{1,0:T(8,128)(2,1)}, f32[8,128]{1,0:T(8,128)}) custom-call(s32[1]{0:T(128)} %bitcast.place, s32[1,4]{1,0:T(1,128)} %bitcast.12, s32[1,32]{1,0:T(1,128)} %bitcast.7, s32[1,16]{1,0:T(1,128)} %bitcast.9, bf16[18,512]{1,0:T(8,128)(2,1)} %table_h.1, bf16[4,512]{1,0:T(4,128)(2,1)} %span_k_h.1, ...), custom_call_target="tpu_custom_call" | custom-call | flops 34500001792 | bytes 108000000 | tf_op jit(solution)/shard_map/plane_values/pallas_call | solution.py:43
  5.2 0.7 %collective-permute-start.1 = (bf16[8,2048]{1,0:T(8,128)(2,1)S(1)}, bf16[8,2048]{1,0:T(8,128)(2,1)S(1)}, u32[]{:S(2)}, u32[]{:S(2)}) collective-permute-start(bf16[8,2048]{1,0:T(8,128)(2,1)S(1)} %get-tuple-element.31.pair), channel_id=1, source_target_pairs={{0,2},{2,0},{4,6},{6,4},{8,10},{10,8},{12,14},{14,12},{16,18},{18,... | collective-permute-start | bytes 98312 | tf_op jit(solution)/shard_map/ppermute | solution.py:24
  6.1 0.5 %copy-done.6 = s32[32]{0:T(128)S(1)} copy-done((s32[32]{0:T(128)S(1)}, s32[32]{0:T(128)}, u32[]{:S(2)}) %copy-start.6) | copy-done | bytes 152
  6.8 0.2 column_queries.1.mine
  7.0 2.8 %collective-permute-start.2 = (bf16[16,2048]{1,0:T(8,128)(2,1)S(1)}, bf16[16,2048]{1,0:T(8,128)(2,1)S(1)}, u32[]{:S(2)}, u32[]{:S(2)}) collective-permute-start(bf16[16,2048]{1,0:T(8,128)(2,1)S(1)} %column_queries.1.mine), channel_id=1, source_target_pairs={{0,18},{2,16},{4,22},{6,20},{8,26},{10,24},{12,30},{14,28},{16,2},... | collective-permute-start | bytes 196616 | tf_op jit(solution)/shard_map/ppermute | solution.py:24
  9.8 1.5 %collective-permute-start.6 = (bf16[288,512]{1,0:T(8,128)(2,1)S(1)}, bf16[288,512]{1,0:T(8,128)(2,1)S(1)}, u32[]{:S(2)}, u32[]{:S(2)}) collective-permute-start(bf16[288,512]{1,0:T(8,128)(2,1)S(1)} %copy-done.10), channel_id=1, source_target_pairs={{0,6},{2,4},{4,2},{6,0},{8,14},{10,12},{12,10},{14,8},{16,22},{18,... | collective-permute-start | bytes 884744 | tf_op jit(solution)/shard_map/ppermute | solution.py:24
  11.3 0.7 %collective-permute-done.2.other = bf16[16,2048]{1,0:T(8,128)(2,1)S(1)} collective-permute-done((bf16[16,2048]{1,0:T(8,128)(2,1)S(1)}, bf16[16,2048]{1,0:T(8,128)(2,1)S(1)}, u32[]{:S(2)}, u32[]{:S(2)}) %collective-permute-start.2) | collective-permute-done | bytes 65568 | tf_op jit(solution)/shard_map/ppermute | solution.py:24
  12.1 1.8 %collective-permute-start.7 = (bf16[256,512]{1,0:T(8,128)(2,1)S(1)}, bf16[256,512]{1,0:T(8,128)(2,1)S(1)}, u32[]{:S(2)}, u32[]{:S(2)}) collective-permute-start(bf16[256,512]{1,0:T(8,128)(2,1)S(1)} %get-tuple-element.35.k3), channel_id=1, source_target_pairs={{0,2},{2,0},{4,6},{6,4},{8,10},{10,8},{12,14},{14,12},{16,18},{18,... | collective-permute-start | bytes 786440 | tf_op jit(solution)/shard_map/ppermute | solution.py:24
  13.8 1.3 %collective-permute-start.5 = (bf16[20,2048]{1,0:T(8,128)(2,1)S(1)}, bf16[20,2048]{1,0:T(8,128)(2,1)S(1)}, u32[]{:S(2)}, u32[]{:S(2)}) collective-permute-start(bf16[20,2048]{1,0:T(8,128)(2,1)S(1)} %get-tuple-element.33.mine), channel_id=1, source_target_pairs={{0,10},{2,8},{4,14},{6,12},{8,2},{10,0},{12,6},{14,4},{16,26},{18,... | collective-permute-start | bytes 245768 | tf_op jit(solution)/shard_map/ppermute | solution.py:24
  15.2 3.5 %collective-permute-done.6.__1_ = bf16[288,512]{1,0:T(8,128)(2,1)S(1)} collective-permute-done((bf16[288,512]{1,0:T(8,128)(2,1)S(1)}, bf16[288,512]{1,0:T(8,128)(2,1)S(1)}, u32[]{:S(2)}, u32[]{:S(2)}) %collective-permute-start.6) | collective-permute-done | bytes 294944 | tf_op jit(solution)/shard_map/ppermute | solution.py:24
  18.7 0.4 %collective-permute-start.9 = (bf16[288,512]{1,0:T(8,128)(2,1)S(1)}, bf16[288,512]{1,0:T(8,128)(2,1)S(1)}, u32[]{:S(2)}, u32[]{:S(2)}) collective-permute-start(bf16[288,512]{1,0:T(8,128)(2,1)S(1)} %get-tuple-element.39.v3), channel_id=1, source_target_pairs={{0,2},{2,0},{4,6},{6,4},{8,10},{10,8},{12,14},{14,12},{16,18},{18,... | collective-permute-start | bytes 884744 | tf_op jit(solution)/shard_map/ppermute | solution.py:24
  19.1 0.3 copy-done.8
  19.5 0.8 %collective-permute-done.9.v2 = bf16[288,512]{1,0:T(8,128)(2,1)S(1)} collective-permute-done((bf16[288,512]{1,0:T(8,128)(2,1)S(1)}, bf16[288,512]{1,0:T(8,128)(2,1)S(1)}, u32[]{:S(2)}, u32[]{:S(2)}) %collective-permute-start.9) | collective-permute-done | bytes 294944 | tf_op jit(solution)/shard_map/ppermute | solution.py:24
  20.4 0.9 %sent_attention.1 = bf16[16,2176]{1,0:T(8,128)(2,1)S(1)} custom-call(bf16[32,40]{1,0:T(8,128)(2,1)S(1)} %get-tuple-element.25.perm, f32[32,64]{1,0:T(8,128)S(1)} %get-tuple-element.26.allowed, bf16[20,2048]{1,0:T(8,128)(2,1)S(1)} %get-tuple-element.33.mine, bf16[20,2048]{1,0:T(8,128)(2,1)S(1)} %get-tuple-element.36.other, ...), custom_call_target="tpu_custom_call" | custom-call | tf_op jit(solution)/shard_map/sent_attention/pallas_call | solution.py:43
  21.3 1.5 %collective-permute-start.10 = (bf16[16,2176]{1,0:T(8,128)(2,1)S(1)}, bf16[16,2176]{1,0:T(8,128)(2,1)S(1)}, u32[]{:S(2)}, u32[]{:S(2)}) collective-permute-start(bf16[16,2176]{1,0:T(8,128)(2,1)S(1)} %sent_attention.1), channel_id=1, source_target_pairs={{0,10},{2,8},{4,14},{6,12},{8,2},{10,0},{12,6},{14,4},{16,26},{18,... | collective-permute-start | bytes 208904 | tf_op jit(solution)/shard_map/ppermute | solution.py:24
  22.8 0.9 %kept_attention.1 = (f32[16,2048]{1,0:T(8,128)S(1)}, f32[16,128]{1,0:T(8,128)S(1)}) custom-call(bf16[32,40]{1,0:T(8,128)(2,1)S(1)} %get-tuple-element.25.perm, f32[32,64]{1,0:T(8,128)S(1)} %get-tuple-element.26.allowed, bf16[20,2048]{1,0:T(8,128)(2,1)S(1)} %get-tuple-element.33.mine, bf16[20,2048]{1,0:T(8,128)(2,1)S(1)} %get-tuple-element.36.other, ...), custom_call_target="tpu_custom_call" | custom-call | tf_op jit(solution)/shard_map/kept_attention/pallas_call | solution.py:43
  23.7 1.7 %collective-permute-done.10.got = bf16[16,2176]{1,0:T(8,128)(2,1)S(1)} collective-permute-done((bf16[16,2176]{1,0:T(8,128)(2,1)S(1)}, bf16[16,2176]{1,0:T(8,128)(2,1)S(1)}, u32[]{:S(2)}, u32[]{:S(2)}) %collective-permute-start.10) | collective-permute-done | bytes 69664 | tf_op jit(solution)/shard_map/ppermute | solution.py:24
  25.7 2.7 %collective-permute-start.11 = (bf16[8,2176]{1,0:T(8,128)(2,1)S(1)}, bf16[8,2176]{1,0:T(8,128)(2,1)S(1)}, u32[]{:S(2)}, u32[]{:S(2)}) collective-permute-start(bf16[8,2176]{1,0:T(8,128)(2,1)S(1)} %sent_partials.1), channel_id=1, source_target_pairs={{0,18},{2,16},{4,22},{6,20},{8,26},{10,24},{12,30},{14,28},{16,2},... | collective-permute-start | bytes 104456 | tf_op jit(solution)/shard_map/ppermute | solution.py:24
  28.5 1.5 %collective-permute-done.11.got = bf16[8,2176]{1,0:T(8,128)(2,1)S(1)} collective-permute-done((bf16[8,2176]{1,0:T(8,128)(2,1)S(1)}, bf16[8,2176]{1,0:T(8,128)(2,1)S(1)}, u32[]{:S(2)}, u32[]{:S(2)}) %collective-permute-start.11) | collective-permute-done | bytes 34848 | tf_op jit(solution)/shard_map/ppermute | solution.py:24
  30.0 0.3 merge_last.1
  30.3 1.8 %collective-permute-start.12 = (f32[8,128]{1,0:T(8,128)S(1)}, f32[8,128]{1,0:T(8,128)S(1)}, u32[]{:S(2)}, u32[]{:S(2)}) collective-permute-start(f32[8,128]{1,0:T(8,128)S(1)} %get-tuple-element.46.squares), channel_id=1, source_target_pairs={{0,1},{1,0},{2,3},{3,2},{4,5},{5,4},{6,7},{7,6},{8,9},{9,8},{10,11... | collective-permute-start | bytes 12296 | tf_op jit(solution)/shard_map/ppermute | solution.py:24
  32.1 1.8 %collective-permute-done.12.other = f32[8,128]{1,0:T(8,128)S(1)} collective-permute-done((f32[8,128]{1,0:T(8,128)S(1)}, f32[8,128]{1,0:T(8,128)S(1)}, u32[]{:S(2)}, u32[]{:S(2)}) %collective-permute-start.12) | collective-permute-done | bytes 4128 | tf_op jit(solution)/shard_map/ppermute | solution.py:24
  33.9 0.7 %normalize.1 = (bf16[4,2048]{1,0:T(4,128)(2,1)}, bf16[2,2048]{1,0:T(2,128)(2,1)}, bf16[1,2048]{1,0:T(2,128)(2,1)}) custom-call(f32[8,2048]{1,0:T(8,128)S(1)} %get-tuple-element.45.att, f32[8,128]{1,0:T(8,128)S(1)} %get-tuple-element.46.squares, f32[8,128]{1,0:T(8,128)S(1)} %collective-permute-done.12.other, f32[1,2048]{1,0:T(1,128)S(1)} %bitcast.6), custom_call_target="tpu_custom_call" | custom-call | tf_op jit(solution)/shard_map/normalize/pallas_call | solution.py:43
  (37 shorter events, 1.1 us)
Async XLA Ops:
  0.6 4.5 %collective-permute-start = (bf16[4,2048]{1,0:T(4,128)(2,1)}, bf16[4,2048]{1,0:T(4,128)(2,1)S(1)}, u32[]{:S(2)}, u32[]{:S(2)}) collective-permute-start(bf16[4,2048]{1,0:T(4,128)(2,1)} %mine.1), channel_id=1, source_target_pairs={{0,6},{2,4},{4,2},{6,0},{8,14},{10,12},{12,10},{14,8},{16,22},{18,... | collective-permute-start | bytes 49160 | tf_op jit(solution)/shard_map/ppermute | solution.py:24
  3.1 8.9 %collective-permute-start.3 = (bf16[256,512]{1,0:T(8,128)(2,1)}, bf16[256,512]{1,0:T(8,128)(2,1)S(1)}, u32[]{:S(2)}, u32[]{:S(2)}) collective-permute-start(bf16[256,512]{1,0:T(8,128)(2,1)} %cached.1), channel_id=1, source_target_pairs={{0,6},{2,4},{4,2},{6,0},{8,14},{10,12},{12,10},{14,8},{16,22},{18,... | collective-permute-start | bytes 786440 | tf_op jit(solution)/shard_map/ppermute | solution.py:24
  3.2 2.0 %copy-start.1 = (bf16[256,512]{1,0:T(8,128)(2,1)S(1)}, bf16[256,512]{1,0:T(8,128)(2,1)}, u32[]{:S(2)}) copy-start(bf16[256,512]{1,0:T(8,128)(2,1)} %cached.1) | copy-start | bytes 786436
  3.2 2.0 %copy-start.3 = (bf16[4,2048]{1,0:T(4,128)(2,1)S(1)}, bf16[4,2048]{1,0:T(4,128)(2,1)}, u32[]{:S(2)}) copy-start(bf16[4,2048]{1,0:T(4,128)(2,1)} %spans.1) | copy-start | bytes 49156
  3.2 2.0 %copy-start.4 = (bf16[4,2048]{1,0:T(4,128)(2,1)S(1)}, bf16[4,2048]{1,0:T(4,128)(2,1)}, u32[]{:S(2)}) copy-start(bf16[4,2048]{1,0:T(4,128)(2,1)} %mine.1) | copy-start | bytes 49156
  5.2 0.9 %copy-start.9 = (f32[8,128]{1,0:T(8,128)S(1)}, f32[8,128]{1,0:T(8,128)}, u32[]{:S(2)}) copy-start(f32[8,128]{1,0:T(8,128)} %get-tuple-element.27._) | copy-start | bytes 12292
  5.2 1.6 %collective-permute-start.1 = (bf16[8,2048]{1,0:T(8,128)(2,1)S(1)}, bf16[8,2048]{1,0:T(8,128)(2,1)S(1)}, u32[]{:S(2)}, u32[]{:S(2)}) collective-permute-start(bf16[8,2048]{1,0:T(8,128)(2,1)S(1)} %get-tuple-element.31.pair), channel_id=1, source_target_pairs={{0,2},{2,0},{4,6},{6,4},{8,10},{10,8},{12,14},{14,12},{16,18},{18,... | collective-permute-start | bytes 98312 | tf_op jit(solution)/shard_map/ppermute | solution.py:24
  6.0 0.7 %copy-start.6 = (s32[32]{0:T(128)S(1)}, s32[32]{0:T(128)}, u32[]{:S(2)}) copy-start(s32[32]{0:T(128)} %param.33) | copy-start | bytes 388
  6.0 0.7 %copy-start.7 = (s32[16]{0:T(128)S(1)}, s32[16]{0:T(128)}, u32[]{:S(2)}) copy-start(s32[16]{0:T(128)} %param.34) | copy-start | bytes 196
  6.0 6.1 %collective-permute-start.4 = (bf16[256,512]{1,0:T(8,128)(2,1)S(1)}, bf16[256,512]{1,0:T(8,128)(2,1)S(1)}, u32[]{:S(2)}, u32[]{:S(2)}) collective-permute-start(bf16[256,512]{1,0:T(8,128)(2,1)S(1)} %get-tuple-element.32.k0), channel_id=1, source_target_pairs={{0,2},{2,0},{4,6},{6,4},{8,10},{10,8},{12,14},{14,12},{16,18},{18,... | collective-permute-start | bytes 786440 | tf_op jit(solution)/shard_map/ppermute | solution.py:24
  6.6 3.2 %copy-start.10 = (bf16[288,512]{1,0:T(8,128)(2,1)S(1)}, bf16[288,512]{1,0:T(8,128)(2,1)}, u32[]{:S(2)}) copy-start(bf16[288,512]{1,0:T(8,128)(2,1)} %get-tuple-element.34) | copy-start | bytes 884740
  7.0 5.0 %collective-permute-start.2 = (bf16[16,2048]{1,0:T(8,128)(2,1)S(1)}, bf16[16,2048]{1,0:T(8,128)(2,1)S(1)}, u32[]{:S(2)}, u32[]{:S(2)}) collective-permute-start(bf16[16,2048]{1,0:T(8,128)(2,1)S(1)} %column_queries.1.mine), channel_id=1, source_target_pairs={{0,18},{2,16},{4,22},{6,20},{8,26},{10,24},{12,30},{14,28},{16,2},... | collective-permute-start | bytes 196616 | tf_op jit(solution)/shard_map/ppermute | solution.py:24
  9.8 8.8 %collective-permute-start.6 = (bf16[288,512]{1,0:T(8,128)(2,1)S(1)}, bf16[288,512]{1,0:T(8,128)(2,1)S(1)}, u32[]{:S(2)}, u32[]{:S(2)}) collective-permute-start(bf16[288,512]{1,0:T(8,128)(2,1)S(1)} %copy-done.10), channel_id=1, source_target_pairs={{0,6},{2,4},{4,2},{6,0},{8,14},{10,12},{12,10},{14,8},{16,22},{18,... | collective-permute-start | bytes 884744 | tf_op jit(solution)/shard_map/ppermute | solution.py:24
  12.1 6.6 %collective-permute-start.7 = (bf16[256,512]{1,0:T(8,128)(2,1)S(1)}, bf16[256,512]{1,0:T(8,128)(2,1)S(1)}, u32[]{:S(2)}, u32[]{:S(2)}) collective-permute-start(bf16[256,512]{1,0:T(8,128)(2,1)S(1)} %get-tuple-element.35.k3), channel_id=1, source_target_pairs={{0,2},{2,0},{4,6},{6,4},{8,10},{10,8},{12,14},{14,12},{16,18},{18,... | collective-permute-start | bytes 786440 | tf_op jit(solution)/shard_map/ppermute | solution.py:24
  13.8 6.5 %copy-start = (bf16[256,512]{1,0:T(8,128)(2,1)S(1)}, bf16[256,512]{1,0:T(8,128)(2,1)}, u32[]{:S(2)}) copy-start(bf16[256,512]{1,0:T(8,128)(2,1)} %v0.3) | copy-start | bytes 786436
  13.8 4.9 %collective-permute-start.5 = (bf16[20,2048]{1,0:T(8,128)(2,1)S(1)}, bf16[20,2048]{1,0:T(8,128)(2,1)S(1)}, u32[]{:S(2)}, u32[]{:S(2)}) collective-permute-start(bf16[20,2048]{1,0:T(8,128)(2,1)S(1)} %get-tuple-element.33.mine), channel_id=1, source_target_pairs={{0,10},{2,8},{4,14},{6,12},{8,2},{10,0},{12,6},{14,4},{16,26},{18,... | collective-permute-start | bytes 245768 | tf_op jit(solution)/shard_map/ppermute | solution.py:24
  15.1 4.4 %collective-permute-start.8 = (bf16[288,512]{1,0:T(8,128)(2,1)S(1)}, bf16[288,512]{1,0:T(8,128)(2,1)S(1)}, u32[]{:S(2)}, u32[]{:S(2)}) collective-permute-start(bf16[288,512]{1,0:T(8,128)(2,1)S(1)} %copy-done.10), channel_id=1, source_target_pairs={{0,2},{2,0},{4,6},{6,4},{8,10},{10,8},{12,14},{14,12},{16,18},{18,... | collective-permute-start | bytes 884744 | tf_op jit(solution)/shard_map/ppermute | solution.py:24
  18.7 1.7 %copy-start.2 = (bf16[32,512]{1,0:T(8,128)(2,1)S(1)}, bf16[32,512]{1,0:T(8,128)(2,1)}, u32[]{:S(2)}) copy-start(bf16[32,512]{1,0:T(8,128)(2,1)} %get-tuple-element.40.extra) | copy-start | bytes 98308
  18.7 0.7 %copy-start.8 = (s32[64]{0:T(128)S(1)}, s32[64]{0:T(128)}, u32[]{:S(2)}) copy-start(s32[64]{0:T(128)} %param.23) | copy-start | bytes 772
  18.7 1.6 %collective-permute-start.9 = (bf16[288,512]{1,0:T(8,128)(2,1)S(1)}, bf16[288,512]{1,0:T(8,128)(2,1)S(1)}, u32[]{:S(2)}, u32[]{:S(2)}) collective-permute-start(bf16[288,512]{1,0:T(8,128)(2,1)S(1)} %get-tuple-element.39.v3), channel_id=1, source_target_pairs={{0,2},{2,0},{4,6},{6,4},{8,10},{10,8},{12,14},{14,12},{16,18},{18,... | collective-permute-start | bytes 884744 | tf_op jit(solution)/shard_map/ppermute | solution.py:24
  21.3 4.1 %collective-permute-start.10 = (bf16[16,2176]{1,0:T(8,128)(2,1)S(1)}, bf16[16,2176]{1,0:T(8,128)(2,1)S(1)}, u32[]{:S(2)}, u32[]{:S(2)}) collective-permute-start(bf16[16,2176]{1,0:T(8,128)(2,1)S(1)} %sent_attention.1), channel_id=1, source_target_pairs={{0,10},{2,8},{4,14},{6,12},{8,2},{10,0},{12,6},{14,4},{16,26},{18,... | collective-permute-start | bytes 208904 | tf_op jit(solution)/shard_map/ppermute | solution.py:24
  25.7 4.3 %collective-permute-start.11 = (bf16[8,2176]{1,0:T(8,128)(2,1)S(1)}, bf16[8,2176]{1,0:T(8,128)(2,1)S(1)}, u32[]{:S(2)}, u32[]{:S(2)}) collective-permute-start(bf16[8,2176]{1,0:T(8,128)(2,1)S(1)} %sent_partials.1), channel_id=1, source_target_pairs={{0,18},{2,16},{4,22},{6,20},{8,26},{10,24},{12,30},{14,28},{16,2},... | collective-permute-start | bytes 104456 | tf_op jit(solution)/shard_map/ppermute | solution.py:24
  30.0 3.9 %copy-start.5 = (f32[2048]{0:T(1024)S(1)}, f32[2048]{0:T(1024)}, u32[]{:S(2)}) copy-start(f32[2048]{0:T(1024)} %param.35) | copy-start | bytes 24580
  30.3 3.6 %collective-permute-start.12 = (f32[8,128]{1,0:T(8,128)S(1)}, f32[8,128]{1,0:T(8,128)S(1)}, u32[]{:S(2)}, u32[]{:S(2)}) collective-permute-start(f32[8,128]{1,0:T(8,128)S(1)} %get-tuple-element.46.squares), channel_id=1, source_target_pairs={{0,1},{1,0},{2,3},{3,2},{4,5},{5,4},{6,7},{7,6},{8,9},{9,8},{10,11... | collective-permute-start | bytes 12296 | tf_op jit(solution)/shard_map/ppermute | solution.py:24

commit v6 on v5

--- a/solution.py
+++ b/solution.py
@@ -122,9 +122,7 @@
             jnp.where(second, token, jnp.where(first, revealed[...].astype(F32), frame))
         )
     sets += shown
-    half = extra.shape[0] // 2
-    rest = jnp.zeros((half - 3 * spans, extra.shape[1]), F32)
-    parts = jnp.concatenate([*sets[0::2], rest, *sets[1::2], rest], axis=0).astype(BF16)
+    parts = jnp.concatenate([*sets[0::2], *sets[1::2]], axis=0).astype(BF16)
     extra[...] = parts
     values[cached:, :] = parts
     done[...] = jnp.zeros(done.shape, F32)
@@ -230,9 +228,18 @@
 def grow_kernel(spans, mine, other, _, __, out, *___):
     a = mine[...].astype(F32)
     b = other[...].astype(F32)
-    out[...] = jnp.concatenate(
-        [a[:spans], b[:spans], a[spans:] + b[spans:]], axis=0
-    ).astype(BF16)
+    parts = [a[:spans], b[:spans], a[spans:] + b[spans:]]
+    width = out.shape[1]
+    pieces = [p[:, at : at + width] for at in range(0, a.shape[1], width) for p in parts]
+    out[...] = jnp.concatenate(pieces, axis=0).astype(BF16)
+
+
+def unfolded(state, width):
+    state = state[...].astype(F32)
+    count = state.shape[0] * state.shape[1] // width
+    return jnp.concatenate(
+        [state[at : at + count] for at in range(0, state.shape[0], count)], axis=1
+    )
 
 
 def split_stats(stats):
@@ -251,16 +258,19 @@
     return packed + pltpu.roll(packed, 112, 1) + pltpu.roll(packed, 96, 1)
 
 
+def queries_kernel(perm, mine, other, out):
+    given = stacked([unfolded(state, out.shape[1]) for state in (mine, other)])
+    out[...] = jnp.dot(perm[...], given, preferred_element_type=F32).astype(BF16)
+
+
 def attention_kernel(
     heads, first_row, extras,
-    perm, allowed, mine, other, k0, k1, k2, k3, v0, v1, v2, v3, extra, *outs,
+    picked, allowed, k0, k1, k2, k3, v0, v1, v2, v3, extra, *outs,
 ):
-    rows = perm.shape[0] // 2
+    rows = picked.shape[0] // 2
     half = slice(first_row, first_row + rows)
     message = len(outs) == 1
-    queries = jnp.dot(
-        perm[half, :], stacked([mine[...], other[...]]), preferred_element_type=F32
-    ).astype(BF16)
+    queries = picked[half, :]
     wide = heads * GROUP * HD
     scaling = HD ** (-0.5)
     cached = k0.shape[0]
@@ -411,7 +421,7 @@
     bits = [(1 << b) + 1 for b in range(2, owners.bit_length() - 1)][::-1]
 
     depth = (blocks // 2) * spans + blocks * picked
-    extras = -(-3 * spans // 16) * 16
+    extras = 3 * spans
 
     q3 = exchange(frame_q, "ctx", 3)
     small = (
@@ -469,12 +479,15 @@
 
     held = spans
     for bit in bits[:-1]:
+        fold = 2 if bit == bits[-2] and (state.shape[0] + held) % 8 else 1
         other = exchange(state, "ctx", bit)
         state, k3, k1 = call(
             functools.partial(grow_kernel, held),
             "more_queries",
             [
-                jax.ShapeDtypeStruct((state.shape[0] + held, q_width), BF16),
+                jax.ShapeDtypeStruct(
+                    (fold * (state.shape[0] + held), q_width // fold), BF16
+                ),
                 jax.ShapeDtypeStruct(k3.shape, BF16),
                 jax.ShapeDtypeStruct(k1.shape, BF16),
             ],
@@ -500,7 +513,13 @@
     )
     keep = rows // 2
     packed = q_width + HD
-    given = (perm, allowed, state, other, k0, k1, k2, k3, cache_v, v1, v2, v3, extra)
+    queries = call(
+        queries_kernel,
+        "ordered_queries",
+        jax.ShapeDtypeStruct((rows, q_width), BF16),
+        perm, state, other,
+    )
+    given = (queries, allowed, k0, k1, k2, k3, cache_v, v1, v2, v3, extra)
     limit = (16 if blocks <= 4 else 40) * 2**20
     send = call(
         functools.partial(attention_kernel, heads, keep, extras),

time: 34.8 us -> 34.4 us (0.989)
  waiting for transfers between devices: 10.2 us -> 10.6 us
    ppermute x13, starting transfers between devices: 17.1 us -> 16.8 us  [exchange(): return lax.ppermute(value, axis, pairs)]
    ppermute x13, waiting for transfers between devices: 10.2 us -> 10.6 us  [exchange(): return lax.ppermute(value, axis, pairs)]
    pallas_call x13 -> x14, Pallas kernels: 5.58 us -> 5.57 us  [call(): pl.pallas_call(kernel, out_shape=out_shape, in_specs=in_specs, out_specs=...]
where the time goes in v6:
time: 34.4 us; the launch traced here: 34.3 us
  starting transfers between devices  16.8 us (49%)
  waiting for transfers between devices  10.6 us (31%)
  Pallas kernels  5.57 us (16%)
  between operations  0.77 us (2%)
  local copies, waits for them, and re-layouts  0.6 us (2%)
    ppermute x13, starting transfers between devices, exchange(): return lax.ppermute(value, axis, pairs)  16.8 us
    ppermute x13, waiting for transfers between devices, exchange(): return lax.ppermute(value, axis, pairs)  10.6 us
    pallas_call x14, Pallas kernels, call(): pl.pallas_call(kernel, out_shape=out_shape, in_specs=in_specs, out_specs=...  5.57 us
  transfers between devices with their start and end apart: 13, of which 7 were waited for; matrix products, arithmetic and copies ran while one was open for 0% of the time, Pallas kernels for 10%

profile of v6, /device:TPU:0, one launch (start us, length us, event | category | flops | bytes accessed | tf_op | source)
XLA Modules:
  0.0 34.3 jit_solution(4191477296237730560)
XLA Ops:
  0.6 2.5 %collective-permute-start = (bf16[4,2048]{1,0:T(4,128)(2,1)}, bf16[4,2048]{1,0:T(4,128)(2,1)S(1)}, u32[]{:S(2)}, u32[]{:S(2)}) collective-permute-start(bf16[4,2048]{1,0:T(4,128)(2,1)} %mine.1), channel_id=1, source_target_pairs={{0,6},{2,4},{4,2},{6,0},{8,14},{10,12},{12,10},{14,8},{16,22},{18,... | collective-permute-start | bytes 49160 | tf_op jit(solution)/shard_map/ppermute | solution.py:24
  3.2 1.9 %plane_values.1 = (bf16[280,512]{1,0:T(8,128)(2,1)}, bf16[24,512]{1,0:T(8,128)(2,1)}, f32[8,128]{1,0:T(8,128)}) custom-call(s32[1]{0:T(128)} %bitcast.place, s32[1,4]{1,0:T(1,128)} %bitcast.12, s32[1,32]{1,0:T(1,128)} %bitcast.7, s32[1,16]{1,0:T(1,128)} %bitcast.9, bf16[18,512]{1,0:T(8,128)(2,1)} %table_h.1, bf16[4,512]{1,0:T(4,128)(2,1)} %span_k_h.1, ...), custom_call_target="tpu_custom_call" | custom-call | flops 34500001792 | bytes 108000000 | tf_op jit(solution)/shard_map/plane_values/pallas_call | solution.py:43
  5.2 0.7 %collective-permute-start.1 = (bf16[8,2048]{1,0:T(8,128)(2,1)S(1)}, bf16[8,2048]{1,0:T(8,128)(2,1)S(1)}, u32[]{:S(2)}, u32[]{:S(2)}) collective-permute-start(bf16[8,2048]{1,0:T(8,128)(2,1)S(1)} %get-tuple-element.30.pair), channel_id=1, source_target_pairs={{0,2},{2,0},{4,6},{6,4},{8,10},{10,8},{12,14},{14,12},{16,18},{18,... | collective-permute-start | bytes 98312 | tf_op jit(solution)/shard_map/ppermute | solution.py:24
  6.1 0.5 %copy-done.6 = s32[32]{0:T(128)S(1)} copy-done((s32[32]{0:T(128)S(1)}, s32[32]{0:T(128)}, u32[]{:S(2)}) %copy-start.6) | copy-done | bytes 152
  6.8 0.2 column_queries.1.mine
  7.0 2.8 %collective-permute-start.2 = (bf16[16,2048]{1,0:T(8,128)(2,1)S(1)}, bf16[16,2048]{1,0:T(8,128)(2,1)S(1)}, u32[]{:S(2)}, u32[]{:S(2)}) collective-permute-start(bf16[16,2048]{1,0:T(8,128)(2,1)S(1)} %column_queries.1.mine), channel_id=1, source_target_pairs={{0,18},{2,16},{4,22},{6,20},{8,26},{10,24},{12,30},{14,28},{16,2},... | collective-permute-start | bytes 196616 | tf_op jit(solution)/shard_map/ppermute | solution.py:24
  9.8 1.5 %collective-permute-start.6 = (bf16[280,512]{1,0:T(8,128)(2,1)S(1)}, bf16[280,512]{1,0:T(8,128)(2,1)S(1)}, u32[]{:S(2)}, u32[]{:S(2)}) collective-permute-start(bf16[280,512]{1,0:T(8,128)(2,1)S(1)} %copy-done.10), channel_id=1, source_target_pairs={{0,6},{2,4},{4,2},{6,0},{8,14},{10,12},{12,10},{14,8},{16,22},{18,... | collective-permute-start | bytes 860168 | tf_op jit(solution)/shard_map/ppermute | solution.py:24
  11.3 0.7 %collective-permute-done.2.other = bf16[16,2048]{1,0:T(8,128)(2,1)S(1)} collective-permute-done((bf16[16,2048]{1,0:T(8,128)(2,1)S(1)}, bf16[16,2048]{1,0:T(8,128)(2,1)S(1)}, u32[]{:S(2)}, u32[]{:S(2)}) %collective-permute-start.2) | collective-permute-done | bytes 65568 | tf_op jit(solution)/shard_map/ppermute | solution.py:24
  12.1 1.8 %collective-permute-start.7 = (bf16[256,512]{1,0:T(8,128)(2,1)S(1)}, bf16[256,512]{1,0:T(8,128)(2,1)S(1)}, u32[]{:S(2)}, u32[]{:S(2)}) collective-permute-start(bf16[256,512]{1,0:T(8,128)(2,1)S(1)} %get-tuple-element.34.k3), channel_id=1, source_target_pairs={{0,2},{2,0},{4,6},{6,4},{8,10},{10,8},{12,14},{14,12},{16,18},{18,... | collective-permute-start | bytes 786440 | tf_op jit(solution)/shard_map/ppermute | solution.py:24
  13.8 1.3 %collective-permute-start.5 = (bf16[40,1024]{1,0:T(8,128)(2,1)S(1)}, bf16[40,1024]{1,0:T(8,128)(2,1)S(1)}, u32[]{:S(2)}, u32[]{:S(2)}) collective-permute-start(bf16[40,1024]{1,0:T(8,128)(2,1)S(1)} %get-tuple-element.32.mine), channel_id=1, source_target_pairs={{0,10},{2,8},{4,14},{6,12},{8,2},{10,0},{12,6},{14,4},{16,26},{18,... | collective-permute-start | bytes 245768 | tf_op jit(solution)/shard_map/ppermute | solution.py:24
  15.2 3.3 %collective-permute-done.6.__1_ = bf16[280,512]{1,0:T(8,128)(2,1)S(1)} collective-permute-done((bf16[280,512]{1,0:T(8,128)(2,1)S(1)}, bf16[280,512]{1,0:T(8,128)(2,1)S(1)}, u32[]{:S(2)}, u32[]{:S(2)}) %collective-permute-start.6) | collective-permute-done | bytes 286752 | tf_op jit(solution)/shard_map/ppermute | solution.py:24
  18.5 0.4 %collective-permute-start.9 = (bf16[280,512]{1,0:T(8,128)(2,1)S(1)}, bf16[280,512]{1,0:T(8,128)(2,1)S(1)}, u32[]{:S(2)}, u32[]{:S(2)}) collective-permute-start(bf16[280,512]{1,0:T(8,128)(2,1)S(1)} %get-tuple-element.39.v3), channel_id=1, source_target_pairs={{0,2},{2,0},{4,6},{6,4},{8,10},{10,8},{12,14},{14,12},{16,18},{18,... | collective-permute-start | bytes 860168 | tf_op jit(solution)/shard_map/ppermute | solution.py:24
  19.2 0.9 %collective-permute-done.9.v2 = bf16[280,512]{1,0:T(8,128)(2,1)S(1)} collective-permute-done((bf16[280,512]{1,0:T(8,128)(2,1)S(1)}, bf16[280,512]{1,0:T(8,128)(2,1)S(1)}, u32[]{:S(2)}, u32[]{:S(2)}) %collective-permute-start.9) | collective-permute-done | bytes 286752 | tf_op jit(solution)/shard_map/ppermute | solution.py:24
  20.2 0.8 %sent_attention.1 = bf16[16,2176]{1,0:T(8,128)(2,1)S(1)} custom-call(bf16[32,2048]{1,0:T(8,128)(2,1)S(1)} %ordered_queries.1.picked, f32[32,48]{1,0:T(8,128)S(1)} %get-tuple-element.36.allowed, bf16[256,512]{1,0:T(8,128)(2,1)S(1)} %get-tuple-element.31.k0, bf16[256,512]{1,0:T(8,128)(2,1)S(1)} %get-tuple-element.37.k1, ...), custom_call_target="tpu_custom_call" | custom-call | tf_op jit(solution)/shard_map/sent_attention/pallas_call | solution.py:43
  21.0 1.5 %collective-permute-start.10 = (bf16[16,2176]{1,0:T(8,128)(2,1)S(1)}, bf16[16,2176]{1,0:T(8,128)(2,1)S(1)}, u32[]{:S(2)}, u32[]{:S(2)}) collective-permute-start(bf16[16,2176]{1,0:T(8,128)(2,1)S(1)} %sent_attention.1), channel_id=1, source_target_pairs={{0,10},{2,8},{4,14},{6,12},{8,2},{10,0},{12,6},{14,4},{16,26},{18,... | collective-permute-start | bytes 208904 | tf_op jit(solution)/shard_map/ppermute | solution.py:24
  22.5 0.8 %kept_attention.1 = (f32[16,2048]{1,0:T(8,128)S(1)}, f32[16,128]{1,0:T(8,128)S(1)}) custom-call(bf16[32,2048]{1,0:T(8,128)(2,1)S(1)} %ordered_queries.1.picked, f32[32,48]{1,0:T(8,128)S(1)} %get-tuple-element.36.allowed, bf16[256,512]{1,0:T(8,128)(2,1)S(1)} %get-tuple-element.31.k0, bf16[256,512]{1,0:T(8,128)(2,1)S(1)} %get-tuple-element.37.k1, ...), custom_call_target="tpu_custom_call" | custom-call | tf_op jit(solution)/shard_map/kept_attention/pallas_call | solution.py:43
  23.4 1.8 %collective-permute-done.10.got = bf16[16,2176]{1,0:T(8,128)(2,1)S(1)} collective-permute-done((bf16[16,2176]{1,0:T(8,128)(2,1)S(1)}, bf16[16,2176]{1,0:T(8,128)(2,1)S(1)}, u32[]{:S(2)}, u32[]{:S(2)}) %collective-permute-start.10) | collective-permute-done | bytes 69664 | tf_op jit(solution)/shard_map/ppermute | solution.py:24
  25.1 0.2 sent_partials.1
  25.4 2.4 %collective-permute-start.11 = (bf16[8,2176]{1,0:T(8,128)(2,1)S(1)}, bf16[8,2176]{1,0:T(8,128)(2,1)S(1)}, u32[]{:S(2)}, u32[]{:S(2)}) collective-permute-start(bf16[8,2176]{1,0:T(8,128)(2,1)S(1)} %sent_partials.1), channel_id=1, source_target_pairs={{0,18},{2,16},{4,22},{6,20},{8,26},{10,24},{12,30},{14,28},{16,2},... | collective-permute-start | bytes 104456 | tf_op jit(solution)/shard_map/ppermute | solution.py:24
  28.0 1.7 %collective-permute-done.11.got = bf16[8,2176]{1,0:T(8,128)(2,1)S(1)} collective-permute-done((bf16[8,2176]{1,0:T(8,128)(2,1)S(1)}, bf16[8,2176]{1,0:T(8,128)(2,1)S(1)}, u32[]{:S(2)}, u32[]{:S(2)}) %collective-permute-start.11) | collective-permute-done | bytes 34848 | tf_op jit(solution)/shard_map/ppermute | solution.py:24
  29.7 0.3 merge_last.1
  30.0 1.7 %collective-permute-start.12 = (f32[8,128]{1,0:T(8,128)S(1)}, f32[8,128]{1,0:T(8,128)S(1)}, u32[]{:S(2)}, u32[]{:S(2)}) collective-permute-start(f32[8,128]{1,0:T(8,128)S(1)} %get-tuple-element.46.squares), channel_id=1, source_target_pairs={{0,1},{1,0},{2,3},{3,2},{4,5},{5,4},{6,7},{7,6},{8,9},{9,8},{10,11... | collective-permute-start | bytes 12296 | tf_op jit(solution)/shard_map/ppermute | solution.py:24
  31.6 1.9 %collective-permute-done.12.other = f32[8,128]{1,0:T(8,128)S(1)} collective-permute-done((f32[8,128]{1,0:T(8,128)S(1)}, f32[8,128]{1,0:T(8,128)S(1)}, u32[]{:S(2)}, u32[]{:S(2)}) %collective-permute-start.12) | collective-permute-done | bytes 4128 | tf_op jit(solution)/shard_map/ppermute | solution.py:24
  33.6 0.7 %normalize.1 = (bf16[4,2048]{1,0:T(4,128)(2,1)}, bf16[2,2048]{1,0:T(2,128)(2,1)}, bf16[1,2048]{1,0:T(2,128)(2,1)}) custom-call(f32[8,2048]{1,0:T(8,128)S(1)} %get-tuple-element.45.att, f32[8,128]{1,0:T(8,128)S(1)} %get-tuple-element.46.squares, f32[8,128]{1,0:T(8,128)S(1)} %collective-permute-done.12.other, f32[1,2048]{1,0:T(1,128)S(1)} %bitcast.6), custom_call_target="tpu_custom_call" | custom-call | tf_op jit(solution)/shard_map/normalize/pallas_call | solution.py:43
  (38 shorter events, 1.1 us)
Async XLA Ops:
  0.6 4.5 %collective-permute-start = (bf16[4,2048]{1,0:T(4,128)(2,1)}, bf16[4,2048]{1,0:T(4,128)(2,1)S(1)}, u32[]{:S(2)}, u32[]{:S(2)}) collective-permute-start(bf16[4,2048]{1,0:T(4,128)(2,1)} %mine.1), channel_id=1, source_target_pairs={{0,6},{2,4},{4,2},{6,0},{8,14},{10,12},{12,10},{14,8},{16,22},{18,... | collective-permute-start | bytes 49160 | tf_op jit(solution)/shard_map/ppermute | solution.py:24
  3.1 8.9 %collective-permute-start.3 = (bf16[256,512]{1,0:T(8,128)(2,1)}, bf16[256,512]{1,0:T(8,128)(2,1)S(1)}, u32[]{:S(2)}, u32[]{:S(2)}) collective-permute-start(bf16[256,512]{1,0:T(8,128)(2,1)} %cached.1), channel_id=1, source_target_pairs={{0,6},{2,4},{4,2},{6,0},{8,14},{10,12},{12,10},{14,8},{16,22},{18,... | collective-permute-start | bytes 786440 | tf_op jit(solution)/shard_map/ppermute | solution.py:24
  3.2 1.9 %copy-start.1 = (bf16[256,512]{1,0:T(8,128)(2,1)S(1)}, bf16[256,512]{1,0:T(8,128)(2,1)}, u32[]{:S(2)}) copy-start(bf16[256,512]{1,0:T(8,128)(2,1)} %cached.1) | copy-start | bytes 786436
  3.2 2.0 %copy-start.3 = (bf16[4,2048]{1,0:T(4,128)(2,1)S(1)}, bf16[4,2048]{1,0:T(4,128)(2,1)}, u32[]{:S(2)}) copy-start(bf16[4,2048]{1,0:T(4,128)(2,1)} %spans.1) | copy-start | bytes 49156
  3.2 2.0 %copy-start.4 = (bf16[4,2048]{1,0:T(4,128)(2,1)S(1)}, bf16[4,2048]{1,0:T(4,128)(2,1)}, u32[]{:S(2)}) copy-start(bf16[4,2048]{1,0:T(4,128)(2,1)} %mine.1) | copy-start | bytes 49156
  5.2 0.9 %copy-start.9 = (f32[8,128]{1,0:T(8,128)S(1)}, f32[8,128]{1,0:T(8,128)}, u32[]{:S(2)}) copy-start(f32[8,128]{1,0:T(8,128)} %get-tuple-element.26._) | copy-start | bytes 12292
  5.2 1.6 %collective-permute-start.1 = (bf16[8,2048]{1,0:T(8,128)(2,1)S(1)}, bf16[8,2048]{1,0:T(8,128)(2,1)S(1)}, u32[]{:S(2)}, u32[]{:S(2)}) collective-permute-start(bf16[8,2048]{1,0:T(8,128)(2,1)S(1)} %get-tuple-element.30.pair), channel_id=1, source_target_pairs={{0,2},{2,0},{4,6},{6,4},{8,10},{10,8},{12,14},{14,12},{16,18},{18,... | collective-permute-start | bytes 98312 | tf_op jit(solution)/shard_map/ppermute | solution.py:24
  6.0 0.7 %copy-start.6 = (s32[32]{0:T(128)S(1)}, s32[32]{0:T(128)}, u32[]{:S(2)}) copy-start(s32[32]{0:T(128)} %param.33) | copy-start | bytes 388
  6.0 0.7 %copy-start.7 = (s32[16]{0:T(128)S(1)}, s32[16]{0:T(128)}, u32[]{:S(2)}) copy-start(s32[16]{0:T(128)} %param.34) | copy-start | bytes 196
  6.0 6.1 %collective-permute-start.4 = (bf16[256,512]{1,0:T(8,128)(2,1)S(1)}, bf16[256,512]{1,0:T(8,128)(2,1)S(1)}, u32[]{:S(2)}, u32[]{:S(2)}) collective-permute-start(bf16[256,512]{1,0:T(8,128)(2,1)S(1)} %get-tuple-element.31.k0), channel_id=1, source_target_pairs={{0,2},{2,0},{4,6},{6,4},{8,10},{10,8},{12,14},{14,12},{16,18},{18,... | collective-permute-start | bytes 786440 | tf_op jit(solution)/shard_map/ppermute | solution.py:24
  6.6 3.2 %copy-start.10 = (bf16[280,512]{1,0:T(8,128)(2,1)S(1)}, bf16[280,512]{1,0:T(8,128)(2,1)}, u32[]{:S(2)}) copy-start(bf16[280,512]{1,0:T(8,128)(2,1)} %get-tuple-element.33) | copy-start | bytes 860164
  6.6 12.3 %copy-start.8 = (s32[64]{0:T(128)S(1)}, s32[64]{0:T(128)}, u32[]{:S(2)}) copy-start(s32[64]{0:T(128)} %param.23) | copy-start | bytes 772
  7.0 5.0 %collective-permute-start.2 = (bf16[16,2048]{1,0:T(8,128)(2,1)S(1)}, bf16[16,2048]{1,0:T(8,128)(2,1)S(1)}, u32[]{:S(2)}, u32[]{:S(2)}) collective-permute-start(bf16[16,2048]{1,0:T(8,128)(2,1)S(1)} %column_queries.1.mine), channel_id=1, source_target_pairs={{0,18},{2,16},{4,22},{6,20},{8,26},{10,24},{12,30},{14,28},{16,2},... | collective-permute-start | bytes 196616 | tf_op jit(solution)/shard_map/ppermute | solution.py:24
  9.8 8.7 %collective-permute-start.6 = (bf16[280,512]{1,0:T(8,128)(2,1)S(1)}, bf16[280,512]{1,0:T(8,128)(2,1)S(1)}, u32[]{:S(2)}, u32[]{:S(2)}) collective-permute-start(bf16[280,512]{1,0:T(8,128)(2,1)S(1)} %copy-done.10), channel_id=1, source_target_pairs={{0,6},{2,4},{4,2},{6,0},{8,14},{10,12},{12,10},{14,8},{16,22},{18,... | collective-permute-start | bytes 860168 | tf_op jit(solution)/shard_map/ppermute | solution.py:24
  12.1 6.4 %collective-permute-start.7 = (bf16[256,512]{1,0:T(8,128)(2,1)S(1)}, bf16[256,512]{1,0:T(8,128)(2,1)S(1)}, u32[]{:S(2)}, u32[]{:S(2)}) collective-permute-start(bf16[256,512]{1,0:T(8,128)(2,1)S(1)} %get-tuple-element.34.k3), channel_id=1, source_target_pairs={{0,2},{2,0},{4,6},{6,4},{8,10},{10,8},{12,14},{14,12},{16,18},{18,... | collective-permute-start | bytes 786440 | tf_op jit(solution)/shard_map/ppermute | solution.py:24
  13.8 4.7 %collective-permute-start.5 = (bf16[40,1024]{1,0:T(8,128)(2,1)S(1)}, bf16[40,1024]{1,0:T(8,128)(2,1)S(1)}, u32[]{:S(2)}, u32[]{:S(2)}) collective-permute-start(bf16[40,1024]{1,0:T(8,128)(2,1)S(1)} %get-tuple-element.32.mine), channel_id=1, source_target_pairs={{0,10},{2,8},{4,14},{6,12},{8,2},{10,0},{12,6},{14,4},{16,26},{18,... | collective-permute-start | bytes 245768 | tf_op jit(solution)/shard_map/ppermute | solution.py:24
  15.1 4.1 %collective-permute-start.8 = (bf16[280,512]{1,0:T(8,128)(2,1)S(1)}, bf16[280,512]{1,0:T(8,128)(2,1)S(1)}, u32[]{:S(2)}, u32[]{:S(2)}) collective-permute-start(bf16[280,512]{1,0:T(8,128)(2,1)S(1)} %copy-done.10), channel_id=1, source_target_pairs={{0,2},{2,0},{4,6},{6,4},{8,10},{10,8},{12,14},{14,12},{16,18},{18,... | collective-permute-start | bytes 860168 | tf_op jit(solution)/shard_map/ppermute | solution.py:24
  18.5 1.6 %copy-start = (bf16[256,512]{1,0:T(8,128)(2,1)S(1)}, bf16[256,512]{1,0:T(8,128)(2,1)}, u32[]{:S(2)}) copy-start(bf16[256,512]{1,0:T(8,128)(2,1)} %v0.3) | copy-start | bytes 786436
  18.5 1.6 %collective-permute-start.9 = (bf16[280,512]{1,0:T(8,128)(2,1)S(1)}, bf16[280,512]{1,0:T(8,128)(2,1)S(1)}, u32[]{:S(2)}, u32[]{:S(2)}) collective-permute-start(bf16[280,512]{1,0:T(8,128)(2,1)S(1)} %get-tuple-element.39.v3), channel_id=1, source_target_pairs={{0,2},{2,0},{4,6},{6,4},{8,10},{10,8},{12,14},{14,12},{16,18},{18,... | collective-permute-start | bytes 860168 | tf_op jit(solution)/shard_map/ppermute | solution.py:24
  19.0 1.1 %copy-start.2 = (bf16[24,512]{1,0:T(8,128)(2,1)S(1)}, bf16[24,512]{1,0:T(8,128)(2,1)}, u32[]{:S(2)}) copy-start(bf16[24,512]{1,0:T(8,128)(2,1)} %get-tuple-element.40.extra) | copy-start | bytes 73732
  21.0 4.1 %collective-permute-start.10 = (bf16[16,2176]{1,0:T(8,128)(2,1)S(1)}, bf16[16,2176]{1,0:T(8,128)(2,1)S(1)}, u32[]{:S(2)}, u32[]{:S(2)}) collective-permute-start(bf16[16,2176]{1,0:T(8,128)(2,1)S(1)} %sent_attention.1), channel_id=1, source_target_pairs={{0,10},{2,8},{4,14},{6,12},{8,2},{10,0},{12,6},{14,4},{16,26},{18,... | collective-permute-start | bytes 208904 | tf_op jit(solution)/shard_map/ppermute | solution.py:24
  25.4 4.3 %collective-permute-start.11 = (bf16[8,2176]{1,0:T(8,128)(2,1)S(1)}, bf16[8,2176]{1,0:T(8,128)(2,1)S(1)}, u32[]{:S(2)}, u32[]{:S(2)}) collective-permute-start(bf16[8,2176]{1,0:T(8,128)(2,1)S(1)} %sent_partials.1), channel_id=1, source_target_pairs={{0,18},{2,16},{4,22},{6,20},{8,26},{10,24},{12,30},{14,28},{16,2},... | collective-permute-start | bytes 104456 | tf_op jit(solution)/shard_map/ppermute | solution.py:24
  29.7 3.9 %copy-start.5 = (f32[2048]{0:T(1024)S(1)}, f32[2048]{0:T(1024)}, u32[]{:S(2)}) copy-start(f32[2048]{0:T(1024)} %param.35) | copy-start | bytes 24580
  30.0 3.6 %collective-permute-start.12 = (f32[8,128]{1,0:T(8,128)S(1)}, f32[8,128]{1,0:T(8,128)S(1)}, u32[]{:S(2)}, u32[]{:S(2)}) collective-permute-start(f32[8,128]{1,0:T(8,128)S(1)} %get-tuple-element.46.squares), channel_id=1, source_target_pairs={{0,1},{1,0},{2,3},{3,2},{4,5},{5,4},{6,7},{7,6},{8,9},{9,8},{10,11... | collective-permute-start | bytes 12296 | tf_op jit(solution)/shard_map/ppermute | solution.py:24

commit v7 on v6

--- a/solution.py
+++ b/solution.py
@@ -122,7 +122,9 @@
             jnp.where(second, token, jnp.where(first, revealed[...].astype(F32), frame))
         )
     sets += shown
-    parts = jnp.concatenate([*sets[0::2], *sets[1::2]], axis=0).astype(BF16)
+    half = extra.shape[0] // 2
+    rest = jnp.zeros((half - 3 * spans, extra.shape[1]), F32)
+    parts = jnp.concatenate([*sets[0::2], rest, *sets[1::2], rest], axis=0).astype(BF16)
     extra[...] = parts
     values[cached:, :] = parts
     done[...] = jnp.zeros(done.shape, F32)
@@ -421,7 +423,7 @@
     bits = [(1 << b) + 1 for b in range(2, owners.bit_length() - 1)][::-1]
 
     depth = (blocks // 2) * spans + blocks * picked
-    extras = 3 * spans
+    extras = -(-3 * spans // 16) * 16
 
     q3 = exchange(frame_q, "ctx", 3)
     small = (

time: 34.4 us -> 34.6 us (level)
  waiting for transfers between devices: 10.6 us -> 11.2 us
  starting transfers between devices: 16.8 us -> 16.4 us
    ppermute x13, waiting for transfers between devices: 10.6 us -> 11.2 us  [exchange(): return lax.ppermute(value, axis, pairs)]
    ppermute x13, starting transfers between devices: 16.8 us -> 16.4 us  [exchange(): return lax.ppermute(value, axis, pairs)]
where the time goes in v7:
time: 34.6 us; the launch traced here: 34.5 us
  starting transfers between devices  16.4 us (47%)
  waiting for transfers between devices  11.2 us (32%)
  Pallas kernels  5.57 us (16%)
  between operations  0.77 us (2%)
  local copies, waits for them, and re-layouts  0.6 us (2%)
    ppermute x13, starting transfers between devices, exchange(): return lax.ppermute(value, axis, pairs)  16.4 us
    ppermute x13, waiting for transfers between devices, exchange(): return lax.ppermute(value, axis, pairs)  11.2 us
    pallas_call x14, Pallas kernels, call(): pl.pallas_call(kernel, out_shape=out_shape, in_specs=in_specs, out_specs=...  5.57 us
  transfers between devices with their start and end apart: 13, of which 7 were waited for; matrix products, arithmetic and copies ran while one was open for 0% of the time, Pallas kernels for 10%

profile of v7, /device:TPU:0, one launch (start us, length us, event | category | flops | bytes accessed | tf_op | source)
XLA Modules:
  0.0 34.5 jit_solution(2862949575706610036)
XLA Ops:
  0.6 2.5 %collective-permute-start = (bf16[4,2048]{1,0:T(4,128)(2,1)}, bf16[4,2048]{1,0:T(4,128)(2,1)S(1)}, u32[]{:S(2)}, u32[]{:S(2)}) collective-permute-start(bf16[4,2048]{1,0:T(4,128)(2,1)} %mine.1), channel_id=1, source_target_pairs={{0,6},{2,4},{4,2},{6,0},{8,14},{10,12},{12,10},{14,8},{16,22},{18,... | collective-permute-start | bytes 49160 | tf_op jit(solution)/shard_map/ppermute | solution.py:24
  3.2 1.9 %plane_values.1 = (bf16[288,512]{1,0:T(8,128)(2,1)}, bf16[32,512]{1,0:T(8,128)(2,1)}, f32[8,128]{1,0:T(8,128)}) custom-call(s32[1]{0:T(128)} %bitcast.place, s32[1,4]{1,0:T(1,128)} %bitcast.12, s32[1,32]{1,0:T(1,128)} %bitcast.7, s32[1,16]{1,0:T(1,128)} %bitcast.9, bf16[18,512]{1,0:T(8,128)(2,1)} %table_h.1, bf16[4,512]{1,0:T(4,128)(2,1)} %span_k_h.1, ...), custom_call_target="tpu_custom_call" | custom-call | flops 34500001792 | bytes 108000000 | tf_op jit(solution)/shard_map/plane_values/pallas_call | solution.py:43
  5.2 0.7 %collective-permute-start.1 = (bf16[8,2048]{1,0:T(8,128)(2,1)S(1)}, bf16[8,2048]{1,0:T(8,128)(2,1)S(1)}, u32[]{:S(2)}, u32[]{:S(2)}) collective-permute-start(bf16[8,2048]{1,0:T(8,128)(2,1)S(1)} %get-tuple-element.30.pair), channel_id=1, source_target_pairs={{0,2},{2,0},{4,6},{6,4},{8,10},{10,8},{12,14},{14,12},{16,18},{18,... | collective-permute-start | bytes 98312 | tf_op jit(solution)/shard_map/ppermute | solution.py:24
  6.1 0.5 %copy-done.6 = s32[32]{0:T(128)S(1)} copy-done((s32[32]{0:T(128)S(1)}, s32[32]{0:T(128)}, u32[]{:S(2)}) %copy-start.6) | copy-done | bytes 152
  6.8 0.2 column_queries.1.mine
  7.0 2.8 %collective-permute-start.2 = (bf16[16,2048]{1,0:T(8,128)(2,1)S(1)}, bf16[16,2048]{1,0:T(8,128)(2,1)S(1)}, u32[]{:S(2)}, u32[]{:S(2)}) collective-permute-start(bf16[16,2048]{1,0:T(8,128)(2,1)S(1)} %column_queries.1.mine), channel_id=1, source_target_pairs={{0,18},{2,16},{4,22},{6,20},{8,26},{10,24},{12,30},{14,28},{16,2},... | collective-permute-start | bytes 196616 | tf_op jit(solution)/shard_map/ppermute | solution.py:24
  9.8 1.5 %collective-permute-start.6 = (bf16[288,512]{1,0:T(8,128)(2,1)S(1)}, bf16[288,512]{1,0:T(8,128)(2,1)S(1)}, u32[]{:S(2)}, u32[]{:S(2)}) collective-permute-start(bf16[288,512]{1,0:T(8,128)(2,1)S(1)} %copy-done.10), channel_id=1, source_target_pairs={{0,6},{2,4},{4,2},{6,0},{8,14},{10,12},{12,10},{14,8},{16,22},{18,... | collective-permute-start | bytes 884744 | tf_op jit(solution)/shard_map/ppermute | solution.py:24
  11.3 0.7 %collective-permute-done.2.other = bf16[16,2048]{1,0:T(8,128)(2,1)S(1)} collective-permute-done((bf16[16,2048]{1,0:T(8,128)(2,1)S(1)}, bf16[16,2048]{1,0:T(8,128)(2,1)S(1)}, u32[]{:S(2)}, u32[]{:S(2)}) %collective-permute-start.2) | collective-permute-done | bytes 65568 | tf_op jit(solution)/shard_map/ppermute | solution.py:24
  12.1 1.8 %collective-permute-start.7 = (bf16[256,512]{1,0:T(8,128)(2,1)S(1)}, bf16[256,512]{1,0:T(8,128)(2,1)S(1)}, u32[]{:S(2)}, u32[]{:S(2)}) collective-permute-start(bf16[256,512]{1,0:T(8,128)(2,1)S(1)} %get-tuple-element.34.k3), channel_id=1, source_target_pairs={{0,2},{2,0},{4,6},{6,4},{8,10},{10,8},{12,14},{14,12},{16,18},{18,... | collective-permute-start | bytes 786440 | tf_op jit(solution)/shard_map/ppermute | solution.py:24
  13.8 1.3 %collective-permute-start.5 = (bf16[40,1024]{1,0:T(8,128)(2,1)S(1)}, bf16[40,1024]{1,0:T(8,128)(2,1)S(1)}, u32[]{:S(2)}, u32[]{:S(2)}) collective-permute-start(bf16[40,1024]{1,0:T(8,128)(2,1)S(1)} %get-tuple-element.32.mine), channel_id=1, source_target_pairs={{0,10},{2,8},{4,14},{6,12},{8,2},{10,0},{12,6},{14,4},{16,26},{18,... | collective-permute-start | bytes 245768 | tf_op jit(solution)/shard_map/ppermute | solution.py:24
  15.2 3.5 %collective-permute-done.6.__1_ = bf16[288,512]{1,0:T(8,128)(2,1)S(1)} collective-permute-done((bf16[288,512]{1,0:T(8,128)(2,1)S(1)}, bf16[288,512]{1,0:T(8,128)(2,1)S(1)}, u32[]{:S(2)}, u32[]{:S(2)}) %collective-permute-start.6) | collective-permute-done | bytes 294944 | tf_op jit(solution)/shard_map/ppermute | solution.py:24
  18.7 0.4 %collective-permute-start.9 = (bf16[288,512]{1,0:T(8,128)(2,1)S(1)}, bf16[288,512]{1,0:T(8,128)(2,1)S(1)}, u32[]{:S(2)}, u32[]{:S(2)}) collective-permute-start(bf16[288,512]{1,0:T(8,128)(2,1)S(1)} %get-tuple-element.39.v3), channel_id=1, source_target_pairs={{0,2},{2,0},{4,6},{6,4},{8,10},{10,8},{12,14},{14,12},{16,18},{18,... | collective-permute-start | bytes 884744 | tf_op jit(solution)/shard_map/ppermute | solution.py:24
  19.4 0.9 %collective-permute-done.9.v2 = bf16[288,512]{1,0:T(8,128)(2,1)S(1)} collective-permute-done((bf16[288,512]{1,0:T(8,128)(2,1)S(1)}, bf16[288,512]{1,0:T(8,128)(2,1)S(1)}, u32[]{:S(2)}, u32[]{:S(2)}) %collective-permute-start.9) | collective-permute-done | bytes 294944 | tf_op jit(solution)/shard_map/ppermute | solution.py:24
  20.4 0.8 %sent_attention.1 = bf16[16,2176]{1,0:T(8,128)(2,1)S(1)} custom-call(bf16[32,2048]{1,0:T(8,128)(2,1)S(1)} %ordered_queries.1.picked, f32[32,64]{1,0:T(8,128)S(1)} %get-tuple-element.36.allowed, bf16[256,512]{1,0:T(8,128)(2,1)S(1)} %get-tuple-element.31.k0, bf16[256,512]{1,0:T(8,128)(2,1)S(1)} %get-tuple-element.37.k1, ...), custom_call_target="tpu_custom_call" | custom-call | tf_op jit(solution)/shard_map/sent_attention/pallas_call | solution.py:43
  21.2 1.5 %collective-permute-start.10 = (bf16[16,2176]{1,0:T(8,128)(2,1)S(1)}, bf16[16,2176]{1,0:T(8,128)(2,1)S(1)}, u32[]{:S(2)}, u32[]{:S(2)}) collective-permute-start(bf16[16,2176]{1,0:T(8,128)(2,1)S(1)} %sent_attention.1), channel_id=1, source_target_pairs={{0,10},{2,8},{4,14},{6,12},{8,2},{10,0},{12,6},{14,4},{16,26},{18,... | collective-permute-start | bytes 208904 | tf_op jit(solution)/shard_map/ppermute | solution.py:24
  22.7 0.8 %kept_attention.1 = (f32[16,2048]{1,0:T(8,128)S(1)}, f32[16,128]{1,0:T(8,128)S(1)}) custom-call(bf16[32,2048]{1,0:T(8,128)(2,1)S(1)} %ordered_queries.1.picked, f32[32,64]{1,0:T(8,128)S(1)} %get-tuple-element.36.allowed, bf16[256,512]{1,0:T(8,128)(2,1)S(1)} %get-tuple-element.31.k0, bf16[256,512]{1,0:T(8,128)(2,1)S(1)} %get-tuple-element.37.k1, ...), custom_call_target="tpu_custom_call" | custom-call | tf_op jit(solution)/shard_map/kept_attention/pallas_call | solution.py:43
  23.5 1.8 %collective-permute-done.10.got = bf16[16,2176]{1,0:T(8,128)(2,1)S(1)} collective-permute-done((bf16[16,2176]{1,0:T(8,128)(2,1)S(1)}, bf16[16,2176]{1,0:T(8,128)(2,1)S(1)}, u32[]{:S(2)}, u32[]{:S(2)}) %collective-permute-start.10) | collective-permute-done | bytes 69664 | tf_op jit(solution)/shard_map/ppermute | solution.py:24
  25.3 0.2 sent_partials.1
  25.6 2.2 %collective-permute-start.11 = (bf16[8,2176]{1,0:T(8,128)(2,1)S(1)}, bf16[8,2176]{1,0:T(8,128)(2,1)S(1)}, u32[]{:S(2)}, u32[]{:S(2)}) collective-permute-start(bf16[8,2176]{1,0:T(8,128)(2,1)S(1)} %sent_partials.1), channel_id=1, source_target_pairs={{0,18},{2,16},{4,22},{6,20},{8,26},{10,24},{12,30},{14,28},{16,2},... | collective-permute-start | bytes 104456 | tf_op jit(solution)/shard_map/ppermute | solution.py:24
  28.0 1.9 %collective-permute-done.11.got = bf16[8,2176]{1,0:T(8,128)(2,1)S(1)} collective-permute-done((bf16[8,2176]{1,0:T(8,128)(2,1)S(1)}, bf16[8,2176]{1,0:T(8,128)(2,1)S(1)}, u32[]{:S(2)}, u32[]{:S(2)}) %collective-permute-start.11) | collective-permute-done | bytes 34848 | tf_op jit(solution)/shard_map/ppermute | solution.py:24
  29.9 0.3 merge_last.1
  30.2 1.5 %collective-permute-start.12 = (f32[8,128]{1,0:T(8,128)S(1)}, f32[8,128]{1,0:T(8,128)S(1)}, u32[]{:S(2)}, u32[]{:S(2)}) collective-permute-start(f32[8,128]{1,0:T(8,128)S(1)} %get-tuple-element.46.squares), channel_id=1, source_target_pairs={{0,1},{1,0},{2,3},{3,2},{4,5},{5,4},{6,7},{7,6},{8,9},{9,8},{10,11... | collective-permute-start | bytes 12296 | tf_op jit(solution)/shard_map/ppermute | solution.py:24
  31.7 2.1 %collective-permute-done.12.other = f32[8,128]{1,0:T(8,128)S(1)} collective-permute-done((f32[8,128]{1,0:T(8,128)S(1)}, f32[8,128]{1,0:T(8,128)S(1)}, u32[]{:S(2)}, u32[]{:S(2)}) %collective-permute-start.12) | collective-permute-done | bytes 4128 | tf_op jit(solution)/shard_map/ppermute | solution.py:24
  33.8 0.7 %normalize.1 = (bf16[4,2048]{1,0:T(4,128)(2,1)}, bf16[2,2048]{1,0:T(2,128)(2,1)}, bf16[1,2048]{1,0:T(2,128)(2,1)}) custom-call(f32[8,2048]{1,0:T(8,128)S(1)} %get-tuple-element.45.att, f32[8,128]{1,0:T(8,128)S(1)} %get-tuple-element.46.squares, f32[8,128]{1,0:T(8,128)S(1)} %collective-permute-done.12.other, f32[1,2048]{1,0:T(1,128)S(1)} %bitcast.6), custom_call_target="tpu_custom_call" | custom-call | tf_op jit(solution)/shard_map/normalize/pallas_call | solution.py:43
  (38 shorter events, 1.1 us)
Async XLA Ops:
  0.6 4.5 %collective-permute-start = (bf16[4,2048]{1,0:T(4,128)(2,1)}, bf16[4,2048]{1,0:T(4,128)(2,1)S(1)}, u32[]{:S(2)}, u32[]{:S(2)}) collective-permute-start(bf16[4,2048]{1,0:T(4,128)(2,1)} %mine.1), channel_id=1, source_target_pairs={{0,6},{2,4},{4,2},{6,0},{8,14},{10,12},{12,10},{14,8},{16,22},{18,... | collective-permute-start | bytes 49160 | tf_op jit(solution)/shard_map/ppermute | solution.py:24
  3.1 8.9 %collective-permute-start.3 = (bf16[256,512]{1,0:T(8,128)(2,1)}, bf16[256,512]{1,0:T(8,128)(2,1)S(1)}, u32[]{:S(2)}, u32[]{:S(2)}) collective-permute-start(bf16[256,512]{1,0:T(8,128)(2,1)} %cached.1), channel_id=1, source_target_pairs={{0,6},{2,4},{4,2},{6,0},{8,14},{10,12},{12,10},{14,8},{16,22},{18,... | collective-permute-start | bytes 786440 | tf_op jit(solution)/shard_map/ppermute | solution.py:24
  3.2 2.0 %copy-start.1 = (bf16[256,512]{1,0:T(8,128)(2,1)S(1)}, bf16[256,512]{1,0:T(8,128)(2,1)}, u32[]{:S(2)}) copy-start(bf16[256,512]{1,0:T(8,128)(2,1)} %cached.1) | copy-start | bytes 786436
  3.2 2.0 %copy-start.3 = (bf16[4,2048]{1,0:T(4,128)(2,1)S(1)}, bf16[4,2048]{1,0:T(4,128)(2,1)}, u32[]{:S(2)}) copy-start(bf16[4,2048]{1,0:T(4,128)(2,1)} %spans.1) | copy-start | bytes 49156
  3.2 2.0 %copy-start.4 = (bf16[4,2048]{1,0:T(4,128)(2,1)S(1)}, bf16[4,2048]{1,0:T(4,128)(2,1)}, u32[]{:S(2)}) copy-start(bf16[4,2048]{1,0:T(4,128)(2,1)} %mine.1) | copy-start | bytes 49156
  5.2 0.9 %copy-start.9 = (f32[8,128]{1,0:T(8,128)S(1)}, f32[8,128]{1,0:T(8,128)}, u32[]{:S(2)}) copy-start(f32[8,128]{1,0:T(8,128)} %get-tuple-element.26._) | copy-start | bytes 12292
  5.2 1.6 %collective-permute-start.1 = (bf16[8,2048]{1,0:T(8,128)(2,1)S(1)}, bf16[8,2048]{1,0:T(8,128)(2,1)S(1)}, u32[]{:S(2)}, u32[]{:S(2)}) collective-permute-start(bf16[8,2048]{1,0:T(8,128)(2,1)S(1)} %get-tuple-element.30.pair), channel_id=1, source_target_pairs={{0,2},{2,0},{4,6},{6,4},{8,10},{10,8},{12,14},{14,12},{16,18},{18,... | collective-permute-start | bytes 98312 | tf_op jit(solution)/shard_map/ppermute | solution.py:24
  6.0 0.7 %copy-start.6 = (s32[32]{0:T(128)S(1)}, s32[32]{0:T(128)}, u32[]{:S(2)}) copy-start(s32[32]{0:T(128)} %param.33) | copy-start | bytes 388
  6.0 0.7 %copy-start.7 = (s32[16]{0:T(128)S(1)}, s32[16]{0:T(128)}, u32[]{:S(2)}) copy-start(s32[16]{0:T(128)} %param.34) | copy-start | bytes 196
  6.0 6.1 %collective-permute-start.4 = (bf16[256,512]{1,0:T(8,128)(2,1)S(1)}, bf16[256,512]{1,0:T(8,128)(2,1)S(1)}, u32[]{:S(2)}, u32[]{:S(2)}) collective-permute-start(bf16[256,512]{1,0:T(8,128)(2,1)S(1)} %get-tuple-element.31.k0), channel_id=1, source_target_pairs={{0,2},{2,0},{4,6},{6,4},{8,10},{10,8},{12,14},{14,12},{16,18},{18,... | collective-permute-start | bytes 786440 | tf_op jit(solution)/shard_map/ppermute | solution.py:24
  6.6 3.2 %copy-start.10 = (bf16[288,512]{1,0:T(8,128)(2,1)S(1)}, bf16[288,512]{1,0:T(8,128)(2,1)}, u32[]{:S(2)}) copy-start(bf16[288,512]{1,0:T(8,128)(2,1)} %get-tuple-element.33) | copy-start | bytes 884740
  6.6 12.4 %copy-start.8 = (s32[64]{0:T(128)S(1)}, s32[64]{0:T(128)}, u32[]{:S(2)}) copy-start(s32[64]{0:T(128)} %param.23) | copy-start | bytes 772
  7.0 5.0 %collective-permute-start.2 = (bf16[16,2048]{1,0:T(8,128)(2,1)S(1)}, bf16[16,2048]{1,0:T(8,128)(2,1)S(1)}, u32[]{:S(2)}, u32[]{:S(2)}) collective-permute-start(bf16[16,2048]{1,0:T(8,128)(2,1)S(1)} %column_queries.1.mine), channel_id=1, source_target_pairs={{0,18},{2,16},{4,22},{6,20},{8,26},{10,24},{12,30},{14,28},{16,2},... | collective-permute-start | bytes 196616 | tf_op jit(solution)/shard_map/ppermute | solution.py:24
  9.8 8.8 %collective-permute-start.6 = (bf16[288,512]{1,0:T(8,128)(2,1)S(1)}, bf16[288,512]{1,0:T(8,128)(2,1)S(1)}, u32[]{:S(2)}, u32[]{:S(2)}) collective-permute-start(bf16[288,512]{1,0:T(8,128)(2,1)S(1)} %copy-done.10), channel_id=1, source_target_pairs={{0,6},{2,4},{4,2},{6,0},{8,14},{10,12},{12,10},{14,8},{16,22},{18,... | collective-permute-start | bytes 884744 | tf_op jit(solution)/shard_map/ppermute | solution.py:24
  12.1 6.6 %collective-permute-start.7 = (bf16[256,512]{1,0:T(8,128)(2,1)S(1)}, bf16[256,512]{1,0:T(8,128)(2,1)S(1)}, u32[]{:S(2)}, u32[]{:S(2)}) collective-permute-start(bf16[256,512]{1,0:T(8,128)(2,1)S(1)} %get-tuple-element.34.k3), channel_id=1, source_target_pairs={{0,2},{2,0},{4,6},{6,4},{8,10},{10,8},{12,14},{14,12},{16,18},{18,... | collective-permute-start | bytes 786440 | tf_op jit(solution)/shard_map/ppermute | solution.py:24
  13.8 4.9 %collective-permute-start.5 = (bf16[40,1024]{1,0:T(8,128)(2,1)S(1)}, bf16[40,1024]{1,0:T(8,128)(2,1)S(1)}, u32[]{:S(2)}, u32[]{:S(2)}) collective-permute-start(bf16[40,1024]{1,0:T(8,128)(2,1)S(1)} %get-tuple-element.32.mine), channel_id=1, source_target_pairs={{0,10},{2,8},{4,14},{6,12},{8,2},{10,0},{12,6},{14,4},{16,26},{18,... | collective-permute-start | bytes 245768 | tf_op jit(solution)/shard_map/ppermute | solution.py:24
  15.1 4.3 %collective-permute-start.8 = (bf16[288,512]{1,0:T(8,128)(2,1)S(1)}, bf16[288,512]{1,0:T(8,128)(2,1)S(1)}, u32[]{:S(2)}, u32[]{:S(2)}) collective-permute-start(bf16[288,512]{1,0:T(8,128)(2,1)S(1)} %copy-done.10), channel_id=1, source_target_pairs={{0,2},{2,0},{4,6},{6,4},{8,10},{10,8},{12,14},{14,12},{16,18},{18,... | collective-permute-start | bytes 884744 | tf_op jit(solution)/shard_map/ppermute | solution.py:24
  18.7 1.7 %copy-start = (bf16[256,512]{1,0:T(8,128)(2,1)S(1)}, bf16[256,512]{1,0:T(8,128)(2,1)}, u32[]{:S(2)}) copy-start(bf16[256,512]{1,0:T(8,128)(2,1)} %v0.3) | copy-start | bytes 786436
  18.7 1.6 %collective-permute-start.9 = (bf16[288,512]{1,0:T(8,128)(2,1)S(1)}, bf16[288,512]{1,0:T(8,128)(2,1)S(1)}, u32[]{:S(2)}, u32[]{:S(2)}) collective-permute-start(bf16[288,512]{1,0:T(8,128)(2,1)S(1)} %get-tuple-element.39.v3), channel_id=1, source_target_pairs={{0,2},{2,0},{4,6},{6,4},{8,10},{10,8},{12,14},{14,12},{16,18},{18,... | collective-permute-start | bytes 884744 | tf_op jit(solution)/shard_map/ppermute | solution.py:24
  19.2 1.1 %copy-start.2 = (bf16[32,512]{1,0:T(8,128)(2,1)S(1)}, bf16[32,512]{1,0:T(8,128)(2,1)}, u32[]{:S(2)}) copy-start(bf16[32,512]{1,0:T(8,128)(2,1)} %get-tuple-element.40.extra) | copy-start | bytes 98308
  21.2 4.1 %collective-permute-start.10 = (bf16[16,2176]{1,0:T(8,128)(2,1)S(1)}, bf16[16,2176]{1,0:T(8,128)(2,1)S(1)}, u32[]{:S(2)}, u32[]{:S(2)}) collective-permute-start(bf16[16,2176]{1,0:T(8,128)(2,1)S(1)} %sent_attention.1), channel_id=1, source_target_pairs={{0,10},{2,8},{4,14},{6,12},{8,2},{10,0},{12,6},{14,4},{16,26},{18,... | collective-permute-start | bytes 208904 | tf_op jit(solution)/shard_map/ppermute | solution.py:24
  25.6 4.3 %collective-permute-start.11 = (bf16[8,2176]{1,0:T(8,128)(2,1)S(1)}, bf16[8,2176]{1,0:T(8,128)(2,1)S(1)}, u32[]{:S(2)}, u32[]{:S(2)}) collective-permute-start(bf16[8,2176]{1,0:T(8,128)(2,1)S(1)} %sent_partials.1), channel_id=1, source_target_pairs={{0,18},{2,16},{4,22},{6,20},{8,26},{10,24},{12,30},{14,28},{16,2},... | collective-permute-start | bytes 104456 | tf_op jit(solution)/shard_map/ppermute | solution.py:24
  29.9 3.9 %copy-start.5 = (f32[2048]{0:T(1024)S(1)}, f32[2048]{0:T(1024)}, u32[]{:S(2)}) copy-start(f32[2048]{0:T(1024)} %param.35) | copy-start | bytes 24580
  30.2 3.6 %collective-permute-start.12 = (f32[8,128]{1,0:T(8,128)S(1)}, f32[8,128]{1,0:T(8,128)S(1)}, u32[]{:S(2)}, u32[]{:S(2)}) collective-permute-start(f32[8,128]{1,0:T(8,128)S(1)} %get-tuple-element.46.squares), channel_id=1, source_target_pairs={{0,1},{1,0},{2,3},{3,2},{4,5},{5,4},{6,7},{7,6},{8,9},{9,8},{10,11... | collective-permute-start | bytes 12296 | tf_op jit(solution)/shard_map/ppermute | solution.py:24

commit v8 on v7

--- a/solution.py
+++ b/solution.py
@@ -345,14 +345,11 @@
     b = jnp.exp(theirs - top)
     total = a + b
     a = a / total
-    b = b / total
     merged = []
     for h in range(heads * GROUP):
         columns = slice(h * HD, (h + 1) * HD)
-        merged.append(
-            kept[half, columns] * a[:, h : h + 1]
-            + got[half, columns].astype(F32) * b[:, h : h + 1]
-        )
+        theirs = got[half, columns].astype(F32)
+        merged.append(theirs + (kept[half, columns] - theirs) * a[:, h : h + 1])
     return merged, top + jnp.log(total)
 
 

time: 34.6 us -> 34.6 us (level)
  no operation moved by 1% of the time
where the time goes in v8:
time: 34.6 us; the launch traced here: 34.4 us
  starting transfers between devices  16.4 us (47%)
  waiting for transfers between devices  11.2 us (32%)
  Pallas kernels  5.49 us (16%)
  between operations  0.78 us (2%)
  local copies, waits for them, and re-layouts  0.6 us (2%)
    ppermute x13, starting transfers between devices, exchange(): return lax.ppermute(value, axis, pairs)  16.4 us
    ppermute x13, waiting for transfers between devices, exchange(): return lax.ppermute(value, axis, pairs)  11.2 us
    pallas_call x14, Pallas kernels, call(): pl.pallas_call(kernel, out_shape=out_shape, in_specs=in_specs, out_specs=...  5.49 us
  transfers between devices with their start and end apart: 13, of which 7 were waited for; matrix products, arithmetic and copies ran while one was open for 0% of the time, Pallas kernels for 10%

profile of v8, /device:TPU:0, one launch (start us, length us, event | category | flops | bytes accessed | tf_op | source)
XLA Modules:
  0.0 34.4 jit_solution(5668842225342904984)
XLA Ops:
  0.6 2.5 %collective-permute-start = (bf16[4,2048]{1,0:T(4,128)(2,1)}, bf16[4,2048]{1,0:T(4,128)(2,1)S(1)}, u32[]{:S(2)}, u32[]{:S(2)}) collective-permute-start(bf16[4,2048]{1,0:T(4,128)(2,1)} %mine.1), channel_id=1, source_target_pairs={{0,6},{2,4},{4,2},{6,0},{8,14},{10,12},{12,10},{14,8},{16,22},{18,... | collective-permute-start | bytes 49160 | tf_op jit(solution)/shard_map/ppermute | solution.py:24
  3.2 1.9 %plane_values.1 = (bf16[288,512]{1,0:T(8,128)(2,1)}, bf16[32,512]{1,0:T(8,128)(2,1)}, f32[8,128]{1,0:T(8,128)}) custom-call(s32[1]{0:T(128)} %bitcast.place, s32[1,4]{1,0:T(1,128)} %bitcast.12, s32[1,32]{1,0:T(1,128)} %bitcast.7, s32[1,16]{1,0:T(1,128)} %bitcast.9, bf16[18,512]{1,0:T(8,128)(2,1)} %table_h.1, bf16[4,512]{1,0:T(4,128)(2,1)} %span_k_h.1, ...), custom_call_target="tpu_custom_call" | custom-call | flops 34500001792 | bytes 108000000 | tf_op jit(solution)/shard_map/plane_values/pallas_call | solution.py:43
  5.2 0.7 %collective-permute-start.1 = (bf16[8,2048]{1,0:T(8,128)(2,1)S(1)}, bf16[8,2048]{1,0:T(8,128)(2,1)S(1)}, u32[]{:S(2)}, u32[]{:S(2)}) collective-permute-start(bf16[8,2048]{1,0:T(8,128)(2,1)S(1)} %get-tuple-element.30.pair), channel_id=1, source_target_pairs={{0,2},{2,0},{4,6},{6,4},{8,10},{10,8},{12,14},{14,12},{16,18},{18,... | collective-permute-start | bytes 98312 | tf_op jit(solution)/shard_map/ppermute | solution.py:24
  6.1 0.5 %copy-done.6 = s32[32]{0:T(128)S(1)} copy-done((s32[32]{0:T(128)S(1)}, s32[32]{0:T(128)}, u32[]{:S(2)}) %copy-start.6) | copy-done | bytes 152
  6.8 0.2 column_queries.1.mine
  7.0 2.8 %collective-permute-start.2 = (bf16[16,2048]{1,0:T(8,128)(2,1)S(1)}, bf16[16,2048]{1,0:T(8,128)(2,1)S(1)}, u32[]{:S(2)}, u32[]{:S(2)}) collective-permute-start(bf16[16,2048]{1,0:T(8,128)(2,1)S(1)} %column_queries.1.mine), channel_id=1, source_target_pairs={{0,18},{2,16},{4,22},{6,20},{8,26},{10,24},{12,30},{14,28},{16,2},... | collective-permute-start | bytes 196616 | tf_op jit(solution)/shard_map/ppermute | solution.py:24
  9.8 1.5 %collective-permute-start.6 = (bf16[288,512]{1,0:T(8,128)(2,1)S(1)}, bf16[288,512]{1,0:T(8,128)(2,1)S(1)}, u32[]{:S(2)}, u32[]{:S(2)}) collective-permute-start(bf16[288,512]{1,0:T(8,128)(2,1)S(1)} %copy-done.10), channel_id=1, source_target_pairs={{0,6},{2,4},{4,2},{6,0},{8,14},{10,12},{12,10},{14,8},{16,22},{18,... | collective-permute-start | bytes 884744 | tf_op jit(solution)/shard_map/ppermute | solution.py:24
  11.3 0.7 %collective-permute-done.2.other = bf16[16,2048]{1,0:T(8,128)(2,1)S(1)} collective-permute-done((bf16[16,2048]{1,0:T(8,128)(2,1)S(1)}, bf16[16,2048]{1,0:T(8,128)(2,1)S(1)}, u32[]{:S(2)}, u32[]{:S(2)}) %collective-permute-start.2) | collective-permute-done | bytes 65568 | tf_op jit(solution)/shard_map/ppermute | solution.py:24
  12.1 1.8 %collective-permute-start.7 = (bf16[256,512]{1,0:T(8,128)(2,1)S(1)}, bf16[256,512]{1,0:T(8,128)(2,1)S(1)}, u32[]{:S(2)}, u32[]{:S(2)}) collective-permute-start(bf16[256,512]{1,0:T(8,128)(2,1)S(1)} %get-tuple-element.34.k3), channel_id=1, source_target_pairs={{0,2},{2,0},{4,6},{6,4},{8,10},{10,8},{12,14},{14,12},{16,18},{18,... | collective-permute-start | bytes 786440 | tf_op jit(solution)/shard_map/ppermute | solution.py:24
  13.8 1.3 %collective-permute-start.5 = (bf16[40,1024]{1,0:T(8,128)(2,1)S(1)}, bf16[40,1024]{1,0:T(8,128)(2,1)S(1)}, u32[]{:S(2)}, u32[]{:S(2)}) collective-permute-start(bf16[40,1024]{1,0:T(8,128)(2,1)S(1)} %get-tuple-element.32.mine), channel_id=1, source_target_pairs={{0,10},{2,8},{4,14},{6,12},{8,2},{10,0},{12,6},{14,4},{16,26},{18,... | collective-permute-start | bytes 245768 | tf_op jit(solution)/shard_map/ppermute | solution.py:24
  15.2 3.5 %collective-permute-done.6.__1_ = bf16[288,512]{1,0:T(8,128)(2,1)S(1)} collective-permute-done((bf16[288,512]{1,0:T(8,128)(2,1)S(1)}, bf16[288,512]{1,0:T(8,128)(2,1)S(1)}, u32[]{:S(2)}, u32[]{:S(2)}) %collective-permute-start.6) | collective-permute-done | bytes 294944 | tf_op jit(solution)/shard_map/ppermute | solution.py:24
  18.7 0.4 %collective-permute-start.9 = (bf16[288,512]{1,0:T(8,128)(2,1)S(1)}, bf16[288,512]{1,0:T(8,128)(2,1)S(1)}, u32[]{:S(2)}, u32[]{:S(2)}) collective-permute-start(bf16[288,512]{1,0:T(8,128)(2,1)S(1)} %get-tuple-element.39.v3), channel_id=1, source_target_pairs={{0,2},{2,0},{4,6},{6,4},{8,10},{10,8},{12,14},{14,12},{16,18},{18,... | collective-permute-start | bytes 884744 | tf_op jit(solution)/shard_map/ppermute | solution.py:24
  19.4 0.9 %collective-permute-done.9.v2 = bf16[288,512]{1,0:T(8,128)(2,1)S(1)} collective-permute-done((bf16[288,512]{1,0:T(8,128)(2,1)S(1)}, bf16[288,512]{1,0:T(8,128)(2,1)S(1)}, u32[]{:S(2)}, u32[]{:S(2)}) %collective-permute-start.9) | collective-permute-done | bytes 294944 | tf_op jit(solution)/shard_map/ppermute | solution.py:24
  20.4 0.8 %sent_attention.1 = bf16[16,2176]{1,0:T(8,128)(2,1)S(1)} custom-call(bf16[32,2048]{1,0:T(8,128)(2,1)S(1)} %ordered_queries.1.picked, f32[32,64]{1,0:T(8,128)S(1)} %get-tuple-element.36.allowed, bf16[256,512]{1,0:T(8,128)(2,1)S(1)} %get-tuple-element.31.k0, bf16[256,512]{1,0:T(8,128)(2,1)S(1)} %get-tuple-element.37.k1, ...), custom_call_target="tpu_custom_call" | custom-call | tf_op jit(solution)/shard_map/sent_attention/pallas_call | solution.py:43
  21.2 1.5 %collective-permute-start.10 = (bf16[16,2176]{1,0:T(8,128)(2,1)S(1)}, bf16[16,2176]{1,0:T(8,128)(2,1)S(1)}, u32[]{:S(2)}, u32[]{:S(2)}) collective-permute-start(bf16[16,2176]{1,0:T(8,128)(2,1)S(1)} %sent_attention.1), channel_id=1, source_target_pairs={{0,10},{2,8},{4,14},{6,12},{8,2},{10,0},{12,6},{14,4},{16,26},{18,... | collective-permute-start | bytes 208904 | tf_op jit(solution)/shard_map/ppermute | solution.py:24
  22.7 0.8 %kept_attention.1 = (f32[16,2048]{1,0:T(8,128)S(1)}, f32[16,128]{1,0:T(8,128)S(1)}) custom-call(bf16[32,2048]{1,0:T(8,128)(2,1)S(1)} %ordered_queries.1.picked, f32[32,64]{1,0:T(8,128)S(1)} %get-tuple-element.36.allowed, bf16[256,512]{1,0:T(8,128)(2,1)S(1)} %get-tuple-element.31.k0, bf16[256,512]{1,0:T(8,128)(2,1)S(1)} %get-tuple-element.37.k1, ...), custom_call_target="tpu_custom_call" | custom-call | tf_op jit(solution)/shard_map/kept_attention/pallas_call | solution.py:43
  23.5 1.8 %collective-permute-done.10.got = bf16[16,2176]{1,0:T(8,128)(2,1)S(1)} collective-permute-done((bf16[16,2176]{1,0:T(8,128)(2,1)S(1)}, bf16[16,2176]{1,0:T(8,128)(2,1)S(1)}, u32[]{:S(2)}, u32[]{:S(2)}) %collective-permute-start.10) | collective-permute-done | bytes 69664 | tf_op jit(solution)/shard_map/ppermute | solution.py:24
  25.3 0.2 sent_partials.1
  25.5 2.2 %collective-permute-start.11 = (bf16[8,2176]{1,0:T(8,128)(2,1)S(1)}, bf16[8,2176]{1,0:T(8,128)(2,1)S(1)}, u32[]{:S(2)}, u32[]{:S(2)}) collective-permute-start(bf16[8,2176]{1,0:T(8,128)(2,1)S(1)} %sent_partials.1), channel_id=1, source_target_pairs={{0,18},{2,16},{4,22},{6,20},{8,26},{10,24},{12,30},{14,28},{16,2},... | collective-permute-start | bytes 104456 | tf_op jit(solution)/shard_map/ppermute | solution.py:24
  28.0 1.9 %collective-permute-done.11.got = bf16[8,2176]{1,0:T(8,128)(2,1)S(1)} collective-permute-done((bf16[8,2176]{1,0:T(8,128)(2,1)S(1)}, bf16[8,2176]{1,0:T(8,128)(2,1)S(1)}, u32[]{:S(2)}, u32[]{:S(2)}) %collective-permute-start.11) | collective-permute-done | bytes 34848 | tf_op jit(solution)/shard_map/ppermute | solution.py:24
  29.9 0.3 merge_last.1
  30.1 1.5 %collective-permute-start.12 = (f32[8,128]{1,0:T(8,128)S(1)}, f32[8,128]{1,0:T(8,128)S(1)}, u32[]{:S(2)}, u32[]{:S(2)}) collective-permute-start(f32[8,128]{1,0:T(8,128)S(1)} %get-tuple-element.46.squares), channel_id=1, source_target_pairs={{0,1},{1,0},{2,3},{3,2},{4,5},{5,4},{6,7},{7,6},{8,9},{9,8},{10,11... | collective-permute-start | bytes 12296 | tf_op jit(solution)/shard_map/ppermute | solution.py:24
  31.6 2.1 %collective-permute-done.12.other = f32[8,128]{1,0:T(8,128)S(1)} collective-permute-done((f32[8,128]{1,0:T(8,128)S(1)}, f32[8,128]{1,0:T(8,128)S(1)}, u32[]{:S(2)}, u32[]{:S(2)}) %collective-permute-start.12) | collective-permute-done | bytes 4128 | tf_op jit(solution)/shard_map/ppermute | solution.py:24
  33.7 0.7 %normalize.1 = (bf16[4,2048]{1,0:T(4,128)(2,1)}, bf16[2,2048]{1,0:T(2,128)(2,1)}, bf16[1,2048]{1,0:T(2,128)(2,1)}) custom-call(f32[8,2048]{1,0:T(8,128)S(1)} %get-tuple-element.45.att, f32[8,128]{1,0:T(8,128)S(1)} %get-tuple-element.46.squares, f32[8,128]{1,0:T(8,128)S(1)} %collective-permute-done.12.other, f32[1,2048]{1,0:T(1,128)S(1)} %bitcast.6), custom_call_target="tpu_custom_call" | custom-call | tf_op jit(solution)/shard_map/normalize/pallas_call | solution.py:43
  (38 shorter events, 1.0 us)
Async XLA Ops:
  0.6 4.5 %collective-permute-start = (bf16[4,2048]{1,0:T(4,128)(2,1)}, bf16[4,2048]{1,0:T(4,128)(2,1)S(1)}, u32[]{:S(2)}, u32[]{:S(2)}) collective-permute-start(bf16[4,2048]{1,0:T(4,128)(2,1)} %mine.1), channel_id=1, source_target_pairs={{0,6},{2,4},{4,2},{6,0},{8,14},{10,12},{12,10},{14,8},{16,22},{18,... | collective-permute-start | bytes 49160 | tf_op jit(solution)/shard_map/ppermute | solution.py:24
  3.1 8.9 %collective-permute-start.3 = (bf16[256,512]{1,0:T(8,128)(2,1)}, bf16[256,512]{1,0:T(8,128)(2,1)S(1)}, u32[]{:S(2)}, u32[]{:S(2)}) collective-permute-start(bf16[256,512]{1,0:T(8,128)(2,1)} %cached.1), channel_id=1, source_target_pairs={{0,6},{2,4},{4,2},{6,0},{8,14},{10,12},{12,10},{14,8},{16,22},{18,... | collective-permute-start | bytes 786440 | tf_op jit(solution)/shard_map/ppermute | solution.py:24
  3.2 2.0 %copy-start.1 = (bf16[256,512]{1,0:T(8,128)(2,1)S(1)}, bf16[256,512]{1,0:T(8,128)(2,1)}, u32[]{:S(2)}) copy-start(bf16[256,512]{1,0:T(8,128)(2,1)} %cached.1) | copy-start | bytes 786436
  3.2 2.0 %copy-start.3 = (bf16[4,2048]{1,0:T(4,128)(2,1)S(1)}, bf16[4,2048]{1,0:T(4,128)(2,1)}, u32[]{:S(2)}) copy-start(bf16[4,2048]{1,0:T(4,128)(2,1)} %spans.1) | copy-start | bytes 49156
  3.2 2.0 %copy-start.4 = (bf16[4,2048]{1,0:T(4,128)(2,1)S(1)}, bf16[4,2048]{1,0:T(4,128)(2,1)}, u32[]{:S(2)}) copy-start(bf16[4,2048]{1,0:T(4,128)(2,1)} %mine.1) | copy-start | bytes 49156
  5.2 0.9 %copy-start.9 = (f32[8,128]{1,0:T(8,128)S(1)}, f32[8,128]{1,0:T(8,128)}, u32[]{:S(2)}) copy-start(f32[8,128]{1,0:T(8,128)} %get-tuple-element.26._) | copy-start | bytes 12292
  5.2 1.6 %collective-permute-start.1 = (bf16[8,2048]{1,0:T(8,128)(2,1)S(1)}, bf16[8,2048]{1,0:T(8,128)(2,1)S(1)}, u32[]{:S(2)}, u32[]{:S(2)}) collective-permute-start(bf16[8,2048]{1,0:T(8,128)(2,1)S(1)} %get-tuple-element.30.pair), channel_id=1, source_target_pairs={{0,2},{2,0},{4,6},{6,4},{8,10},{10,8},{12,14},{14,12},{16,18},{18,... | collective-permute-start | bytes 98312 | tf_op jit(solution)/shard_map/ppermute | solution.py:24
  6.0 0.7 %copy-start.6 = (s32[32]{0:T(128)S(1)}, s32[32]{0:T(128)}, u32[]{:S(2)}) copy-start(s32[32]{0:T(128)} %param.33) | copy-start | bytes 388
  6.0 0.7 %copy-start.7 = (s32[16]{0:T(128)S(1)}, s32[16]{0:T(128)}, u32[]{:S(2)}) copy-start(s32[16]{0:T(128)} %param.34) | copy-start | bytes 196
  6.0 6.1 %collective-permute-start.4 = (bf16[256,512]{1,0:T(8,128)(2,1)S(1)}, bf16[256,512]{1,0:T(8,128)(2,1)S(1)}, u32[]{:S(2)}, u32[]{:S(2)}) collective-permute-start(bf16[256,512]{1,0:T(8,128)(2,1)S(1)} %get-tuple-element.31.k0), channel_id=1, source_target_pairs={{0,2},{2,0},{4,6},{6,4},{8,10},{10,8},{12,14},{14,12},{16,18},{18,... | collective-permute-start | bytes 786440 | tf_op jit(solution)/shard_map/ppermute | solution.py:24
  6.6 3.2 %copy-start.10 = (bf16[288,512]{1,0:T(8,128)(2,1)S(1)}, bf16[288,512]{1,0:T(8,128)(2,1)}, u32[]{:S(2)}) copy-start(bf16[288,512]{1,0:T(8,128)(2,1)} %get-tuple-element.33) | copy-start | bytes 884740
  6.6 12.4 %copy-start.8 = (s32[64]{0:T(128)S(1)}, s32[64]{0:T(128)}, u32[]{:S(2)}) copy-start(s32[64]{0:T(128)} %param.23) | copy-start | bytes 772
  7.0 5.0 %collective-permute-start.2 = (bf16[16,2048]{1,0:T(8,128)(2,1)S(1)}, bf16[16,2048]{1,0:T(8,128)(2,1)S(1)}, u32[]{:S(2)}, u32[]{:S(2)}) collective-permute-start(bf16[16,2048]{1,0:T(8,128)(2,1)S(1)} %column_queries.1.mine), channel_id=1, source_target_pairs={{0,18},{2,16},{4,22},{6,20},{8,26},{10,24},{12,30},{14,28},{16,2},... | collective-permute-start | bytes 196616 | tf_op jit(solution)/shard_map/ppermute | solution.py:24
  9.8 8.8 %collective-permute-start.6 = (bf16[288,512]{1,0:T(8,128)(2,1)S(1)}, bf16[288,512]{1,0:T(8,128)(2,1)S(1)}, u32[]{:S(2)}, u32[]{:S(2)}) collective-permute-start(bf16[288,512]{1,0:T(8,128)(2,1)S(1)} %copy-done.10), channel_id=1, source_target_pairs={{0,6},{2,4},{4,2},{6,0},{8,14},{10,12},{12,10},{14,8},{16,22},{18,... | collective-permute-start | bytes 884744 | tf_op jit(solution)/shard_map/ppermute | solution.py:24
  12.1 6.6 %collective-permute-start.7 = (bf16[256,512]{1,0:T(8,128)(2,1)S(1)}, bf16[256,512]{1,0:T(8,128)(2,1)S(1)}, u32[]{:S(2)}, u32[]{:S(2)}) collective-permute-start(bf16[256,512]{1,0:T(8,128)(2,1)S(1)} %get-tuple-element.34.k3), channel_id=1, source_target_pairs={{0,2},{2,0},{4,6},{6,4},{8,10},{10,8},{12,14},{14,12},{16,18},{18,... | collective-permute-start | bytes 786440 | tf_op jit(solution)/shard_map/ppermute | solution.py:24
  13.8 4.9 %collective-permute-start.5 = (bf16[40,1024]{1,0:T(8,128)(2,1)S(1)}, bf16[40,1024]{1,0:T(8,128)(2,1)S(1)}, u32[]{:S(2)}, u32[]{:S(2)}) collective-permute-start(bf16[40,1024]{1,0:T(8,128)(2,1)S(1)} %get-tuple-element.32.mine), channel_id=1, source_target_pairs={{0,10},{2,8},{4,14},{6,12},{8,2},{10,0},{12,6},{14,4},{16,26},{18,... | collective-permute-start | bytes 245768 | tf_op jit(solution)/shard_map/ppermute | solution.py:24
  15.1 4.3 %collective-permute-start.8 = (bf16[288,512]{1,0:T(8,128)(2,1)S(1)}, bf16[288,512]{1,0:T(8,128)(2,1)S(1)}, u32[]{:S(2)}, u32[]{:S(2)}) collective-permute-start(bf16[288,512]{1,0:T(8,128)(2,1)S(1)} %copy-done.10), channel_id=1, source_target_pairs={{0,2},{2,0},{4,6},{6,4},{8,10},{10,8},{12,14},{14,12},{16,18},{18,... | collective-permute-start | bytes 884744 | tf_op jit(solution)/shard_map/ppermute | solution.py:24
  18.7 1.7 %copy-start = (bf16[256,512]{1,0:T(8,128)(2,1)S(1)}, bf16[256,512]{1,0:T(8,128)(2,1)}, u32[]{:S(2)}) copy-start(bf16[256,512]{1,0:T(8,128)(2,1)} %v0.3) | copy-start | bytes 786436
  18.7 1.6 %collective-permute-start.9 = (bf16[288,512]{1,0:T(8,128)(2,1)S(1)}, bf16[288,512]{1,0:T(8,128)(2,1)S(1)}, u32[]{:S(2)}, u32[]{:S(2)}) collective-permute-start(bf16[288,512]{1,0:T(8,128)(2,1)S(1)} %get-tuple-element.39.v3), channel_id=1, source_target_pairs={{0,2},{2,0},{4,6},{6,4},{8,10},{10,8},{12,14},{14,12},{16,18},{18,... | collective-permute-start | bytes 884744 | tf_op jit(solution)/shard_map/ppermute | solution.py:24
  19.2 1.1 %copy-start.2 = (bf16[32,512]{1,0:T(8,128)(2,1)S(1)}, bf16[32,512]{1,0:T(8,128)(2,1)}, u32[]{:S(2)}) copy-start(bf16[32,512]{1,0:T(8,128)(2,1)} %get-tuple-element.40.extra) | copy-start | bytes 98308
  21.2 4.1 %collective-permute-start.10 = (bf16[16,2176]{1,0:T(8,128)(2,1)S(1)}, bf16[16,2176]{1,0:T(8,128)(2,1)S(1)}, u32[]{:S(2)}, u32[]{:S(2)}) collective-permute-start(bf16[16,2176]{1,0:T(8,128)(2,1)S(1)} %sent_attention.1), channel_id=1, source_target_pairs={{0,10},{2,8},{4,14},{6,12},{8,2},{10,0},{12,6},{14,4},{16,26},{18,... | collective-permute-start | bytes 208904 | tf_op jit(solution)/shard_map/ppermute | solution.py:24
  25.5 4.3 %collective-permute-start.11 = (bf16[8,2176]{1,0:T(8,128)(2,1)S(1)}, bf16[8,2176]{1,0:T(8,128)(2,1)S(1)}, u32[]{:S(2)}, u32[]{:S(2)}) collective-permute-start(bf16[8,2176]{1,0:T(8,128)(2,1)S(1)} %sent_partials.1), channel_id=1, source_target_pairs={{0,18},{2,16},{4,22},{6,20},{8,26},{10,24},{12,30},{14,28},{16,2},... | collective-permute-start | bytes 104456 | tf_op jit(solution)/shard_map/ppermute | solution.py:24
  29.9 3.9 %copy-start.5 = (f32[2048]{0:T(1024)S(1)}, f32[2048]{0:T(1024)}, u32[]{:S(2)}) copy-start(f32[2048]{0:T(1024)} %param.35) | copy-start | bytes 24580
  30.1 3.6 %collective-permute-start.12 = (f32[8,128]{1,0:T(8,128)S(1)}, f32[8,128]{1,0:T(8,128)S(1)}, u32[]{:S(2)}, u32[]{:S(2)}) collective-permute-start(f32[8,128]{1,0:T(8,128)S(1)} %get-tuple-element.46.squares), channel_id=1, source_target_pairs={{0,1},{1,0},{2,3},{3,2},{4,5},{5,4},{6,7},{7,6},{8,9},{9,8},{10,11... | collective-permute-start | bytes 12296 | tf_op jit(solution)/shard_map/ppermute | solution.py:24
